TPU v7x, 32 devices: a whole 2x2x4 slice. The times are simulated.
32 devices in a mesh: grp: 2 (over x), blk: 16 (over z, y, core).
Axes of the slice: x: 2, y: 2, z: 4, core: 2. Of those that a mesh axis runs over, the one named last changes fastest.
Arguments:
- heads: float32 [8192, 768], P(('grp', 'blk')), parts along dimension 0, may hold values from -1.5 to 1.5
- head_state: float32 [8192], P(('grp', 'blk')), parts along dimension 0, may hold values from 0.005 to 0.2
- tails: float32 [16384, 768], P(('grp', 'blk')), parts along dimension 0, may hold values from -1.5 to 1.5
- tail_state: float32 [16384], P(('grp', 'blk')), parts along dimension 0, may hold values from 0.005 to 0.2
- relation: float32 [1536, 768], P(('grp', 'blk')), parts along dimension 0, may hold values from -0.21875 to 0.21875
- relation_state: float32 [1536], P(('grp', 'blk')), parts along dimension 0, may hold values from 50 to 2000
- pos_head: int32 [2, 16384], P(None, ('grp', 'blk')), parts along dimension 1, may hold values from 0 to 255
- pos_tail: int32 [2, 16384], P(None, ('grp', 'blk')), parts along dimension 1, may hold values from 0 to 511
Outputs:
- heads_out: float32 [8192, 768], P(('grp', 'blk')), parts along dimension 0
- head_state_out: float32 [8192], P(('grp', 'blk')), parts along dimension 0
- tails_out: float32 [16384, 768], P(('grp', 'blk')), parts along dimension 0
- tail_state_out: float32 [16384], P(('grp', 'blk')), parts along dimension 0
- relation_out: float32 [1536, 768], P(('grp', 'blk')), parts along dimension 0
- relation_state_out: float32 [1536], P(('grp', 'blk')), parts along dimension 0
There are 2 independent parts, one for each index of `grp`. A program takes and returns all parts, laid end to end along the dimension named above; each array names one. Nothing has to cross between parts.
All inputs are finite; a program needn't handle non-finite values.
Results may differ from a plain program's by a relative error of at most 0.0003.
Values sent between devices are 32-bit elements; how exact they have to be, the bound alone decides.
No kernel may reach another device: no remote copies, remote signals or barrier semaphores. Data moves between devices by JAX's collectives and lax.ppermute only.
A program may use at most 64 MiB of HBM per device.

v0:
```python
import jax
import jax.numpy as jnp
from jax import lax
from jax.sharding import PartitionSpec as P

HIGH = lax.Precision.HIGHEST


def shifted(value, axis, by):
    length = lax.axis_size(axis)
    return lax.ppermute(value, axis, [(i, (i + by) % length) for i in range(length)])


def row_adagrad(param, state, grad):
    new_state = state + jnp.mean(grad * grad, axis=-1)
    return (param - 0.1 * grad / jnp.sqrt(new_state)[:, None], new_state)


def positives_table(head_idx, tail_idx, head_rows, tail_rows):
    onehot_heads = (head_idx[:, None] == jnp.arange(head_rows, dtype=jnp.int32)[None, :]).astype(
        jnp.bfloat16
    )
    onehot_tails = (tail_idx[:, None] == jnp.arange(tail_rows, dtype=jnp.int32)[None, :]).astype(
        jnp.bfloat16
    )
    return lax.dot_general(
        onehot_heads, onehot_tails, (((0,), (0,)), ((), ())), preferred_element_type=jnp.float32
    )


def tile_grads(product, tail_block, head_idx, tail_idx):
    scores = lax.dot_general(
        product,
        tail_block,
        (((1,), (1,)), ((), ())),
        precision=HIGH,
        preferred_element_type=jnp.float32,
    )
    marks = positives_table(head_idx, tail_idx, product.shape[0], tail_block.shape[0])
    grad_scores = (jax.nn.sigmoid(scores) - marks) * 0.0625
    grad_tails = lax.dot_general(
        grad_scores,
        product,
        (((0,), (0,)), ((), ())),
        precision=HIGH,
        preferred_element_type=jnp.float32,
    )
    grad_product = jnp.dot(
        grad_scores, tail_block, precision=HIGH, preferred_element_type=jnp.float32
    )
    return (grad_tails, grad_product)


def relation_term(old_heads, grad_product):

    def term(start, count):
        return lax.dot_general(
            old_heads,
            grad_product,
            (((0,), (0,)), ((), ())),
            precision=HIGH,
            preferred_element_type=jnp.float32,
        )

    return term


def body(heads, head_state, tails, tail_state, relation, relation_state, pos_head, pos_tail):
    share = relation.shape[0]
    first_row = lax.axis_index("blk") * share
    full, full_state = (
        lax.all_gather(relation, "blk", axis=0, tiled=True),
        lax.all_gather(relation_state, "blk", axis=0, tiled=True),
    )
    for bucket in range(2):
        product = jnp.dot(heads, full, precision=HIGH, preferred_element_type=jnp.float32)
        grad_tails, grad_product = tile_grads(product, tails, pos_head[bucket], pos_tail[bucket])
        tails, tail_state = row_adagrad(tails, tail_state, grad_tails)
        if bucket == 0:
            tails, tail_state = shifted((tails, tail_state), "blk", 1)
        grad_heads = lax.dot_general(
            grad_product,
            full,
            (((1,), (1,)), ((), ())),
            precision=HIGH,
            preferred_element_type=jnp.float32,
        )
        term = relation_term(heads, grad_product)
        heads, head_state = row_adagrad(heads, head_state, grad_heads)
        if bucket == 0:
            own_grad = lax.psum_scatter(
                term(jnp.int32(0), share * lax.axis_size("blk")),
                "blk",
                scatter_dimension=0,
                tiled=True,
            )
            relation, relation_state = row_adagrad(relation, relation_state, own_grad)
            full, full_state = (
                lax.all_gather(relation, "blk", axis=0, tiled=True),
                lax.all_gather(relation_state, "blk", axis=0, tiled=True),
            )
        else:
            own_grad = lax.psum_scatter(
                term(jnp.int32(0), share * lax.axis_size("blk")),
                "blk",
                scatter_dimension=0,
                tiled=True,
            )
            rows_now = lax.dynamic_slice_in_dim(full, first_row, share, 0)
            state_now = lax.dynamic_slice_in_dim(full_state, first_row, share, 0)
            relation, relation_state = row_adagrad(rows_now, state_now, own_grad)
    return (heads, head_state, tails, tail_state, relation, relation_state)


def solution(mesh):
    return jax.shard_map(
        body,
        mesh=mesh,
        in_specs=(
            P(("grp", "blk"), None),
            P(("grp", "blk")),
            P(("grp", "blk"), None),
            P(("grp", "blk")),
            P(("grp", "blk"), None),
            P(("grp", "blk")),
            P(None, ("grp", "blk")),
            P(None, ("grp", "blk")),
        ),
        out_specs=(
            P(("grp", "blk"), None),
            P(("grp", "blk")),
            P(("grp", "blk"), None),
            P(("grp", "blk")),
            P(("grp", "blk"), None),
            P(("grp", "blk")),
        ),
        check_vma=False,
    )
```

profile of v0, /device:TPU:0, one launch (start us, length us, event | category | flops | bytes accessed | tf_op | source)
XLA Modules:
  0.0 269.7 jit_solution(14279852047561015619)
XLA Ops:
  7.2 0.0 all-gather.3.cloned.1.call-start
  7.2 0.7 all-gather.3.cloned.1.call-update
  7.9 0.0 reduce-scatter.7.cloned.1.call-start
  7.9 0.8 fusion.23
  8.7 0.8 fusion.24
  9.5 0.6 fusion.10
  10.1 45.1 %all-gather.3.cloned.1.call-done = f32[768,768]{1,0:T(8,128)} async-done(((f32[48,768]{1,0:T(8,128)}), f32[768,768]{1,0:T(8,128)}) %all-gather.3.cloned.1.call-update) | async-done | bytes 2359312 | tf_op jit(solution)/shard_map/all_gather | solution.py:72
  55.2 4.1 %fusion.25 = f32[256,768]{1,0:T(8,128)S(1)} fusion(f32[256,768]{1,0:T(8,128)} %param.8, f32[768,768]{1,0:T(8,128)} %all-gather.3.cloned.1.call-done), kind=kOutput, calls=%fused_computation.51 | convolution fusion | flops 1811939328 | bytes 3932160 | tf_op jit(solution)/shard_map/dot_general | solution.py:76
  59.3 1.6 fusion.5
  61.0 1.5 fusion.26
  62.5 3.5 %convolution_bitcast_fusion = f32[768,768]{0,1:T(8,128)} fusion(f32[256,768]{1,0:T(8,128)S(1)} %fusion.26, f32[256,768]{1,0:T(8,128)S(1)} %copy-done.2), kind=kOutput, calls=%fused_computation | convolution fusion | flops 1811939328 | bytes 3932160 | tf_op jit(solution)/shard_map/dot_general | solution.py:57
  66.0 3.1 %copy.23 = f32[768,768]{1,0:T(8,128)} copy(f32[768,768]{0,1:T(8,128)} %convolution_bitcast_fusion) | data formatting | bytes 4718592
  69.1 0.0 all-gather.5.cloned.1.call-start
  69.1 0.8 copy-done.11
  70.0 0.9 copy.17
  70.9 0.6 dynamic-slice
  72.1 58.9 %reduce-scatter.7.cloned.1.call-done = f32[48,768]{1,0:T(8,128)} async-done(((f32[768,768]{1,0:T(8,128)}), f32[48,768]{1,0:T(8,128)}) %reduce-scatter.7.cloned.1.call-update) | async-done | bytes 147472
  131.0 1.1 copy.24
  132.0 0.1 multiply_reduce_fusion.5
  132.2 0.1 fusion.17
  132.3 1.8 divide_subtract_fusion.5
  134.1 1.8 copy.18
  135.9 0.0 reduce-scatter.9.cloned.1.call-start
  136.0 2.9 %multiply_reduce_fusion.1 = (f32[512]{0:T(512)S(1)}, f32[512,768]{1,0:T(8,128)S(1)}) fusion(f32[256,512]{1,0:T(8,128)} %copy-done.7, f32[256,768]{1,0:T(8,128)} %copy-done.3), kind=kOutput, calls=%fused_computation.4 | convolution fusion | flops 1208745472 | bytes 2885632 | tf_op jit(solution)/shard_map/dot_general | solution.py:41
  138.9 1.4 divide_subtract_fusion.1
  140.3 1.4 fusion.11
  141.7 2.3 multiply_reduce_fusion.3
  144.0 0.2 divide_subtract_fusion.3
  144.2 43.9 %all-gather.5.cloned.1.call-done = f32[768,768]{1,0:T(8,128)} async-done(((f32[48,768]{1,0:T(8,128)}), f32[768,768]{1,0:T(8,128)}) %all-gather.5.cloned.1.call-update) | async-done | bytes 2359312 | tf_op jit(solution)/shard_map/all_gather | solution.py:99
  188.1 3.8 %fusion.27 = f32[256,768]{1,0:T(8,128)S(1)} fusion(f32[256,768]{1,0:T(8,128)S(1)} %divide_subtract_fusion.3, f32[768,768]{1,0:T(8,128)} %all-gather.5.cloned.1.call-done), kind=kOutput, calls=%fused_computation.53 | convolution fusion | flops 1811939328 | bytes 3932160 | tf_op jit(solution)/shard_map/dot_general | solution.py:76
  192.0 1.6 fusion.9
  193.6 1.5 fusion.28
  195.1 3.5 %fusion.29 = f32[768,768]{1,0:T(8,128)} fusion(f32[256,768]{1,0:T(8,128)S(1)} %divide_subtract_fusion.3, f32[256,768]{1,0:T(8,128)S(1)} %fusion.28), kind=kOutput, calls=%fused_computation.55 | convolution fusion | flops 1811939328 | bytes 3932160
  198.6 0.3 collective-permute-start.1
  198.9 34.1 %all-reduce = f32[768]{0:T(1024)S(1)} all-reduce(f32[768]{0:T(1024)S(1)} %get-tuple-element.30), channel_id=1, replica_groups=mesh['grp'=2,'blk'=16] {'blk'}, use_global_device_ids=true, to_apply=%add | all-reduce | flops 768 | bytes 6144
  233.0 4.8 %multiply_reduce_fusion.2 = (f32[256]{0:T(256)S(1)}, f32[256,768]{1,0:T(8,128)}) fusion(f32[256,768]{1,0:T(8,128)S(1)} %fusion.28, f32[768,768]{1,0:T(8,128)} %all-gather.5.cloned.1.call-done), kind=kOutput, calls=%fused_computation.22 | convolution fusion | flops 1812332288 | bytes 3933184 | tf_op jit(solution)/shard_map/dot_general | solution.py:81
  237.8 0.6 fusion.21
  238.4 2.6 multiply_reduce_fusion
  241.0 1.6 constant_dynamic-slice_fusion
  242.6 1.1 copy.27
  243.7 1.4 fusion.20
  245.1 1.0 divide_subtract_fusion.2
  246.1 1.4 divide_subtract_fusion
  247.5 12.9 %reduce-scatter.9.cloned.1.call-done = f32[48,768]{1,0:T(8,128)} async-done(((f32[768,768]{1,0:T(8,128)}), f32[48,768]{1,0:T(8,128)}) %reduce-scatter.9.cloned.1.call-update) | async-done | bytes 147472
  260.5 1.1 copy.26
  261.6 0.1 multiply_reduce_fusion.4
  261.7 0.6 fusion.19
  262.3 0.8 copy.21
  (43 shorter events, 0.2 us)
Async XLA Ops:
  7.2 48.1 %all-gather.3.cloned.1.call-start = ((), (), s32[]{:S(2)}) async-start(), calls=%async_computation.2 | async-start | bytes 2506752 | tf_op jit(solution)/shard_map/all_gather | solution.py:72
  7.9 123.1 %reduce-scatter.7.cloned.1.call-start = ((), (), s32[]{:S(2)}) async-start(), calls=%async_computation.4 | async-start | bytes 2506752
  10.1 49.3 %copy-start = (f32[512,768]{1,0:T(8,128)S(1)}, f32[512,768]{1,0:T(8,128)}, u32[]{:S(2)}) copy-start(f32[512,768]{1,0:T(8,128)} %param.10) | copy-start | bytes 4718596
  59.3 1.6 copy-start.3
  60.9 1.5 copy-start.7
  61.0 1.5 copy-start.2
  69.0 0.9 copy-start.11
  69.0 1.8 copy-start.16
  69.0 63.1 %copy-start.15 = (f32[48]{0:T(128)S(1)}, f32[48]{0:T(128)}, u32[]{:S(2)}) copy-start(f32[48]{0:T(128)} %param.13) | copy-start | bytes 580
  69.1 119.0 %all-gather.5.cloned.1.call-start = ((), (), s32[]{:S(2)}) async-start(), calls=%async_computation.3 | async-start | bytes 2506752 | tf_op jit(solution)/shard_map/all_gather | solution.py:99
  135.9 2.9 %copy-start.14 = (f32[512]{0:T(512)S(1)}, f32[512]{0:T(512)}, u32[]{:S(2)}) copy-start(f32[512]{0:T(512)} %param.11) | copy-start | bytes 6148
  135.9 124.6 %reduce-scatter.9.cloned.1.call-start = ((), (), s32[]{:S(2)}) async-start(), calls=%async_computation.5 | async-start | bytes 2506752
  138.8 2.8 %copy-start.1 = (f32[768,768]{1,0:T(8,128)S(1)}, f32[768,768]{1,0:T(8,128)}, u32[]{:S(2)}) copy-start(f32[768,768]{1,0:T(8,128)} %all-gather.3.cloned.1.call-done) | copy-start | bytes 7077892
  140.3 51.6 %collective-permute-start = (f32[512,768]{1,0:T(8,128)}, f32[512,768]{1,0:T(8,128)S(1)}, u32[]{:S(2)}, u32[]{:S(2)}) collective-permute-start(f32[512,768]{1,0:T(8,128)} %divide_subtract_fusion.1), channel_id=1, source_target_pairs={{0,1},{1,2},{2,3},{3,4},{4,5},{5,6},{6,7},{7,8},{8,9},{9,10},{10,1... | collective-permute-start | bytes 4718600 | tf_op jit(solution)/shard_map/ppermute | solution.py:11
  141.7 2.3 copy-start.13
  144.2 47.8 %copy-start.12 = (f32[256,512]{1,0:T(8,128)S(1)}, f32[256,512]{1,0:T(8,128)}, u32[]{:S(2)}) copy-start(f32[256,512]{1,0:T(8,128)} %fusion.11) | copy-start | bytes 1572868
  191.9 1.6 copy-start.4
  193.6 1.5 copy-start.8
  198.6 45.1 %collective-permute-start.1 = (f32[512]{0:T(512)S(1)}, f32[512]{0:T(512)}, u32[]{:S(2)}, u32[]{:S(2)}) collective-permute-start(f32[512]{0:T(512)S(1)} %get-tuple-element.25), channel_id=1, source_target_pairs={{0,1},{1,2},{2,3},{3,4},{4,5},{5,6},{6,7},{7,8},{8,9},{9,10},{10,1... | collective-permute-start | bytes 6152 | tf_op jit(solution)/shard_map/ppermute | solution.py:11
  233.0 5.4 %copy-start.5 = (f32[256,768]{1,0:T(8,128)S(1)}, f32[256,768]{1,0:T(8,128)}, u32[]{:S(2)}) copy-start(f32[256,768]{1,0:T(8,128)} %copy-done.4) | copy-start | bytes 2359300
  233.0 5.4 %copy-start.9 = (f32[256,512]{1,0:T(8,128)S(1)}, f32[256,512]{1,0:T(8,128)}, u32[]{:S(2)}) copy-start(f32[256,512]{1,0:T(8,128)} %copy-done.8) | copy-start | bytes 1572868
  238.4 6.7 %copy-start.10 = (f32[256,768]{1,0:T(8,128)S(1)}, f32[256,768]{1,0:T(8,128)}, u32[]{:S(2)}) copy-start(f32[256,768]{1,0:T(8,128)} %get-tuple-element.37) | copy-start | bytes 2359300
  243.7 2.4 copy-start.6
Sparse Core Ops, SparseCore 0:
  10.3 44.9 all-gather.2
  69.2 61.7 reduce-scatter.6
  136.0 52.0 all-gather.4
  198.7 61.7 reduce-scatter.8
where the time goes:
time: 270 us
  waiting for transfers between devices  162 us (60%)
  matrix products  35.6 us (13%)
  blocking collectives  34.1 us (13%)
  between operations  14.7 us (5%)
  local copies, waits for them, and re-layouts  14.4 us (5%)
  other arithmetic  8.84 us (3%)
    all_gather x2, waiting for transfers between devices, body(): lax.all_gather(relation, 'blk', axis=0, tiled=True)  89 us
    unnamed x6, waiting for transfers between devices  72.5 us
    unnamed x1, blocking collectives  34.1 us
    unnamed x42, local copies, waits for them, and re-layouts  9.49 us
    dot_general x2, matrix products, body(): jnp.dot(heads, full, precision=HIGH, preferred_element_type=jnp.float32)  7.91 us
    dot_general x2, matrix products, body(): lax.dot_general(grad_product, full, (((1,), (1,)), ((), ())), precision=H...  7.1 us
    sub x6, other arithmetic, row_adagrad(): return (param - 0.1 * grad / jnp.sqrt(new_state)[:, None], new_state)  5.94 us
    dot_general x2, matrix products, tile_grads(): lax.dot_general(grad_scores, product, (((0,), (0,)), ((), ())), precision...  5.5 us
  transfers between devices with their start and end apart: 6, of which 4 were waited for; matrix products, arithmetic and copies ran while one was open for 11% of the time, Pallas kernels for 0%

commit v1 on v0

v1 whole, which is shorter than its diff:
```python
import functools

import jax
import jax.numpy as jnp
from jax import lax
from jax.experimental import pallas as pl
from jax.experimental.pallas import tpu as pltpu
from jax.sharding import PartitionSpec as P

F32 = jnp.float32
BF16 = jnp.bfloat16
NN = (((1,), (0,)), ((), ()))
NT = (((1,), (1,)), ((), ()))
VMEM = pl.BlockSpec(memory_space=pltpu.VMEM)
SMEM = pl.BlockSpec(memory_space=pltpu.SMEM)


def split(x):
    high = x.astype(BF16)
    return high, (x - high.astype(F32)).astype(BF16)


def dot3(a, b, dims):
    def one(p, q):
        return lax.dot_general(p, q, dims, preferred_element_type=F32)

    return one(a[0], b[0]) + (one(a[0], b[1]) + one(a[1], b[0]))


def diagonal(n):
    return lax.broadcasted_iota(jnp.int32, (n, n), 0) == lax.broadcasted_iota(jnp.int32, (n, n), 1)


def adagrad(param, state_row, grad):
    n = param.shape[0]
    eye = diagonal(n)
    state = jnp.sum(jnp.where(eye, state_row, 0.0), axis=1, keepdims=True)
    state = state + jnp.sum(grad * grad, axis=1, keepdims=True) * (1.0 / grad.shape[1])
    back = jnp.sum(jnp.where(eye, state, 0.0), axis=0, keepdims=True)
    return param - grad * (0.1 / jnp.sqrt(state)), back


def to_slots(me, source, target, slots):
    rows = source.shape[0] // slots
    for r in range(slots):
        start = pl.multiple_of((me ^ r) * rows, rows)
        target[r * rows : (r + 1) * rows, :] = source[pl.ds(start, rows), :]


def from_slots(me, source, target, slots):
    rows = source.shape[0] // slots
    for r in range(slots):
        start = pl.multiple_of((me ^ r) * rows, rows)
        target[pl.ds(start, rows), :] = source[r * rows : (r + 1) * rows, :]


def write_head_parts(me, heads, outs, normal, slotted, slots):
    normal[...] = heads.T
    to_slots(me, normal, slotted, slots)
    turned = slotted[...]
    outs[2][...], outs[3][...] = split(turned)
    outs[0][...], outs[1][...] = split(turned.T)


def prepare_kernel(slots, me_ref, heads, tails, pos_head, pos_tail, *rest):
    outs, tail_parts, marks, scratch = rest[:4], rest[4:6], rest[6], rest[7:]
    write_head_parts(me_ref[0], heads[...], outs, *scratch, slots)
    tail_parts[0][...], tail_parts[1][...] = split(tails[...])
    head_rows, tail_rows, pairs = heads.shape[0], tails.shape[0], pos_head.shape[1]
    for bucket in range(2):
        in_head = lax.broadcasted_iota(jnp.int32, (head_rows, pairs), 0) == pos_head[bucket : bucket + 1, :]
        in_tail = lax.broadcasted_iota(jnp.int32, (tail_rows, pairs), 0) == pos_tail[bucket : bucket + 1, :]
        marks[bucket] = lax.dot_general(
            jnp.where(in_head, 1.0, 0.0).astype(BF16),
            jnp.where(in_tail, 1.0, 0.0).astype(BF16),
            NT,
            preferred_element_type=F32,
        )


def bucket_kernel(bucket, slots, *refs):
    blocks, refs = refs[:slots], refs[slots:]
    heads, turned, tails, marks = refs[0:2], refs[2:4], refs[4:6], refs[6]
    relation, product, scores, grad, pieces = refs[7:9], refs[9:11], refs[11], refs[12:14], refs[14:]
    rows = blocks[0].shape[0]
    for r in range(slots):
        at = slice(r * rows, (r + 1) * rows)
        relation[0][at, :], relation[1][at, :] = split(blocks[r][...])
    prod = split(dot3((heads[0][...], heads[1][...]), (relation[0][...], relation[1][...]), NN))
    product[0][...], product[1][...] = prod
    tail = (tails[0][...], tails[1][...])
    grad_scores = (jax.nn.sigmoid(dot3(prod, tail, NT)) - marks[bucket]) * 0.0625
    scores[...] = grad_scores
    grad_product = split(dot3(split(grad_scores), tail, NN))
    grad[0][...], grad[1][...] = grad_product
    whole = dot3((turned[0][...], turned[1][...]), grad_product, NN)
    for r in range(slots):
        pieces[r][...] = whole[r * rows : (r + 1) * rows, :]


def tails_kernel(grad_scores, product_high, product_low, tails, state, tails_out, state_out):
    grad = dot3(split(grad_scores[...].T), (product_high[...], product_low[...]), NN)
    tails_out[...], state_out[...] = adagrad(tails[...], state[...], grad)


def heads_kernel(slots, last, me_ref, grad_high, grad_low, rel_high, rel_low, heads, state, *rest):
    heads_out, state_out, rest = rest[0], rest[1], rest[2:]
    outs, rest = (None, rest) if last else (rest[:4], rest[4:])
    high, low = rest[0], rest[1]
    from_slots(me_ref[0], rel_high, high, slots)
    from_slots(me_ref[0], rel_low, low, slots)
    grad = dot3((grad_high[...], grad_low[...]), (high[...], low[...]), NT)
    new_heads, state_out[...] = adagrad(heads[...], state[...], grad)
    heads_out[...] = new_heads
    if not last:
        write_head_parts(me_ref[0], new_heads, outs, *rest[2:], slots)


def split_kernel(tails, high, low):
    high[...], low[...] = split(tails[...])


def relation_kernel(relation, state, *rest):
    pieces, (relation_out, state_out) = rest[:-2], rest[-2:]
    grad = pieces[0][...]
    for piece in pieces[1:]:
        grad = grad + piece[...]
    relation_out[...], state_out[...] = adagrad(relation[...], state[...], grad)


def call(kernel, outs, args, scratch=(), smem_first=False, flops=0):
    specs = [VMEM] * len(args)
    if smem_first:
        specs[0] = SMEM
    moved = sum(a.size * a.dtype.itemsize for a in args)
    return pl.pallas_call(
        kernel,
        out_shape=[jax.ShapeDtypeStruct(s, t) for s, t in outs],
        in_specs=specs,
        out_specs=[VMEM] * len(outs),
        scratch_shapes=[pltpu.VMEM(s, t) for s, t in scratch],
        compiler_params=pltpu.CompilerParams(vmem_limit_bytes=48 * 1024 * 1024),
        cost_estimate=pl.CostEstimate(flops=flops, bytes_accessed=moved, transcendentals=0),
    )(*args)


def partner(value, mask):
    n = lax.axis_size("blk")
    return lax.ppermute(value, "blk", [(i, i ^ mask) for i in range(n)])


def gather_blocks(own):
    n = lax.axis_size("blk")
    far = range(4, n, 4)
    got = {0: own, 2: partner(own, 2)}
    for k in far:
        got[k] = partner(own, k)
    for k in far:
        got[k ^ 2] = partner(got[k], 2)
    for k in (0, *far):
        got[k ^ 1] = partner(got[k], 1)
        got[k ^ 3] = partner(got[k ^ 2], 1)
    return [got[r] for r in range(n)]


def scatter_blocks(pieces):
    n = len(pieces)
    terms = []
    for k in (*range(n - 4, 0, -4), 0):
        across = pieces[k ^ 2] + partner(pieces[k ^ 3], 1)
        here = pieces[k] + partner(pieces[k ^ 1], 1)
        here = here + partner(across, 2)
        terms.append(partner(here, k) if k else here)
    return terms


def body(heads, head_state, tails, tail_state, relation, relation_state, pos_head, pos_tail):
    share, width = relation.shape
    n = lax.axis_size("blk")
    by_blocks = share % 16 == 0 and n & (n - 1) == 0 and n >= 4
    slots = n if by_blocks else 1
    me = (lax.axis_index("blk").astype(jnp.int32) if by_blocks else jnp.int32(0)).reshape(1)
    head_rows, tail_rows = heads.shape[0], tails.shape[0]
    head_state, tail_state, relation_state = (s.reshape(1, -1) for s in (head_state, tail_state, relation_state))

    def gathered(rows):
        return gather_blocks(rows) if by_blocks else [lax.all_gather(rows, "blk", axis=0, tiled=True)]

    def scattered(pieces):
        if by_blocks:
            return scatter_blocks(pieces)
        return [lax.psum_scatter(pieces[0], "blk", scatter_dimension=0, tiled=True)]

    head_parts = [((head_rows, width), BF16)] * 2 + [((width, head_rows), BF16)] * 2
    turned = [((width, head_rows), F32)] * 2
    tail_parts = [((tail_rows, width), BF16)] * 2
    relation_parts = [((width, width), BF16)] * 2
    row_parts = [((head_rows, width), BF16)] * 2
    block = ((width // slots, width), F32)
    table = ((head_rows, tail_rows), F32)

    *parts, marks = call(
        functools.partial(prepare_kernel, slots),
        [*head_parts, *tail_parts, ((2, *table[0]), F32)],
        [me, heads, tails, pos_head, pos_tail],
        scratch=turned,
        smem_first=True,
    )
    head_half, tail_half = parts[:4], parts[4:]
    for bucket in range(2):
        last = bucket == 1
        blocks = gathered(relation)
        out = call(
            functools.partial(bucket_kernel, bucket, slots),
            [*relation_parts, *row_parts, table, *row_parts, *[block] * slots],
            [*blocks, *head_half, *tail_half, marks],
            flops=6 * head_rows * width * (2 * width + 2 * tail_rows),
        )
        relation_half, product, grad_scores, grad_product, pieces = out[0:2], out[2:4], out[4], out[5:7], out[7:]
        terms = scattered(pieces)
        tails, tail_state = call(
            tails_kernel,
            [(tails.shape, F32), (tail_state.shape, F32)],
            [grad_scores, *product, tails, tail_state],
            flops=6 * head_rows * width * tail_rows,
        )
        if not last:
            tails, tail_state = (
                lax.ppermute(v, "blk", [(i, (i + 1) % n) for i in range(n)]) for v in (tails, tail_state)
            )
            tail_half = call(split_kernel, tail_parts, [tails])
        out = call(
            functools.partial(heads_kernel, slots, last),
            [(heads.shape, F32), (head_state.shape, F32), *([] if last else head_parts)],
            [me, *grad_product, *relation_half, heads, head_state],
            scratch=[*relation_parts, *([] if last else turned)],
            smem_first=True,
            flops=6 * head_rows * width * width,
        )
        heads, head_state, head_half = out[0], out[1], out[2:]
        relation, relation_state = call(
            relation_kernel,
            [(relation.shape, F32), (relation_state.shape, F32)],
            [relation, relation_state, *terms],
        )
    return (
        heads,
        head_state.reshape(-1),
        tails,
        tail_state.reshape(-1),
        relation,
        relation_state.reshape(-1),
    )


def solution(mesh):
    rows, flat, pairs = P(("grp", "blk"), None), P(("grp", "blk")), P(None, ("grp", "blk"))
    return jax.shard_map(
        body,
        mesh=mesh,
        in_specs=(rows, flat, rows, flat, rows, flat, pairs, pairs),
        out_specs=(rows, flat, rows, flat, rows, flat),
        check_vma=False,
    )
```

time: 270 us -> 167 us (0.62)
  waiting for transfers between devices: 162 us -> 85 us
  starting transfers between devices: 0.47 us -> 40 us
  matrix products: 35.6 us -> 0 us
  blocking collectives: 34.1 us -> 0 us
  Pallas kernels: 0 us -> 27.8 us
  between operations: 14.7 us -> 1.07 us
  other arithmetic: 8.84 us -> 0.35 us
    all_gather x2 -> x0, waiting for transfers between devices: 89 us -> none  [body(): lax.all_gather(relation, 'blk', axis=0, tiled=True)]
    ppermute x2 -> x62, waiting for transfers between devices: 0.01 us -> 85 us  [the longest x60 80.7 us: partner(): return lax.ppermute(value, 'blk', [(i, i ^ mask) for i in range(n)])]
    unnamed x6 -> x0, waiting for transfers between devices: 72.5 us -> none
    ppermute x2 -> x62, starting transfers between devices: 0.31 us -> 40 us  [the longest x60 38.8 us: partner(): return lax.ppermute(value, 'blk', [(i, i ^ mask) for i in range(n)])]
    unnamed x1 -> x0, blocking collectives: 34.1 us -> none
    dot_general x13 -> x0, matrix products: 32.1 us -> none  [the longest x2 7.91 us: body(): jnp.dot(heads, full, precision=HIGH, preferred_element_type=jnp.float32)]
    pallas_call x0 -> x10, Pallas kernels: none -> 27.8 us  [call(): pl.pallas_call(kernel, out_shape=[jax.ShapeDtypeStruct(s, t) for s, t in...]
    sub x6 -> x0, other arithmetic: 5.94 us -> none  [row_adagrad(): return (param - 0.1 * grad / jnp.sqrt(new_state)[:, None], new_state)]
  transfers between devices with their start and end apart: 6 -> 62, of which waited for: 4 -> 22; matrix products, arithmetic and copies ran while one was open for 11% -> 0% of each run, Pallas kernels for 0% -> 7%
where the time goes in v1:
time: 167 us
  waiting for transfers between devices  85 us (51%)
  starting transfers between devices  40 us (24%)
  Pallas kernels  27.8 us (17%)
  local copies, waits for them, and re-layouts  12.4 us (7%)
    ppermute x60, waiting for transfers between devices, partner(): return lax.ppermute(value, 'blk', [(i, i ^ mask) for i in range(n)])  80.7 us
    ppermute x60, starting transfers between devices, partner(): return lax.ppermute(value, 'blk', [(i, i ^ mask) for i in range(n)])  38.8 us
    pallas_call x10, Pallas kernels, call(): pl.pallas_call(kernel, out_shape=[jax.ShapeDtypeStruct(s, t) for s, t in...  27.8 us
    unnamed x58, local copies, waits for them, and re-layouts  12.4 us
    ppermute x2, waiting for transfers between devices, body(): lax.ppermute(v, 'blk', [(i, (i + 1) % n) for i in range(n)])  4.27 us
  transfers between devices with their start and end apart: 62, of which 22 were waited for; matrix products, arithmetic and copies ran while one was open for 0% of the time, Pallas kernels for 7%

profile of v1, /device:TPU:0, one launch (start us, length us, event | category | flops | bytes accessed | tf_op | source)
XLA Modules:
  0.0 166.6 jit_solution(8066355277562477334)
XLA Ops:
  0.6 5.1 %collective-permute-start.11 = (f32[48,768]{1,0:T(8,128)}, f32[48,768]{1,0:T(8,128)S(1)}, u32[]{:S(2)}, u32[]{:S(2)}) collective-permute-start(f32[48,768]{1,0:T(8,128)} %relation.1), channel_id=1, source_target_pairs={{0,12},{1,13},{2,14},{3,15},{4,8},{5,9},{6,10},{7,11},{8,4},{9,5},... | collective-permute-start | bytes 442376 | tf_op jit(solution)/shard_map/ppermute | solution.py:149
  6.4 1.7 collective-permute-start.1
  8.1 2.7 %collective-permute-done.11.refs_12_ = f32[48,768]{1,0:T(8,128)S(1)} collective-permute-done((f32[48,768]{1,0:T(8,128)}, f32[48,768]{1,0:T(8,128)S(1)}, u32[]{:S(2)}, u32[]{:S(2)}) %collective-permute-start.11) | collective-permute-done | bytes 147488 | tf_op jit(solution)/shard_map/ppermute | solution.py:149
  10.7 1.7 %collective-permute-start.13 = (f32[48,768]{1,0:T(8,128)S(1)}, f32[48,768]{1,0:T(8,128)S(1)}, u32[]{:S(2)}, u32[]{:S(2)}) collective-permute-start(f32[48,768]{1,0:T(8,128)S(1)} %collective-permute-done.11.refs_12_), channel_id=1, source_target_pairs={{0,2},{1,3},{2,0},{3,1},{4,6},{5,7},{6,4},{7,5},{8,10},{9,11},{10,... | collective-permute-start | bytes 442376 | tf_op jit(solution)/shard_map/ppermute | solution.py:149
  12.5 6.0 %collective-permute-done.7.refs_8_ = f32[48,768]{1,0:T(8,128)S(1)} collective-permute-done((f32[48,768]{1,0:T(8,128)}, f32[48,768]{1,0:T(8,128)S(1)}, u32[]{:S(2)}, u32[]{:S(2)}) %collective-permute-start.7) | collective-permute-done | bytes 147488 | tf_op jit(solution)/shard_map/ppermute | solution.py:149
  18.4 1.5 collective-permute-start.9
  21.2 3.9 %collective-permute-done.9.refs_10_ = f32[48,768]{1,0:T(8,128)S(1)} collective-permute-done((f32[48,768]{1,0:T(8,128)S(1)}, f32[48,768]{1,0:T(8,128)S(1)}, u32[]{:S(2)}, u32[]{:S(2)}) %collective-permute-start.9) | collective-permute-done | bytes 147488 | tf_op jit(solution)/shard_map/ppermute | solution.py:149
  25.6 2.3 %collective-permute-done.5.refs_6_ = f32[48,768]{1,0:T(8,128)S(1)} collective-permute-done((f32[48,768]{1,0:T(8,128)S(1)}, f32[48,768]{1,0:T(8,128)S(1)}, u32[]{:S(2)}, u32[]{:S(2)}) %collective-permute-start.5) | collective-permute-done | bytes 147488 | tf_op jit(solution)/shard_map/ppermute | solution.py:149
  27.9 1.1 copy-done.1
  30.4 2.5 %shard_map.127 = (bf16[256,768]{1,0:T(8,128)(2,1)S(1)}, bf16[256,768]{1,0:T(8,128)(2,1)S(1)}, bf16[768,256]{1,0:T(8,128)(2,1)S(1)}, bf16[768,256]{1,0:T(8,128)(2...) custom-call(s32[1]{0:T(128)} %bitcast.me_ref, ...), custom_call_target="tpu_custom_call" | custom-call | bytes 2367492 | tf_op jit(solution)/shard_map/pallas_call | solution.py:136
  32.9 1.0 copy-done.16
  38.7 7.8 %shard_map.128 = (bf16[768,768]{1,0:T(8,128)(2,1)}, bf16[768,768]{1,0:T(8,128)(2,1)}, bf16[256,768]{1,0:T(8,128)(2,1)S(1)}, bf16[256,768]{1,0:T(8,128)(2,1)S(1)}...) custom-call(f32[48,768]{1,0:T(8,128)S(1)} %copy-done.10, ...), custom_call_target="tpu_custom_call" | custom-call | flops 3019898880 | bytes 6553600 | tf_op jit(solution)/shard_map/pallas_call | solution.py:136
  47.0 1.0 copy-done.7
  48.1 1.1 shard_map.131
  49.9 1.1 collective-permute-start.24
  52.1 1.0 collective-permute-done.24
  54.2 20.0 %collective-permute-done.17 = f32[48,768]{1,0:T(8,128)S(1)} collective-permute-done((f32[48,768]{1,0:T(8,128)S(1)}, f32[48,768]{1,0:T(8,128)S(1)}, u32[]{:S(2)}, u32[]{:S(2)}) %collective-permute-start.17) | collective-permute-done | bytes 147488 | tf_op jit(solution)/shard_map/ppermute | solution.py:149
  74.3 2.1 %collective-permute-start.25 = (f32[48,768]{1,0:T(8,128)S(1)}, f32[48,768]{1,0:T(8,128)S(1)}, u32[]{:S(2)}, u32[]{:S(2)}) collective-permute-start(f32[48,768]{1,0:T(8,128)S(1)} %add.79), channel_id=1, source_target_pairs={{0,2},{1,3},{2,0},{3,1},{4,6},{5,7},{6,4},{7,5},{8,10},{9,11},{10,... | collective-permute-start | bytes 442376 | tf_op jit(solution)/shard_map/ppermute | solution.py:149
  76.4 4.7 %collective-permute-done.21 = f32[48,768]{1,0:T(8,128)S(1)} collective-permute-done((f32[48,768]{1,0:T(8,128)S(1)}, f32[48,768]{1,0:T(8,128)S(1)}, u32[]{:S(2)}, u32[]{:S(2)}) %collective-permute-start.21) | collective-permute-done | bytes 147488 | tf_op jit(solution)/shard_map/ppermute | solution.py:149
  81.1 1.6 collective-permute-start.18
  82.6 1.3 collective-permute-done.25
  84.8 1.5 collective-permute-start.26
  86.4 3.2 %collective-permute-done.18.rest_0_ = f32[48,768]{1,0:T(8,128)S(1)} collective-permute-done((f32[48,768]{1,0:T(8,128)S(1)}, f32[48,768]{1,0:T(8,128)S(1)}, u32[]{:S(2)}, u32[]{:S(2)}) %collective-permute-start.18) | collective-permute-done | bytes 147488 | tf_op jit(solution)/shard_map/ppermute | solution.py:149
  89.6 4.5 %collective-permute-done.22.rest_1_ = f32[48,768]{1,0:T(8,128)S(1)} collective-permute-done((f32[48,768]{1,0:T(8,128)S(1)}, f32[48,768]{1,0:T(8,128)S(1)}, u32[]{:S(2)}, u32[]{:S(2)}) %collective-permute-start.22) | collective-permute-done | bytes 147488 | tf_op jit(solution)/shard_map/ppermute | solution.py:149
  94.2 3.3 %collective-permute-start.41 = (f32[48,768]{1,0:T(8,128)S(1)}, f32[48,768]{1,0:T(8,128)S(1)}, u32[]{:S(2)}, u32[]{:S(2)}) collective-permute-start(f32[48,768]{1,0:T(8,128)S(1)} %get-tuple-element.100.refs_0_.relation), channel_id=1, source_target_pairs={{0,12},{1,13},{2,14},{3,15},{4,8},{5,9},{6,10},{7,11},{8,4},{9,5},... | collective-permute-start | bytes 442376 | tf_op jit(solution)/shard_map/ppermute | solution.py:149
  97.5 1.1 collective-permute-start.33
  98.7 1.1 collective-permute-start.31
  99.8 3.1 %collective-permute-done.41.refs_12_ = f32[48,768]{1,0:T(8,128)S(1)} collective-permute-done((f32[48,768]{1,0:T(8,128)S(1)}, f32[48,768]{1,0:T(8,128)S(1)}, u32[]{:S(2)}, u32[]{:S(2)}) %collective-permute-start.41) | collective-permute-done | bytes 147488 | tf_op jit(solution)/shard_map/ppermute | solution.py:149
  102.9 5.9 %collective-permute-done.37.refs_8_ = f32[48,768]{1,0:T(8,128)S(1)} collective-permute-done((f32[48,768]{1,0:T(8,128)S(1)}, f32[48,768]{1,0:T(8,128)S(1)}, u32[]{:S(2)}, u32[]{:S(2)}) %collective-permute-start.37) | collective-permute-done | bytes 147488 | tf_op jit(solution)/shard_map/ppermute | solution.py:149
  109.5 1.4 collective-permute-start.39
  111.0 4.2 %collective-permute-done.43.refs_14_ = f32[48,768]{1,0:T(8,128)S(1)} collective-permute-done((f32[48,768]{1,0:T(8,128)S(1)}, f32[48,768]{1,0:T(8,128)S(1)}, u32[]{:S(2)}, u32[]{:S(2)}) %collective-permute-start.43) | collective-permute-done | bytes 147488 | tf_op jit(solution)/shard_map/ppermute | solution.py:149
  115.4 3.0 %collective-permute-done.39.refs_10_ = f32[48,768]{1,0:T(8,128)S(1)} collective-permute-done((f32[48,768]{1,0:T(8,128)S(1)}, f32[48,768]{1,0:T(8,128)S(1)}, u32[]{:S(2)}, u32[]{:S(2)}) %collective-permute-start.39) | collective-permute-done | bytes 147488 | tf_op jit(solution)/shard_map/ppermute | solution.py:149
  118.9 1.5 collective-permute-done.35.refs_6_
  120.9 3.2 %shard_map.130 = (f32[256,768]{1,0:T(8,128)S(1)}, f32[1,256]{1,0:T(1,128)S(1)}, bf16[256,768]{1,0:T(8,128)(2,1)S(1)}, bf16[256,768]{1,0:T(8,128)(2,1)S(1)}, bf16...) custom-call(s32[1]{0:T(128)} %bitcast.me_ref, bf16[256,768]{1,0:T(8,128)(2,1)S(1)} %get-tuple-element.101.grad_high, ...), custom_call_target="tpu_custom_call" | custom-call | flops 905969664 | bytes 3933188 | tf_op jit(solution)/shard_map/pallas_call | solution.py:136
  124.3 1.1 copy-done.19
  126.4 7.7 %shard_map.133 = (bf16[768,768]{1,0:T(8,128)(2,1)}, bf16[768,768]{1,0:T(8,128)(2,1)}, bf16[256,768]{1,0:T(8,128)(2,1)S(1)}, bf16[256,768]{1,0:T(8,128)(2,1)S(1)}...) custom-call(f32[48,768]{1,0:T(8,128)S(1)} %get-tuple-element.100.ref, ...), custom_call_target="tpu_custom_call" | custom-call | flops 3019898880 | bytes 6553600 | tf_op jit(solution)/shard_map/pallas_call | solution.py:136
  135.7 4.3 %collective-permute-done.46.state = f32[1,512]{1,0:T(1,128)S(1)} collective-permute-done((f32[1,512]{1,0:T(1,128)S(1)}, f32[1,512]{1,0:T(1,128)S(1)}, u32[]{:S(2)}, u32[]{:S(2)}) %collective-permute-start.46) | collective-permute-done | bytes 2080 | tf_op jit(solution)/shard_map/ppermute | solution.py:229
  140.0 1.0 copy-done.6
  141.0 2.2 %shard_map.135 = (f32[512,768]{1,0:T(8,128)}, f32[1,512]{1,0:T(1,128)}) custom-call(f32[256,512]{1,0:T(8,128)S(1)} %copy-done.6, bf16[256,768]{1,0:T(8,128)(2,1)S(1)} %get-tuple-element.124.product_high, bf16[256,768]{1,0:T(8,128)(2,1)S(1)} %get-tuple-element.125.product_low, f32[512,768]{1,0:T(8,128)S(1)} %collective-permute-done.45.tails, ...), custom_call_target="tpu_custom_call" | custom-call | flops 603979776 | bytes 2885632 | tf_op jit(solution)/shard_map/pallas_call | solution.py:136
  143.2 2.3 %shard_map.134 = (f32[256,768]{1,0:T(8,128)}, f32[1,256]{1,0:T(1,128)}) custom-call(s32[1]{0:T(128)} %bitcast.me_ref, bf16[256,768]{1,0:T(8,128)(2,1)S(1)} %get-tuple-element.115.grad_high, bf16[256,768]{1,0:T(8,128)(2,1)S(1)} %copy-done.9, bf16[768,768]{1,0:T(8,128)(2,1)S(1)} %copy-done.4, bf16[768,768]{1,0:T(8,128)(2,1)S(1)} %copy-done.5, ...), custom_call_target="tpu_custom_call" | custom-call | flops 905969664 | bytes 3933188 | tf_op jit(solution)/shard_map/pallas_call | solution.py:136
  146.3 2.1 %collective-permute-start.53 = (f32[48,768]{1,0:T(8,128)S(1)}, f32[48,768]{1,0:T(8,128)S(1)}, u32[]{:S(2)}, u32[]{:S(2)}) collective-permute-start(f32[48,768]{1,0:T(8,128)S(1)} %add.88), channel_id=1, source_target_pairs={{0,2},{1,3},{2,0},{3,1},{4,6},{5,7},{6,4},{7,5},{8,10},{9,11},{10,... | collective-permute-start | bytes 442376 | tf_op jit(solution)/shard_map/ppermute | solution.py:149
  148.5 2.0 %collective-permute-start.61 = (f32[48,768]{1,0:T(8,128)S(1)}, f32[48,768]{1,0:T(8,128)S(1)}, u32[]{:S(2)}, u32[]{:S(2)}) collective-permute-start(f32[48,768]{1,0:T(8,128)S(1)} %add.94), channel_id=1, source_target_pairs={{0,2},{1,3},{2,0},{3,1},{4,6},{5,7},{6,4},{7,5},{8,10},{9,11},{10,... | collective-permute-start | bytes 442376 | tf_op jit(solution)/shard_map/ppermute | solution.py:149
  150.5 2.6 %collective-permute-done.53 = f32[48,768]{1,0:T(8,128)S(1)} collective-permute-done((f32[48,768]{1,0:T(8,128)S(1)}, f32[48,768]{1,0:T(8,128)S(1)}, u32[]{:S(2)}, u32[]{:S(2)}) %collective-permute-start.53) | collective-permute-done | bytes 147488 | tf_op jit(solution)/shard_map/ppermute | solution.py:149
  153.5 2.7 %collective-permute-done.57 = f32[48,768]{1,0:T(8,128)S(1)} collective-permute-done((f32[48,768]{1,0:T(8,128)S(1)}, f32[48,768]{1,0:T(8,128)S(1)}, u32[]{:S(2)}, u32[]{:S(2)}) %collective-permute-start.57) | collective-permute-done | bytes 147488 | tf_op jit(solution)/shard_map/ppermute | solution.py:149
  156.2 1.4 collective-permute-start.58
  157.6 1.5 collective-permute-done.61
  159.2 2.5 %collective-permute-done.50.rest_0_ = f32[48,768]{1,0:T(8,128)S(1)} collective-permute-done((f32[48,768]{1,0:T(8,128)S(1)}, f32[48,768]{1,0:T(8,128)S(1)}, u32[]{:S(2)}, u32[]{:S(2)}) %collective-permute-start.50) | collective-permute-done | bytes 147488 | tf_op jit(solution)/shard_map/ppermute | solution.py:149
  161.7 4.2 %collective-permute-done.54.rest_1_ = f32[48,768]{1,0:T(8,128)S(1)} collective-permute-done((f32[48,768]{1,0:T(8,128)S(1)}, f32[48,768]{1,0:T(8,128)S(1)}, u32[]{:S(2)}, u32[]{:S(2)}) %collective-permute-start.54) | collective-permute-done | bytes 147488 | tf_op jit(solution)/shard_map/ppermute | solution.py:149
  (160 shorter events, 20.0 us)
Async XLA Ops:
  0.6 10.1 %collective-permute-start.11 = (f32[48,768]{1,0:T(8,128)}, f32[48,768]{1,0:T(8,128)S(1)}, u32[]{:S(2)}, u32[]{:S(2)}) collective-permute-start(f32[48,768]{1,0:T(8,128)} %relation.1), channel_id=1, source_target_pairs={{0,12},{1,13},{2,14},{3,15},{4,8},{5,9},{6,10},{7,11},{8,4},{9,5},... | collective-permute-start | bytes 442376 | tf_op jit(solution)/shard_map/ppermute | solution.py:149
  5.7 12.7 %collective-permute-start.7 = (f32[48,768]{1,0:T(8,128)}, f32[48,768]{1,0:T(8,128)S(1)}, u32[]{:S(2)}, u32[]{:S(2)}) collective-permute-start(f32[48,768]{1,0:T(8,128)} %relation.1), channel_id=1, source_target_pairs={{0,8},{1,9},{2,10},{3,11},{4,12},{5,13},{6,14},{7,15},{8,0},{9,1},... | collective-permute-start | bytes 442376 | tf_op jit(solution)/shard_map/ppermute | solution.py:149
  5.8 12.7 %collective-permute-start.3 = (f32[48,768]{1,0:T(8,128)}, f32[48,768]{1,0:T(8,128)S(1)}, u32[]{:S(2)}, u32[]{:S(2)}) collective-permute-start(f32[48,768]{1,0:T(8,128)} %relation.1), channel_id=1, source_target_pairs={{0,4},{1,5},{2,6},{3,7},{4,0},{5,1},{6,2},{7,3},{8,12},{9,13},{10,... | collective-permute-start | bytes 442376 | tf_op jit(solution)/shard_map/ppermute | solution.py:149
  6.4 13.6 %collective-permute-start.1 = (f32[48,768]{1,0:T(8,128)}, f32[48,768]{1,0:T(8,128)S(1)}, u32[]{:S(2)}, u32[]{:S(2)}) collective-permute-start(f32[48,768]{1,0:T(8,128)} %relation.1), channel_id=1, source_target_pairs={{0,2},{1,3},{2,0},{3,1},{4,6},{5,7},{6,4},{7,5},{8,10},{9,11},{10,... | collective-permute-start | bytes 442376 | tf_op jit(solution)/shard_map/ppermute | solution.py:149
  8.1 12.1 %collective-permute-start = (f32[48,768]{1,0:T(8,128)}, f32[48,768]{1,0:T(8,128)S(1)}, u32[]{:S(2)}, u32[]{:S(2)}) collective-permute-start(f32[48,768]{1,0:T(8,128)} %relation.1), channel_id=1, source_target_pairs={{0,1},{1,0},{2,3},{3,2},{4,5},{5,4},{6,7},{7,6},{8,9},{9,8},{10,11... | collective-permute-start | bytes 442376 | tf_op jit(solution)/shard_map/ppermute | solution.py:149
  10.7 10.0 %collective-permute-start.13 = (f32[48,768]{1,0:T(8,128)S(1)}, f32[48,768]{1,0:T(8,128)S(1)}, u32[]{:S(2)}, u32[]{:S(2)}) collective-permute-start(f32[48,768]{1,0:T(8,128)S(1)} %collective-permute-done.11.refs_12_), channel_id=1, source_target_pairs={{0,2},{1,3},{2,0},{3,1},{4,6},{5,7},{6,4},{7,5},{8,10},{9,11},{10,... | collective-permute-start | bytes 442376 | tf_op jit(solution)/shard_map/ppermute | solution.py:149
  18.4 6.6 %collective-permute-start.9 = (f32[48,768]{1,0:T(8,128)S(1)}, f32[48,768]{1,0:T(8,128)S(1)}, u32[]{:S(2)}, u32[]{:S(2)}) collective-permute-start(f32[48,768]{1,0:T(8,128)S(1)} %collective-permute-done.7.refs_8_), channel_id=1, source_target_pairs={{0,2},{1,3},{2,0},{3,1},{4,6},{5,7},{6,4},{7,5},{8,10},{9,11},{10,... | collective-permute-start | bytes 442376 | tf_op jit(solution)/shard_map/ppermute | solution.py:149
  20.2 7.7 %collective-permute-start.5 = (f32[48,768]{1,0:T(8,128)S(1)}, f32[48,768]{1,0:T(8,128)S(1)}, u32[]{:S(2)}, u32[]{:S(2)}) collective-permute-start(f32[48,768]{1,0:T(8,128)S(1)} %collective-permute-done.3.refs_4_), channel_id=1, source_target_pairs={{0,2},{1,3},{2,0},{3,1},{4,6},{5,7},{6,4},{7,5},{8,10},{9,11},{10,... | collective-permute-start | bytes 442376 | tf_op jit(solution)/shard_map/ppermute | solution.py:149
  20.7 18.0 %collective-permute-start.4 = (f32[48,768]{1,0:T(8,128)S(1)}, f32[48,768]{1,0:T(8,128)S(1)}, u32[]{:S(2)}, u32[]{:S(2)}) collective-permute-start(f32[48,768]{1,0:T(8,128)S(1)} %collective-permute-done.3.refs_4_), channel_id=1, source_target_pairs={{0,1},{1,0},{2,3},{3,2},{4,5},{5,4},{6,7},{7,6},{8,9},{9,8},{10,11... | collective-permute-start | bytes 442376 | tf_op jit(solution)/shard_map/ppermute | solution.py:149
  20.7 18.0 %collective-permute-start.2 = (f32[48,768]{1,0:T(8,128)S(1)}, f32[48,768]{1,0:T(8,128)S(1)}, u32[]{:S(2)}, u32[]{:S(2)}) collective-permute-start(f32[48,768]{1,0:T(8,128)S(1)} %collective-permute-done.1.refs_2_), channel_id=1, source_target_pairs={{0,1},{1,0},{2,3},{3,2},{4,5},{5,4},{6,7},{7,6},{8,9},{9,8},{10,11... | collective-permute-start | bytes 442376 | tf_op jit(solution)/shard_map/ppermute | solution.py:149
  25.1 13.6 %collective-permute-start.14 = (f32[48,768]{1,0:T(8,128)S(1)}, f32[48,768]{1,0:T(8,128)S(1)}, u32[]{:S(2)}, u32[]{:S(2)}) collective-permute-start(f32[48,768]{1,0:T(8,128)S(1)} %collective-permute-done.13.refs_14_), channel_id=1, source_target_pairs={{0,1},{1,0},{2,3},{3,2},{4,5},{5,4},{6,7},{7,6},{8,9},{9,8},{10,11... | collective-permute-start | bytes 442376 | tf_op jit(solution)/shard_map/ppermute | solution.py:149
  25.1 13.6 %collective-permute-start.10 = (f32[48,768]{1,0:T(8,128)S(1)}, f32[48,768]{1,0:T(8,128)S(1)}, u32[]{:S(2)}, u32[]{:S(2)}) collective-permute-start(f32[48,768]{1,0:T(8,128)S(1)} %collective-permute-done.9.refs_10_), channel_id=1, source_target_pairs={{0,1},{1,0},{2,3},{3,2},{4,5},{5,4},{6,7},{7,6},{8,9},{9,8},{10,11... | collective-permute-start | bytes 442376 | tf_op jit(solution)/shard_map/ppermute | solution.py:149
  27.9 10.8 %collective-permute-start.6 = (f32[48,768]{1,0:T(8,128)S(1)}, f32[48,768]{1,0:T(8,128)S(1)}, u32[]{:S(2)}, u32[]{:S(2)}) collective-permute-start(f32[48,768]{1,0:T(8,128)S(1)} %collective-permute-done.5.refs_6_), channel_id=1, source_target_pairs={{0,1},{1,0},{2,3},{3,2},{4,5},{5,4},{6,7},{7,6},{8,9},{9,8},{10,11... | collective-permute-start | bytes 442376 | tf_op jit(solution)/shard_map/ppermute | solution.py:149
  49.1 71.3 %collective-permute-start.45 = (f32[512,768]{1,0:T(8,128)S(1)}, f32[512,768]{1,0:T(8,128)S(1)}, u32[]{:S(2)}, u32[]{:S(2)}) collective-permute-start(f32[512,768]{1,0:T(8,128)S(1)} %get-tuple-element.112), channel_id=1, source_target_pairs={{0,1},{1,2},{2,3},{3,4},{4,5},{5,6},{6,7},{7,8},{8,9},{9,10},{10,1... | collective-permute-start | bytes 4718600 | tf_op jit(solution)/shard_map/ppermute | solution.py:229
  51.5 22.7 %collective-permute-start.17 = (f32[48,768]{1,0:T(8,128)S(1)}, f32[48,768]{1,0:T(8,128)S(1)}, u32[]{:S(2)}, u32[]{:S(2)}) collective-permute-start(f32[48,768]{1,0:T(8,128)S(1)} %add.73), channel_id=1, source_target_pairs={{0,2},{1,3},{2,0},{3,1},{4,6},{5,7},{6,4},{7,5},{8,10},{9,11},{10,... | collective-permute-start | bytes 442376 | tf_op jit(solution)/shard_map/ppermute | solution.py:149
  53.1 21.2 %collective-permute-start.19 = (f32[48,768]{1,0:T(8,128)S(1)}, f32[48,768]{1,0:T(8,128)S(1)}, u32[]{:S(2)}, u32[]{:S(2)}) collective-permute-start(f32[48,768]{1,0:T(8,128)S(1)} %get-tuple-element.89), channel_id=1, source_target_pairs={{0,1},{1,0},{2,3},{3,2},{4,5},{5,4},{6,7},{7,6},{8,9},{9,8},{10,11... | collective-permute-start | bytes 442376 | tf_op jit(solution)/shard_map/ppermute | solution.py:149
  53.5 27.5 %collective-permute-start.23 = (f32[48,768]{1,0:T(8,128)S(1)}, f32[48,768]{1,0:T(8,128)S(1)}, u32[]{:S(2)}, u32[]{:S(2)}) collective-permute-start(f32[48,768]{1,0:T(8,128)S(1)} %get-tuple-element.93), channel_id=1, source_target_pairs={{0,1},{1,0},{2,3},{3,2},{4,5},{5,4},{6,7},{7,6},{8,9},{9,8},{10,11... | collective-permute-start | bytes 442376 | tf_op jit(solution)/shard_map/ppermute | solution.py:149
  53.8 31.0 %collective-permute-start.27 = (f32[48,768]{1,0:T(8,128)S(1)}, f32[48,768]{1,0:T(8,128)S(1)}, u32[]{:S(2)}, u32[]{:S(2)}) collective-permute-start(f32[48,768]{1,0:T(8,128)S(1)} %get-tuple-element.97), channel_id=1, source_target_pairs={{0,1},{1,0},{2,3},{3,2},{4,5},{5,4},{6,7},{7,6},{8,9},{9,8},{10,11... | collective-permute-start | bytes 442376 | tf_op jit(solution)/shard_map/ppermute | solution.py:149
  74.2 6.8 %collective-permute-start.21 = (f32[48,768]{1,0:T(8,128)S(1)}, f32[48,768]{1,0:T(8,128)S(1)}, u32[]{:S(2)}, u32[]{:S(2)}) collective-permute-start(f32[48,768]{1,0:T(8,128)S(1)} %add.76), channel_id=1, source_target_pairs={{0,2},{1,3},{2,0},{3,1},{4,6},{5,7},{6,4},{7,5},{8,10},{9,11},{10,... | collective-permute-start | bytes 442376 | tf_op jit(solution)/shard_map/ppermute | solution.py:149
  74.3 9.6 %collective-permute-start.25 = (f32[48,768]{1,0:T(8,128)S(1)}, f32[48,768]{1,0:T(8,128)S(1)}, u32[]{:S(2)}, u32[]{:S(2)}) collective-permute-start(f32[48,768]{1,0:T(8,128)S(1)} %add.79), channel_id=1, source_target_pairs={{0,2},{1,3},{2,0},{3,1},{4,6},{5,7},{6,4},{7,5},{8,10},{9,11},{10,... | collective-permute-start | bytes 442376 | tf_op jit(solution)/shard_map/ppermute | solution.py:149
  81.1 8.5 %collective-permute-start.18 = (f32[48,768]{1,0:T(8,128)S(1)}, f32[48,768]{1,0:T(8,128)S(1)}, u32[]{:S(2)}, u32[]{:S(2)}) collective-permute-start(f32[48,768]{1,0:T(8,128)S(1)} %add_add_fusion.7), channel_id=1, source_target_pairs={{0,12},{1,13},{2,14},{3,15},{4,8},{5,9},{6,10},{7,11},{8,4},{9,5},... | collective-permute-start | bytes 442376 | tf_op jit(solution)/shard_map/ppermute | solution.py:149
  83.9 10.2 %collective-permute-start.22 = (f32[48,768]{1,0:T(8,128)S(1)}, f32[48,768]{1,0:T(8,128)S(1)}, u32[]{:S(2)}, u32[]{:S(2)}) collective-permute-start(f32[48,768]{1,0:T(8,128)S(1)} %add_add_fusion.6), channel_id=1, source_target_pairs={{0,8},{1,9},{2,10},{3,11},{4,12},{5,13},{6,14},{7,15},{8,0},{9,1},... | collective-permute-start | bytes 442376 | tf_op jit(solution)/shard_map/ppermute | solution.py:149
  84.8 9.3 %collective-permute-start.26 = (f32[48,768]{1,0:T(8,128)S(1)}, f32[48,768]{1,0:T(8,128)S(1)}, u32[]{:S(2)}, u32[]{:S(2)}) collective-permute-start(f32[48,768]{1,0:T(8,128)S(1)} %add_add_fusion.5), channel_id=1, source_target_pairs={{0,4},{1,5},{2,6},{3,7},{4,0},{5,1},{6,2},{7,3},{8,12},{9,13},{10,... | collective-permute-start | bytes 442376 | tf_op jit(solution)/shard_map/ppermute | solution.py:149
  94.2 8.7 %collective-permute-start.41 = (f32[48,768]{1,0:T(8,128)S(1)}, f32[48,768]{1,0:T(8,128)S(1)}, u32[]{:S(2)}, u32[]{:S(2)}) collective-permute-start(f32[48,768]{1,0:T(8,128)S(1)} %get-tuple-element.100.refs_0_.relation), channel_id=1, source_target_pairs={{0,12},{1,13},{2,14},{3,15},{4,8},{5,9},{6,10},{7,11},{8,4},{9,5},... | collective-permute-start | bytes 442376 | tf_op jit(solution)/shard_map/ppermute | solution.py:149
  97.5 11.2 %collective-permute-start.37 = (f32[48,768]{1,0:T(8,128)S(1)}, f32[48,768]{1,0:T(8,128)S(1)}, u32[]{:S(2)}, u32[]{:S(2)}) collective-permute-start(f32[48,768]{1,0:T(8,128)S(1)} %get-tuple-element.100.refs_0_.relation), channel_id=1, source_target_pairs={{0,8},{1,9},{2,10},{3,11},{4,12},{5,13},{6,14},{7,15},{8,0},{9,1},... | collective-permute-start | bytes 442376 | tf_op jit(solution)/shard_map/ppermute | solution.py:149
  97.5 12.0 %collective-permute-start.33 = (f32[48,768]{1,0:T(8,128)S(1)}, f32[48,768]{1,0:T(8,128)S(1)}, u32[]{:S(2)}, u32[]{:S(2)}) collective-permute-start(f32[48,768]{1,0:T(8,128)S(1)} %get-tuple-element.100.refs_0_.relation), channel_id=1, source_target_pairs={{0,4},{1,5},{2,6},{3,7},{4,0},{5,1},{6,2},{7,3},{8,12},{9,13},{10,... | collective-permute-start | bytes 442376 | tf_op jit(solution)/shard_map/ppermute | solution.py:149
  98.7 10.8 %collective-permute-start.31 = (f32[48,768]{1,0:T(8,128)S(1)}, f32[48,768]{1,0:T(8,128)S(1)}, u32[]{:S(2)}, u32[]{:S(2)}) collective-permute-start(f32[48,768]{1,0:T(8,128)S(1)} %get-tuple-element.100.refs_0_.relation), channel_id=1, source_target_pairs={{0,2},{1,3},{2,0},{3,1},{4,6},{5,7},{6,4},{7,5},{8,10},{9,11},{10,... | collective-permute-start | bytes 442376 | tf_op jit(solution)/shard_map/ppermute | solution.py:149
  102.9 8.0 %collective-permute-start.30 = (f32[48,768]{1,0:T(8,128)S(1)}, f32[48,768]{1,0:T(8,128)S(1)}, u32[]{:S(2)}, u32[]{:S(2)}) collective-permute-start(f32[48,768]{1,0:T(8,128)S(1)} %get-tuple-element.100.refs_0_.relation), channel_id=1, source_target_pairs={{0,1},{1,0},{2,3},{3,2},{4,5},{5,4},{6,7},{7,6},{8,9},{9,8},{10,11... | collective-permute-start | bytes 442376 | tf_op jit(solution)/shard_map/ppermute | solution.py:149
  108.8 6.5 %collective-permute-start.43 = (f32[48,768]{1,0:T(8,128)S(1)}, f32[48,768]{1,0:T(8,128)S(1)}, u32[]{:S(2)}, u32[]{:S(2)}) collective-permute-start(f32[48,768]{1,0:T(8,128)S(1)} %collective-permute-done.41.refs_12_), channel_id=1, source_target_pairs={{0,2},{1,3},{2,0},{3,1},{4,6},{5,7},{6,4},{7,5},{8,10},{9,11},{10,... | collective-permute-start | bytes 442376 | tf_op jit(solution)/shard_map/ppermute | solution.py:149
  109.5 8.9 %collective-permute-start.39 = (f32[48,768]{1,0:T(8,128)S(1)}, f32[48,768]{1,0:T(8,128)S(1)}, u32[]{:S(2)}, u32[]{:S(2)}) collective-permute-start(f32[48,768]{1,0:T(8,128)S(1)} %collective-permute-done.37.refs_8_), channel_id=1, source_target_pairs={{0,2},{1,3},{2,0},{3,1},{4,6},{5,7},{6,4},{7,5},{8,10},{9,11},{10,... | collective-permute-start | bytes 442376 | tf_op jit(solution)/shard_map/ppermute | solution.py:149
  110.9 7.5 %collective-permute-start.38 = (f32[48,768]{1,0:T(8,128)S(1)}, f32[48,768]{1,0:T(8,128)S(1)}, u32[]{:S(2)}, u32[]{:S(2)}) collective-permute-start(f32[48,768]{1,0:T(8,128)S(1)} %collective-permute-done.37.refs_8_), channel_id=1, source_target_pairs={{0,1},{1,0},{2,3},{3,2},{4,5},{5,4},{6,7},{7,6},{8,9},{9,8},{10,11... | collective-permute-start | bytes 442376 | tf_op jit(solution)/shard_map/ppermute | solution.py:149
  115.4 11.0 %collective-permute-start.34 = (f32[48,768]{1,0:T(8,128)S(1)}, f32[48,768]{1,0:T(8,128)S(1)}, u32[]{:S(2)}, u32[]{:S(2)}) collective-permute-start(f32[48,768]{1,0:T(8,128)S(1)} %collective-permute-done.33.refs_4_), channel_id=1, source_target_pairs={{0,1},{1,0},{2,3},{3,2},{4,5},{5,4},{6,7},{7,6},{8,9},{9,8},{10,11... | collective-permute-start | bytes 442376 | tf_op jit(solution)/shard_map/ppermute | solution.py:149
  118.4 8.0 %collective-permute-start.32 = (f32[48,768]{1,0:T(8,128)S(1)}, f32[48,768]{1,0:T(8,128)S(1)}, u32[]{:S(2)}, u32[]{:S(2)}) collective-permute-start(f32[48,768]{1,0:T(8,128)S(1)} %collective-permute-done.31.refs_2_), channel_id=1, source_target_pairs={{0,1},{1,0},{2,3},{3,2},{4,5},{5,4},{6,7},{7,6},{8,9},{9,8},{10,11... | collective-permute-start | bytes 442376 | tf_op jit(solution)/shard_map/ppermute | solution.py:149
  118.4 8.0 %collective-permute-start.44 = (f32[48,768]{1,0:T(8,128)S(1)}, f32[48,768]{1,0:T(8,128)S(1)}, u32[]{:S(2)}, u32[]{:S(2)}) collective-permute-start(f32[48,768]{1,0:T(8,128)S(1)} %collective-permute-done.43.refs_14_), channel_id=1, source_target_pairs={{0,1},{1,0},{2,3},{3,2},{4,5},{5,4},{6,7},{7,6},{8,9},{9,8},{10,11... | collective-permute-start | bytes 442376 | tf_op jit(solution)/shard_map/ppermute | solution.py:149
  120.4 6.0 %collective-permute-start.36 = (f32[48,768]{1,0:T(8,128)S(1)}, f32[48,768]{1,0:T(8,128)S(1)}, u32[]{:S(2)}, u32[]{:S(2)}) collective-permute-start(f32[48,768]{1,0:T(8,128)S(1)} %collective-permute-done.35.refs_6_), channel_id=1, source_target_pairs={{0,1},{1,0},{2,3},{3,2},{4,5},{5,4},{6,7},{7,6},{8,9},{9,8},{10,11... | collective-permute-start | bytes 442376 | tf_op jit(solution)/shard_map/ppermute | solution.py:149
  134.6 10.9 %collective-permute-start.52 = (f32[48,768]{1,0:T(8,128)S(1)}, f32[48,768]{1,0:T(8,128)S(1)}, u32[]{:S(2)}, u32[]{:S(2)}) collective-permute-start(f32[48,768]{1,0:T(8,128)S(1)} %get-tuple-element.137), channel_id=1, source_target_pairs={{0,1},{1,0},{2,3},{3,2},{4,5},{5,4},{6,7},{7,6},{8,9},{9,8},{10,11... | collective-permute-start | bytes 442376 | tf_op jit(solution)/shard_map/ppermute | solution.py:149
  134.8 10.7 %collective-permute-start.56 = (f32[48,768]{1,0:T(8,128)S(1)}, f32[48,768]{1,0:T(8,128)S(1)}, u32[]{:S(2)}, u32[]{:S(2)}) collective-permute-start(f32[48,768]{1,0:T(8,128)S(1)} %get-tuple-element.141), channel_id=1, source_target_pairs={{0,1},{1,0},{2,3},{3,2},{4,5},{5,4},{6,7},{7,6},{8,9},{9,8},{10,11... | collective-permute-start | bytes 442376 | tf_op jit(solution)/shard_map/ppermute | solution.py:149
  135.1 11.0 %collective-permute-start.60 = (f32[48,768]{1,0:T(8,128)S(1)}, f32[48,768]{1,0:T(8,128)S(1)}, u32[]{:S(2)}, u32[]{:S(2)}) collective-permute-start(f32[48,768]{1,0:T(8,128)S(1)} %get-tuple-element.145), channel_id=1, source_target_pairs={{0,1},{1,0},{2,3},{3,2},{4,5},{5,4},{6,7},{7,6},{8,9},{9,8},{10,11... | collective-permute-start | bytes 442376 | tf_op jit(solution)/shard_map/ppermute | solution.py:149
  135.5 10.7 %collective-permute-start.47 = (f32[48,768]{1,0:T(8,128)S(1)}, f32[48,768]{1,0:T(8,128)S(1)}, u32[]{:S(2)}, u32[]{:S(2)}) collective-permute-start(f32[48,768]{1,0:T(8,128)S(1)} %get-tuple-element.131), channel_id=1, source_target_pairs={{0,1},{1,0},{2,3},{3,2},{4,5},{5,4},{6,7},{7,6},{8,9},{9,8},{10,11... | collective-permute-start | bytes 442376 | tf_op jit(solution)/shard_map/ppermute | solution.py:149
  140.0 8.4 %collective-permute-start.49 = (f32[48,768]{1,0:T(8,128)S(1)}, f32[48,768]{1,0:T(8,128)S(1)}, u32[]{:S(2)}, u32[]{:S(2)}) collective-permute-start(f32[48,768]{1,0:T(8,128)S(1)} %add.85), channel_id=1, source_target_pairs={{0,2},{1,3},{2,0},{3,1},{4,6},{5,7},{6,4},{7,5},{8,10},{9,11},{10,... | collective-permute-start | bytes 442376 | tf_op jit(solution)/shard_map/ppermute | solution.py:149
  145.5 7.9 %collective-permute-start.55 = (f32[48,768]{1,0:T(8,128)S(1)}, f32[48,768]{1,0:T(8,128)S(1)}, u32[]{:S(2)}, u32[]{:S(2)}) collective-permute-start(f32[48,768]{1,0:T(8,128)S(1)} %get-tuple-element.139), channel_id=1, source_target_pairs={{0,1},{1,0},{2,3},{3,2},{4,5},{5,4},{6,7},{7,6},{8,9},{9,8},{10,11... | collective-permute-start | bytes 442376 | tf_op jit(solution)/shard_map/ppermute | solution.py:149
  146.1 11.5 %collective-permute-start.59 = (f32[48,768]{1,0:T(8,128)S(1)}, f32[48,768]{1,0:T(8,128)S(1)}, u32[]{:S(2)}, u32[]{:S(2)}) collective-permute-start(f32[48,768]{1,0:T(8,128)S(1)} %get-tuple-element.143), channel_id=1, source_target_pairs={{0,1},{1,0},{2,3},{3,2},{4,5},{5,4},{6,7},{7,6},{8,9},{9,8},{10,11... | collective-permute-start | bytes 442376 | tf_op jit(solution)/shard_map/ppermute | solution.py:149
  146.3 6.8 %collective-permute-start.53 = (f32[48,768]{1,0:T(8,128)S(1)}, f32[48,768]{1,0:T(8,128)S(1)}, u32[]{:S(2)}, u32[]{:S(2)}) collective-permute-start(f32[48,768]{1,0:T(8,128)S(1)} %add.88), channel_id=1, source_target_pairs={{0,2},{1,3},{2,0},{3,1},{4,6},{5,7},{6,4},{7,5},{8,10},{9,11},{10,... | collective-permute-start | bytes 442376 | tf_op jit(solution)/shard_map/ppermute | solution.py:149
  148.3 7.9 %collective-permute-start.57 = (f32[48,768]{1,0:T(8,128)S(1)}, f32[48,768]{1,0:T(8,128)S(1)}, u32[]{:S(2)}, u32[]{:S(2)}) collective-permute-start(f32[48,768]{1,0:T(8,128)S(1)} %add.91), channel_id=1, source_target_pairs={{0,2},{1,3},{2,0},{3,1},{4,6},{5,7},{6,4},{7,5},{8,10},{9,11},{10,... | collective-permute-start | bytes 442376 | tf_op jit(solution)/shard_map/ppermute | solution.py:149
  148.5 10.7 %collective-permute-start.61 = (f32[48,768]{1,0:T(8,128)S(1)}, f32[48,768]{1,0:T(8,128)S(1)}, u32[]{:S(2)}, u32[]{:S(2)}) collective-permute-start(f32[48,768]{1,0:T(8,128)S(1)} %add.94), channel_id=1, source_target_pairs={{0,2},{1,3},{2,0},{3,1},{4,6},{5,7},{6,4},{7,5},{8,10},{9,11},{10,... | collective-permute-start | bytes 442376 | tf_op jit(solution)/shard_map/ppermute | solution.py:149
  153.0 8.6 %collective-permute-start.50 = (f32[48,768]{1,0:T(8,128)S(1)}, f32[48,768]{1,0:T(8,128)S(1)}, u32[]{:S(2)}, u32[]{:S(2)}) collective-permute-start(f32[48,768]{1,0:T(8,128)S(1)} %add_add_fusion.3), channel_id=1, source_target_pairs={{0,12},{1,13},{2,14},{3,15},{4,8},{5,9},{6,10},{7,11},{8,4},{9,5},... | collective-permute-start | bytes 442376 | tf_op jit(solution)/shard_map/ppermute | solution.py:149
  153.4 12.4 %collective-permute-start.54 = (f32[48,768]{1,0:T(8,128)S(1)}, f32[48,768]{1,0:T(8,128)S(1)}, u32[]{:S(2)}, u32[]{:S(2)}) collective-permute-start(f32[48,768]{1,0:T(8,128)S(1)} %add_add_fusion.2), channel_id=1, source_target_pairs={{0,8},{1,9},{2,10},{3,11},{4,12},{5,13},{6,14},{7,15},{8,0},{9,1},... | collective-permute-start | bytes 442376 | tf_op jit(solution)/shard_map/ppermute | solution.py:149
  156.2 9.6 %collective-permute-start.58 = (f32[48,768]{1,0:T(8,128)S(1)}, f32[48,768]{1,0:T(8,128)S(1)}, u32[]{:S(2)}, u32[]{:S(2)}) collective-permute-start(f32[48,768]{1,0:T(8,128)S(1)} %add_add_fusion.1), channel_id=1, source_target_pairs={{0,4},{1,5},{2,6},{3,7},{4,0},{5,1},{6,2},{7,3},{8,12},{9,13},{10,... | collective-permute-start | bytes 442376 | tf_op jit(solution)/shard_map/ppermute | solution.py:149
  (43 other events, 430.5 us)

commit v2 on v1

--- a/solution.py
+++ b/solution.py
@@ -98,9 +98,17 @@
         pieces[r][...] = whole[r * rows : (r + 1) * rows, :]
 
 
-def tails_kernel(grad_scores, product_high, product_low, tails, state, tails_out, state_out):
+def tails_kernel(grad_scores, product_high, product_low, tails, state, *outs):
+    rows = grad_scores.shape[1]
     grad = dot3(split(grad_scores[...].T), (product_high[...], product_low[...]), NN)
-    tails_out[...], state_out[...] = adagrad(tails[...], state[...], grad)
+    first = state.shape[0] - 1 if state.shape[0] == 1 else rows
+    new, new_state = adagrad(tails[:rows, :], state[first : first + 1, :rows], grad)
+    if len(outs) == 2:
+        outs[0][...], outs[1][...] = new, new_state
+    else:
+        outs[0][:rows, :] = new
+        outs[0][rows:, :] = jnp.zeros((outs[0].shape[0] - rows, outs[0].shape[1]), F32)
+        outs[0][rows : rows + 1, :rows] = new_state
 
 
 def heads_kernel(slots, last, me_ref, grad_high, grad_low, rel_high, rel_low, heads, state, *rest):
@@ -117,7 +125,7 @@
 
 
 def split_kernel(tails, high, low):
-    high[...], low[...] = split(tails[...])
+    high[...], low[...] = split(tails[: high.shape[0], :])
 
 
 def relation_kernel(relation, state, *rest):
@@ -139,7 +147,7 @@
         in_specs=specs,
         out_specs=[VMEM] * len(outs),
         scratch_shapes=[pltpu.VMEM(s, t) for s, t in scratch],
-        compiler_params=pltpu.CompilerParams(vmem_limit_bytes=48 * 1024 * 1024),
+        compiler_params=pltpu.CompilerParams(vmem_limit_bytes=20 * 1024 * 1024),
         cost_estimate=pl.CostEstimate(flops=flops, bytes_accessed=moved, transcendentals=0),
     )(*args)
 
@@ -149,29 +157,38 @@
     return lax.ppermute(value, "blk", [(i, i ^ mask) for i in range(n)])
 
 
-def gather_blocks(own):
+def after(value, *others):
+    return lax.optimization_barrier((value, *others))[0]
+
+
+def gather_blocks(own, beside=None):
     n = lax.axis_size("blk")
     far = range(4, n, 4)
-    got = {0: own, 2: partner(own, 2)}
-    for k in far:
+    got = {0: own}
+    for k in (*far, 2):
         got[k] = partner(own, k)
+    if beside:
+        got[4] = after(got[4], *beside())
     for k in far:
         got[k ^ 2] = partner(got[k], 2)
+    before = ()
     for k in (0, *far):
-        got[k ^ 1] = partner(got[k], 1)
-        got[k ^ 3] = partner(got[k ^ 2], 1)
+        first, second = after(got[k], *before), after(got[k ^ 2], *before)
+        got[k ^ 1], got[k ^ 3] = partner(first, 1), partner(second, 1)
+        before = got[k ^ 1], got[k ^ 3]
     return [got[r] for r in range(n)]
 
 
 def scatter_blocks(pieces):
     n = len(pieces)
+    order = (*range(n - 4, 0, -4), 0)
+    across = {k: pieces[k ^ 2] + partner(pieces[k ^ 3], 1) for k in order}
+    here = {k: pieces[k] + partner(pieces[k ^ 1], 1) for k in order}
     terms = []
-    for k in (*range(n - 4, 0, -4), 0):
-        across = pieces[k ^ 2] + partner(pieces[k ^ 3], 1)
-        here = pieces[k] + partner(pieces[k ^ 1], 1)
-        here = here + partner(across, 2)
-        terms.append(partner(here, k) if k else here)
-    return terms
+    for k in order:
+        total = here[k] + partner(across[k], 2)
+        terms.append(partner(total, k) if k else total)
+    return terms, [across[k] for k in order]
 
 
 def body(heads, head_state, tails, tail_state, relation, relation_state, pos_head, pos_tail):
@@ -180,16 +197,16 @@
     by_blocks = share % 16 == 0 and n & (n - 1) == 0 and n >= 4
     slots = n if by_blocks else 1
     me = (lax.axis_index("blk").astype(jnp.int32) if by_blocks else jnp.int32(0)).reshape(1)
-    head_rows, tail_rows = heads.shape[0], tails.shape[0]
+    head_rows, (tail_rows, _), tails_shape = heads.shape[0], tails.shape, tails.shape
     head_state, tail_state, relation_state = (s.reshape(1, -1) for s in (head_state, tail_state, relation_state))
 
-    def gathered(rows):
-        return gather_blocks(rows) if by_blocks else [lax.all_gather(rows, "blk", axis=0, tiled=True)]
+    def gathered(rows, beside=None):
+        return gather_blocks(rows, beside) if by_blocks else [lax.all_gather(rows, "blk", axis=0, tiled=True)]
 
     def scattered(pieces):
         if by_blocks:
             return scatter_blocks(pieces)
-        return [lax.psum_scatter(pieces[0], "blk", scatter_dimension=0, tiled=True)]
+        return [lax.psum_scatter(pieces[0], "blk", scatter_dimension=0, tiled=True)], []
 
     head_parts = [((head_rows, width), BF16)] * 2 + [((width, head_rows), BF16)] * 2
     turned = [((width, head_rows), F32)] * 2
@@ -209,7 +226,7 @@
     head_half, tail_half = parts[:4], parts[4:]
     for bucket in range(2):
         last = bucket == 1
-        blocks = gathered(relation)
+        blocks = gathered(relation, lambda: list(parts) + [marks]) if bucket == 0 else gathered(relation)
         out = call(
             functools.partial(bucket_kernel, bucket, slots),
             [*relation_parts, *row_parts, table, *row_parts, *[block] * slots],
@@ -217,22 +234,23 @@
             flops=6 * head_rows * width * (2 * width + 2 * tail_rows),
         )
         relation_half, product, grad_scores, grad_product, pieces = out[0:2], out[2:4], out[4], out[5:7], out[7:]
-        terms = scattered(pieces)
-        tails, tail_state = call(
+        terms, summed = scattered(pieces)
+        grown = (tail_rows + 8, width)
+        out = call(
             tails_kernel,
-            [(tails.shape, F32), (tail_state.shape, F32)],
-            [grad_scores, *product, tails, tail_state],
+            [(tails_shape, F32), (tail_state.shape, F32)] if last else [(grown, F32)],
+            [after(grad_scores, *summed), *product, tails, tails if last else tail_state],
             flops=6 * head_rows * width * tail_rows,
         )
-        if not last:
-            tails, tail_state = (
-                lax.ppermute(v, "blk", [(i, (i + 1) % n) for i in range(n)]) for v in (tails, tail_state)
-            )
+        if last:
+            tails, tail_state = out
+        else:
+            tails = lax.ppermute(out[0], "blk", [(i, (i + 1) % n) for i in range(n)])
             tail_half = call(split_kernel, tail_parts, [tails])
         out = call(
             functools.partial(heads_kernel, slots, last),
             [(heads.shape, F32), (head_state.shape, F32), *([] if last else head_parts)],
-            [me, *grad_product, *relation_half, heads, head_state],
+            [me, after(grad_product[0], *summed), grad_product[1], *relation_half, heads, head_state],
             scratch=[*relation_parts, *([] if last else turned)],
             smem_first=True,
             flops=6 * head_rows * width * width,

time: 167 us -> 135 us (0.81)
  waiting for transfers between devices: 85 us -> 42.2 us
  starting transfers between devices: 40 us -> 68.1 us
  local copies, waits for them, and re-layouts: 12.4 us -> 3.95 us
  Pallas kernels: 27.8 us -> 19.6 us
    ppermute x60, waiting for transfers between devices: 80.7 us -> 42.2 us  [partner(): return lax.ppermute(value, 'blk', [(i, i ^ mask) for i in range(n)])]
    ppermute x60, starting transfers between devices: 38.8 us -> 68.1 us  [partner(): return lax.ppermute(value, 'blk', [(i, i ^ mask) for i in range(n)])]
    unnamed x58 -> x20, local copies, waits for them, and re-layouts: 12.4 us -> 3.95 us
    pallas_call x10, Pallas kernels: 27.8 us -> 19.6 us  [call(): pl.pallas_call(kernel, out_shape=[jax.ShapeDtypeStruct(s, t) for s, t in...]
    ppermute x2 -> x1, waiting for transfers between devices: 4.27 us -> 0.01 us  [body(): tails = lax.ppermute(out[0], 'blk', [(i, (i + 1) % n) for i in range(n)])]
  transfers between devices with their start and end apart: 62 -> 61, of which waited for: 22 -> 19; matrix products, arithmetic and copies ran while one was open for 0% -> 0% of each run, Pallas kernels for 7% -> 7%
where the time goes in v2:
time: 135 us
  starting transfers between devices  68.1 us (50%)
  waiting for transfers between devices  42.2 us (31%)
  Pallas kernels  19.6 us (15%)
  local copies, waits for them, and re-layouts  3.95 us (3%)
    ppermute x60, starting transfers between devices, partner(): return lax.ppermute(value, 'blk', [(i, i ^ mask) for i in range(n)])  68.1 us
    ppermute x60, waiting for transfers between devices, partner(): return lax.ppermute(value, 'blk', [(i, i ^ mask) for i in range(n)])  42.2 us
    pallas_call x10, Pallas kernels, call(): pl.pallas_call(kernel, out_shape=[jax.ShapeDtypeStruct(s, t) for s, t in...  19.6 us
    unnamed x20, local copies, waits for them, and re-layouts  3.95 us
  transfers between devices with their start and end apart: 61, of which 19 were waited for; matrix products, arithmetic and copies ran while one was open for 0% of the time, Pallas kernels for 7%

profile of v2, /device:TPU:0, one launch (start us, length us, event | category | flops | bytes accessed | tf_op | source)
XLA Modules:
  0.0 135.2 jit_solution(18109763392755529261)
XLA Ops:
  0.6 3.0 %collective-permute-start.1 = (f32[48,768]{1,0:T(8,128)}, f32[48,768]{1,0:T(8,128)S(1)}, u32[]{:S(2)}, u32[]{:S(2)}) collective-permute-start(f32[48,768]{1,0:T(8,128)} %relation.1), channel_id=1, source_target_pairs={{0,2},{1,3},{2,0},{3,1},{4,6},{5,7},{6,4},{7,5},{8,10},{9,11},{10,... | collective-permute-start | bytes 442376 | tf_op jit(solution)/shard_map/ppermute | solution.py:157
  3.7 1.6 %collective-permute-start.3 = (f32[48,768]{1,0:T(8,128)}, f32[48,768]{1,0:T(8,128)S(1)}, u32[]{:S(2)}, u32[]{:S(2)}) collective-permute-start(f32[48,768]{1,0:T(8,128)} %relation.1), channel_id=1, source_target_pairs={{0,4},{1,5},{2,6},{3,7},{4,0},{5,1},{6,2},{7,3},{8,12},{9,13},{10,... | collective-permute-start | bytes 442376 | tf_op jit(solution)/shard_map/ppermute | solution.py:157
  5.2 2.6 %collective-permute-start.7 = (f32[48,768]{1,0:T(8,128)}, f32[48,768]{1,0:T(8,128)S(1)}, u32[]{:S(2)}, u32[]{:S(2)}) collective-permute-start(f32[48,768]{1,0:T(8,128)} %relation.1), channel_id=1, source_target_pairs={{0,8},{1,9},{2,10},{3,11},{4,12},{5,13},{6,14},{7,15},{8,0},{9,1},... | collective-permute-start | bytes 442376 | tf_op jit(solution)/shard_map/ppermute | solution.py:157
  7.8 1.4 %copy-done = f32[512,768]{1,0:T(8,128)S(1)} copy-done((f32[512,768]{1,0:T(8,128)S(1)}, f32[512,768]{1,0:T(8,128)}, u32[]{:S(2)}) %copy-start) | copy-done | bytes 1572888
  9.2 1.1 copy-done.2
  11.1 0.7 copy-done.6
  11.8 1.1 shard_map.127
  14.0 1.2 collective-permute-start.11
  15.1 1.5 %collective-permute-start.9 = (f32[48,768]{1,0:T(8,128)S(1)}, f32[48,768]{1,0:T(8,128)S(1)}, u32[]{:S(2)}, u32[]{:S(2)}) collective-permute-start(f32[48,768]{1,0:T(8,128)S(1)} %collective-permute-done.7.refs_8_), channel_id=1, source_target_pairs={{0,2},{1,3},{2,0},{3,1},{4,6},{5,7},{6,4},{7,5},{8,10},{9,11},{10,... | collective-permute-start | bytes 442376 | tf_op jit(solution)/shard_map/ppermute | solution.py:157
  16.7 3.5 %collective-permute-done.5.refs_6_ = f32[48,768]{1,0:T(8,128)S(1)} collective-permute-done((f32[48,768]{1,0:T(8,128)S(1)}, f32[48,768]{1,0:T(8,128)S(1)}, u32[]{:S(2)}, u32[]{:S(2)}) %collective-permute-start.5) | collective-permute-done | bytes 147488 | tf_op jit(solution)/shard_map/ppermute | solution.py:157
  20.2 1.2 collective-permute-done.11.refs_12_
  21.4 1.5 %collective-permute-start.13 = (f32[48,768]{1,0:T(8,128)S(1)}, f32[48,768]{1,0:T(8,128)S(1)}, u32[]{:S(2)}, u32[]{:S(2)}) collective-permute-start(f32[48,768]{1,0:T(8,128)S(1)} %collective-permute-done.11.refs_12_), channel_id=1, source_target_pairs={{0,2},{1,3},{2,0},{3,1},{4,6},{5,7},{6,4},{7,5},{8,10},{9,11},{10,... | collective-permute-start | bytes 442376 | tf_op jit(solution)/shard_map/ppermute | solution.py:157
  23.5 3.0 %collective-permute-done.13.refs_14_ = f32[48,768]{1,0:T(8,128)S(1)} collective-permute-done((f32[48,768]{1,0:T(8,128)S(1)}, f32[48,768]{1,0:T(8,128)S(1)}, u32[]{:S(2)}, u32[]{:S(2)}) %collective-permute-start.13) | collective-permute-done | bytes 147488 | tf_op jit(solution)/shard_map/ppermute | solution.py:157
  27.1 0.9 collective-permute-done.12.refs_13_
  28.2 4.9 %shard_map.128 = (bf16[768,768]{1,0:T(8,128)(2,1)S(1)}, bf16[768,768]{1,0:T(8,128)(2,1)S(1)}, bf16[256,768]{1,0:T(8,128)(2,1)S(1)}, bf16[256,768]{1,0:T(8,128)(2...) custom-call(f32[48,768]{1,0:T(8,128)S(1)} %copy-done.4, ...), custom_call_target="tpu_custom_call" | custom-call | flops 3019898880 | bytes 6553600 | tf_op jit(solution)/shard_map/pallas_call | solution.py:144
  34.6 1.6 %collective-permute-start.17 = (f32[48,768]{1,0:T(8,128)S(1)}, f32[48,768]{1,0:T(8,128)S(1)}, u32[]{:S(2)}, u32[]{:S(2)}) collective-permute-start(f32[48,768]{1,0:T(8,128)S(1)} %add.73), channel_id=1, source_target_pairs={{0,2},{1,3},{2,0},{3,1},{4,6},{5,7},{6,4},{7,5},{8,10},{9,11},{10,... | collective-permute-start | bytes 442376 | tf_op jit(solution)/shard_map/ppermute | solution.py:157
  36.9 1.1 shard_map.131
  38.6 2.1 %collective-permute-done.17 = f32[48,768]{1,0:T(8,128)S(1)} collective-permute-done((f32[48,768]{1,0:T(8,128)S(1)}, f32[48,768]{1,0:T(8,128)S(1)}, u32[]{:S(2)}, u32[]{:S(2)}) %collective-permute-start.17) | collective-permute-done | bytes 147488 | tf_op jit(solution)/shard_map/ppermute | solution.py:157
  40.8 2.0 %collective-permute-start.25 = (f32[48,768]{1,0:T(8,128)S(1)}, f32[48,768]{1,0:T(8,128)S(1)}, u32[]{:S(2)}, u32[]{:S(2)}) collective-permute-start(f32[48,768]{1,0:T(8,128)S(1)} %add.79), channel_id=1, source_target_pairs={{0,2},{1,3},{2,0},{3,1},{4,6},{5,7},{6,4},{7,5},{8,10},{9,11},{10,... | collective-permute-start | bytes 442376 | tf_op jit(solution)/shard_map/ppermute | solution.py:157
  42.8 1.6 %collective-permute-done.21 = f32[48,768]{1,0:T(8,128)S(1)} collective-permute-done((f32[48,768]{1,0:T(8,128)S(1)}, f32[48,768]{1,0:T(8,128)S(1)}, u32[]{:S(2)}, u32[]{:S(2)}) %collective-permute-start.21) | collective-permute-done | bytes 147488 | tf_op jit(solution)/shard_map/ppermute | solution.py:157
  44.4 1.0 collective-permute-start.29
  45.4 0.7 collective-permute-start.18
  46.2 0.8 collective-permute-done.25
  47.0 7.7 %collective-permute-start.22 = (f32[48,768]{1,0:T(8,128)S(1)}, f32[48,768]{1,0:T(8,128)S(1)}, u32[]{:S(2)}, u32[]{:S(2)}) collective-permute-start(f32[48,768]{1,0:T(8,128)S(1)} %add_add_fusion.6), channel_id=1, source_target_pairs={{0,8},{1,9},{2,10},{3,11},{4,12},{5,13},{6,14},{7,15},{8,0},{9,1},... | collective-permute-start | bytes 442376 | tf_op jit(solution)/shard_map/ppermute | solution.py:157
  54.8 10.9 %collective-permute-start.26 = (f32[48,768]{1,0:T(8,128)S(1)}, f32[48,768]{1,0:T(8,128)S(1)}, u32[]{:S(2)}, u32[]{:S(2)}) collective-permute-start(f32[48,768]{1,0:T(8,128)S(1)} %add_add_fusion.5), channel_id=1, source_target_pairs={{0,4},{1,5},{2,6},{3,7},{4,0},{5,1},{6,2},{7,3},{8,12},{9,13},{10,... | collective-permute-start | bytes 442376 | tf_op jit(solution)/shard_map/ppermute | solution.py:157
  65.7 1.1 collective-permute-done.29
  66.9 3.0 %collective-permute-done.26.rest_2_ = f32[48,768]{1,0:T(8,128)S(1)} collective-permute-done((f32[48,768]{1,0:T(8,128)S(1)}, f32[48,768]{1,0:T(8,128)S(1)}, u32[]{:S(2)}, u32[]{:S(2)}) %collective-permute-start.26) | collective-permute-done | bytes 147488 | tf_op jit(solution)/shard_map/ppermute | solution.py:157
  70.0 2.5 %collective-permute-start.33 = (f32[48,768]{1,0:T(8,128)S(1)}, f32[48,768]{1,0:T(8,128)S(1)}, u32[]{:S(2)}, u32[]{:S(2)}) collective-permute-start(f32[48,768]{1,0:T(8,128)S(1)} %get-tuple-element.122.refs_0_.relation), channel_id=1, source_target_pairs={{0,4},{1,5},{2,6},{3,7},{4,0},{5,1},{6,2},{7,3},{8,12},{9,13},{10,... | collective-permute-start | bytes 442376 | tf_op jit(solution)/shard_map/ppermute | solution.py:157
  72.6 4.5 %collective-permute-start.31 = (f32[48,768]{1,0:T(8,128)S(1)}, f32[48,768]{1,0:T(8,128)S(1)}, u32[]{:S(2)}, u32[]{:S(2)}) collective-permute-start(f32[48,768]{1,0:T(8,128)S(1)} %get-tuple-element.122.refs_0_.relation), channel_id=1, source_target_pairs={{0,2},{1,3},{2,0},{3,1},{4,6},{5,7},{6,4},{7,5},{8,10},{9,11},{10,... | collective-permute-start | bytes 442376 | tf_op jit(solution)/shard_map/ppermute | solution.py:157
  77.2 6.6 %collective-permute-start.35 = (f32[48,768]{1,0:T(8,128)S(1)}, f32[48,768]{1,0:T(8,128)S(1)}, u32[]{:S(2)}, u32[]{:S(2)}) collective-permute-start(f32[48,768]{1,0:T(8,128)S(1)} %collective-permute-done.33.refs_4_), channel_id=1, source_target_pairs={{0,2},{1,3},{2,0},{3,1},{4,6},{5,7},{6,4},{7,5},{8,10},{9,11},{10,... | collective-permute-start | bytes 442376 | tf_op jit(solution)/shard_map/ppermute | solution.py:157
  83.9 1.6 %collective-permute-start.41 = (f32[48,768]{1,0:T(8,128)S(1)}, f32[48,768]{1,0:T(8,128)S(1)}, u32[]{:S(2)}, u32[]{:S(2)}) collective-permute-start(f32[48,768]{1,0:T(8,128)S(1)} %get-tuple-element.122.refs_0_.relation), channel_id=1, source_target_pairs={{0,12},{1,13},{2,14},{3,15},{4,8},{5,9},{6,10},{7,11},{8,4},{9,5},... | collective-permute-start | bytes 442376 | tf_op jit(solution)/shard_map/ppermute | solution.py:157
  85.4 1.5 %collective-permute-done.37.refs_8_ = f32[48,768]{1,0:T(8,128)S(1)} collective-permute-done((f32[48,768]{1,0:T(8,128)S(1)}, f32[48,768]{1,0:T(8,128)S(1)}, u32[]{:S(2)}, u32[]{:S(2)}) %collective-permute-start.37) | collective-permute-done | bytes 147488 | tf_op jit(solution)/shard_map/ppermute | solution.py:157
  87.5 4.5 %collective-permute-done.41.refs_12_ = f32[48,768]{1,0:T(8,128)S(1)} collective-permute-done((f32[48,768]{1,0:T(8,128)S(1)}, f32[48,768]{1,0:T(8,128)S(1)}, u32[]{:S(2)}, u32[]{:S(2)}) %collective-permute-start.41) | collective-permute-done | bytes 147488 | tf_op jit(solution)/shard_map/ppermute | solution.py:157
  92.6 4.7 %collective-permute-done.43.refs_14_ = f32[48,768]{1,0:T(8,128)S(1)} collective-permute-done((f32[48,768]{1,0:T(8,128)S(1)}, f32[48,768]{1,0:T(8,128)S(1)}, u32[]{:S(2)}, u32[]{:S(2)}) %collective-permute-start.43) | collective-permute-done | bytes 147488 | tf_op jit(solution)/shard_map/ppermute | solution.py:157
  97.9 1.9 %shard_map.130 = (f32[256,768]{1,0:T(8,128)S(1)}, f32[1,256]{1,0:T(1,128)S(1)}, bf16[256,768]{1,0:T(8,128)(2,1)S(1)}, bf16[256,768]{1,0:T(8,128)(2,1)S(1)}, bf16...) custom-call(s32[1]{0:T(128)} %bitcast.me_ref, bf16[256,768]{1,0:T(8,128)(2,1)S(1)} %get-tuple-element.130.grad_high, ...), custom_call_target="tpu_custom_call" | custom-call | flops 905969664 | bytes 3933188 | tf_op jit(solution)/shard_map/pallas_call | solution.py:144
  100.1 4.9 %shard_map.133 = (bf16[768,768]{1,0:T(8,128)(2,1)S(1)}, bf16[768,768]{1,0:T(8,128)(2,1)S(1)}, bf16[256,768]{1,0:T(8,128)(2,1)S(1)}, bf16[256,768]{1,0:T(8,128)(2...) custom-call(f32[48,768]{1,0:T(8,128)S(1)} %get-tuple-element.122.ref, ...), custom_call_target="tpu_custom_call" | custom-call | flops 3019898880 | bytes 6553600 | tf_op jit(solution)/shard_map/pallas_call | solution.py:144
  107.7 2.2 %shard_map.135 = (f32[512,768]{1,0:T(8,128)}, f32[1,512]{1,0:T(1,128)}) custom-call(f32[256,512]{1,0:T(8,128)S(1)} %get-tuple-element.162.grad_scores, bf16[256,768]{1,0:T(8,128)(2,1)S(1)} %get-tuple-element.163.product_high, bf16[256,768]{1,0:T(8,128)(2,1)S(1)} %get-tuple-element.164.product_low, f32[520,768]{1,0:T(8,128)S(1)} %collective-permute-done.45.tails.state, ...), custom_call_target="tpu_custom_call" | custom-call | flops 603979776 | bytes 4505600 | tf_op jit(solution)/shard_map/pallas_call | solution.py:144
  109.9 2.3 %shard_map.134 = (f32[256,768]{1,0:T(8,128)}, f32[1,256]{1,0:T(1,128)}) custom-call(s32[1]{0:T(128)} %bitcast.me_ref, bf16[256,768]{1,0:T(8,128)(2,1)S(1)} %get-tuple-element.153.grad_high, bf16[256,768]{1,0:T(8,128)(2,1)S(1)} %get-tuple-element.154.grad_low, bf16[768,768]{1,0:T(8,128)(2,1)S(1)} %get-tuple-element.155.rel_high, ...), custom_call_target="tpu_custom_call" | custom-call | flops 905969664 | bytes 3933188 | tf_op jit(solution)/shard_map/pallas_call | solution.py:144
  112.2 1.6 %collective-permute-start.54 = (f32[48,768]{1,0:T(8,128)S(1)}, f32[48,768]{1,0:T(8,128)S(1)}, u32[]{:S(2)}, u32[]{:S(2)}) collective-permute-start(f32[48,768]{1,0:T(8,128)S(1)} %add.85), channel_id=1, source_target_pairs={{0,2},{1,3},{2,0},{3,1},{4,6},{5,7},{6,4},{7,5},{8,10},{9,11},{10,... | collective-permute-start | bytes 442376 | tf_op jit(solution)/shard_map/ppermute | solution.py:157
  114.3 1.7 %collective-permute-start.60 = (f32[48,768]{1,0:T(8,128)S(1)}, f32[48,768]{1,0:T(8,128)S(1)}, u32[]{:S(2)}, u32[]{:S(2)}) collective-permute-start(f32[48,768]{1,0:T(8,128)S(1)} %add.87), channel_id=1, source_target_pairs={{0,2},{1,3},{2,0},{3,1},{4,6},{5,7},{6,4},{7,5},{8,10},{9,11},{10,... | collective-permute-start | bytes 442376 | tf_op jit(solution)/shard_map/ppermute | solution.py:157
  116.0 2.9 %collective-permute-done.54 = f32[48,768]{1,0:T(8,128)S(1)} collective-permute-done((f32[48,768]{1,0:T(8,128)S(1)}, f32[48,768]{1,0:T(8,128)S(1)}, u32[]{:S(2)}, u32[]{:S(2)}) %collective-permute-start.54) | collective-permute-done | bytes 147488 | tf_op jit(solution)/shard_map/ppermute | solution.py:157
  118.9 0.9 collective-permute-start.52
  119.8 2.2 %collective-permute-start.55 = (f32[48,768]{1,0:T(8,128)S(1)}, f32[48,768]{1,0:T(8,128)S(1)}, u32[]{:S(2)}, u32[]{:S(2)}) collective-permute-start(f32[48,768]{1,0:T(8,128)S(1)} %add_add_fusion.2), channel_id=1, source_target_pairs={{0,8},{1,9},{2,10},{3,11},{4,12},{5,13},{6,14},{7,15},{8,0},{9,1},... | collective-permute-start | bytes 442376 | tf_op jit(solution)/shard_map/ppermute | solution.py:157
  122.0 1.6 %collective-permute-start.58 = (f32[48,768]{1,0:T(8,128)S(1)}, f32[48,768]{1,0:T(8,128)S(1)}, u32[]{:S(2)}, u32[]{:S(2)}) collective-permute-start(f32[48,768]{1,0:T(8,128)S(1)} %add_add_fusion.1), channel_id=1, source_target_pairs={{0,4},{1,5},{2,6},{3,7},{4,0},{5,1},{6,2},{7,3},{8,12},{9,13},{10,... | collective-permute-start | bytes 442376 | tf_op jit(solution)/shard_map/ppermute | solution.py:157
  123.7 0.9 collective-permute-done.60
  124.7 2.8 %collective-permute-done.52.rest_0_ = f32[48,768]{1,0:T(8,128)S(1)} collective-permute-done((f32[48,768]{1,0:T(8,128)S(1)}, f32[48,768]{1,0:T(8,128)S(1)}, u32[]{:S(2)}, u32[]{:S(2)}) %collective-permute-start.52) | collective-permute-done | bytes 147488 | tf_op jit(solution)/shard_map/ppermute | solution.py:157
  127.4 6.9 %collective-permute-done.55.rest_1_ = f32[48,768]{1,0:T(8,128)S(1)} collective-permute-done((f32[48,768]{1,0:T(8,128)S(1)}, f32[48,768]{1,0:T(8,128)S(1)}, u32[]{:S(2)}, u32[]{:S(2)}) %collective-permute-start.55) | collective-permute-done | bytes 147488 | tf_op jit(solution)/shard_map/ppermute | solution.py:157
  134.4 0.8 shard_map.136
  (120 shorter events, 11.5 us)
Async XLA Ops:
  0.6 12.2 %collective-permute-start.1 = (f32[48,768]{1,0:T(8,128)}, f32[48,768]{1,0:T(8,128)S(1)}, u32[]{:S(2)}, u32[]{:S(2)}) collective-permute-start(f32[48,768]{1,0:T(8,128)} %relation.1), channel_id=1, source_target_pairs={{0,2},{1,3},{2,0},{3,1},{4,6},{5,7},{6,4},{7,5},{8,10},{9,11},{10,... | collective-permute-start | bytes 442376 | tf_op jit(solution)/shard_map/ppermute | solution.py:157
  3.7 9.8 %collective-permute-start.3 = (f32[48,768]{1,0:T(8,128)}, f32[48,768]{1,0:T(8,128)S(1)}, u32[]{:S(2)}, u32[]{:S(2)}) collective-permute-start(f32[48,768]{1,0:T(8,128)} %relation.1), channel_id=1, source_target_pairs={{0,4},{1,5},{2,6},{3,7},{4,0},{5,1},{6,2},{7,3},{8,12},{9,13},{10,... | collective-permute-start | bytes 442376 | tf_op jit(solution)/shard_map/ppermute | solution.py:157
  5.2 9.9 %collective-permute-start.7 = (f32[48,768]{1,0:T(8,128)}, f32[48,768]{1,0:T(8,128)S(1)}, u32[]{:S(2)}, u32[]{:S(2)}) collective-permute-start(f32[48,768]{1,0:T(8,128)} %relation.1), channel_id=1, source_target_pairs={{0,8},{1,9},{2,10},{3,11},{4,12},{5,13},{6,14},{7,15},{8,0},{9,1},... | collective-permute-start | bytes 442376 | tf_op jit(solution)/shard_map/ppermute | solution.py:157
  7.8 8.8 %collective-permute-start = (f32[48,768]{1,0:T(8,128)}, f32[48,768]{1,0:T(8,128)S(1)}, u32[]{:S(2)}, u32[]{:S(2)}) collective-permute-start(f32[48,768]{1,0:T(8,128)} %relation.1), channel_id=1, source_target_pairs={{0,1},{1,0},{2,3},{3,2},{4,5},{5,4},{6,7},{7,6},{8,9},{9,8},{10,11... | collective-permute-start | bytes 442376 | tf_op jit(solution)/shard_map/ppermute | solution.py:157
  12.9 3.8 %collective-permute-start.2 = (f32[48,768]{1,0:T(8,128)S(1)}, f32[48,768]{1,0:T(8,128)S(1)}, u32[]{:S(2)}, u32[]{:S(2)}) collective-permute-start(f32[48,768]{1,0:T(8,128)S(1)} %collective-permute-done.1.refs_2_), channel_id=1, source_target_pairs={{0,1},{1,0},{2,3},{3,2},{4,5},{5,4},{6,7},{7,6},{8,9},{9,8},{10,11... | collective-permute-start | bytes 442376 | tf_op jit(solution)/shard_map/ppermute | solution.py:157
  13.5 6.7 %collective-permute-start.5 = (f32[48,768]{1,0:T(8,128)S(1)}, f32[48,768]{1,0:T(8,128)S(1)}, u32[]{:S(2)}, u32[]{:S(2)}) collective-permute-start(f32[48,768]{1,0:T(8,128)S(1)} %collective-permute-done.3.refs_4_), channel_id=1, source_target_pairs={{0,2},{1,3},{2,0},{3,1},{4,6},{5,7},{6,4},{7,5},{8,10},{9,11},{10,... | collective-permute-start | bytes 442376 | tf_op jit(solution)/shard_map/ppermute | solution.py:157
  14.0 7.5 %collective-permute-start.11 = (f32[48,768]{1,0:T(8,128)S(1)}, f32[48,768]{1,0:T(8,128)S(1)}, u32[]{:S(2)}, u32[]{:S(2)}) collective-permute-start(f32[48,768]{1,0:T(8,128)S(1)} %copy-done.4), channel_id=1, source_target_pairs={{0,12},{1,13},{2,14},{3,15},{4,8},{5,9},{6,10},{7,11},{8,4},{9,5},... | collective-permute-start | bytes 442376 | tf_op jit(solution)/shard_map/ppermute | solution.py:157
  15.1 7.8 %collective-permute-start.9 = (f32[48,768]{1,0:T(8,128)S(1)}, f32[48,768]{1,0:T(8,128)S(1)}, u32[]{:S(2)}, u32[]{:S(2)}) collective-permute-start(f32[48,768]{1,0:T(8,128)S(1)} %collective-permute-done.7.refs_8_), channel_id=1, source_target_pairs={{0,2},{1,3},{2,0},{3,1},{4,6},{5,7},{6,4},{7,5},{8,10},{9,11},{10,... | collective-permute-start | bytes 442376 | tf_op jit(solution)/shard_map/ppermute | solution.py:157
  16.6 6.3 %collective-permute-start.4 = (f32[48,768]{1,0:T(8,128)S(1)}, f32[48,768]{1,0:T(8,128)S(1)}, u32[]{:S(2)}, u32[]{:S(2)}) collective-permute-start(f32[48,768]{1,0:T(8,128)S(1)} %collective-permute-done.3.refs_4_), channel_id=1, source_target_pairs={{0,1},{1,0},{2,3},{3,2},{4,5},{5,4},{6,7},{7,6},{8,9},{9,8},{10,11... | collective-permute-start | bytes 442376 | tf_op jit(solution)/shard_map/ppermute | solution.py:157
  21.4 5.1 %collective-permute-start.13 = (f32[48,768]{1,0:T(8,128)S(1)}, f32[48,768]{1,0:T(8,128)S(1)}, u32[]{:S(2)}, u32[]{:S(2)}) collective-permute-start(f32[48,768]{1,0:T(8,128)S(1)} %collective-permute-done.11.refs_12_), channel_id=1, source_target_pairs={{0,2},{1,3},{2,0},{3,1},{4,6},{5,7},{6,4},{7,5},{8,10},{9,11},{10,... | collective-permute-start | bytes 442376 | tf_op jit(solution)/shard_map/ppermute | solution.py:157
  23.0 3.6 %collective-permute-start.8 = (f32[48,768]{1,0:T(8,128)S(1)}, f32[48,768]{1,0:T(8,128)S(1)}, u32[]{:S(2)}, u32[]{:S(2)}) collective-permute-start(f32[48,768]{1,0:T(8,128)S(1)} %collective-permute-done.7.refs_8_), channel_id=1, source_target_pairs={{0,1},{1,0},{2,3},{3,2},{4,5},{5,4},{6,7},{7,6},{8,9},{9,8},{10,11... | collective-permute-start | bytes 442376 | tf_op jit(solution)/shard_map/ppermute | solution.py:157
  23.0 3.5 %collective-permute-start.10 = (f32[48,768]{1,0:T(8,128)S(1)}, f32[48,768]{1,0:T(8,128)S(1)}, u32[]{:S(2)}, u32[]{:S(2)}) collective-permute-start(f32[48,768]{1,0:T(8,128)S(1)} %collective-permute-done.9.refs_10_), channel_id=1, source_target_pairs={{0,1},{1,0},{2,3},{3,2},{4,5},{5,4},{6,7},{7,6},{8,9},{9,8},{10,11... | collective-permute-start | bytes 442376 | tf_op jit(solution)/shard_map/ppermute | solution.py:157
  34.2 3.8 %collective-permute-start.15 = (f32[48,768]{1,0:T(8,128)S(1)}, f32[48,768]{1,0:T(8,128)S(1)}, u32[]{:S(2)}, u32[]{:S(2)}) collective-permute-start(f32[48,768]{1,0:T(8,128)S(1)} %get-tuple-element.107), channel_id=1, source_target_pairs={{0,1},{1,0},{2,3},{3,2},{4,5},{5,4},{6,7},{7,6},{8,9},{9,8},{10,11... | collective-permute-start | bytes 442376 | tf_op jit(solution)/shard_map/ppermute | solution.py:157
  34.6 6.1 %collective-permute-start.17 = (f32[48,768]{1,0:T(8,128)S(1)}, f32[48,768]{1,0:T(8,128)S(1)}, u32[]{:S(2)}, u32[]{:S(2)}) collective-permute-start(f32[48,768]{1,0:T(8,128)S(1)} %add.73), channel_id=1, source_target_pairs={{0,2},{1,3},{2,0},{3,1},{4,6},{5,7},{6,4},{7,5},{8,10},{9,11},{10,... | collective-permute-start | bytes 442376 | tf_op jit(solution)/shard_map/ppermute | solution.py:157
  36.2 4.6 %collective-permute-start.19 = (f32[48,768]{1,0:T(8,128)S(1)}, f32[48,768]{1,0:T(8,128)S(1)}, u32[]{:S(2)}, u32[]{:S(2)}) collective-permute-start(f32[48,768]{1,0:T(8,128)S(1)} %get-tuple-element.111), channel_id=1, source_target_pairs={{0,1},{1,0},{2,3},{3,2},{4,5},{5,4},{6,7},{7,6},{8,9},{9,8},{10,11... | collective-permute-start | bytes 442376 | tf_op jit(solution)/shard_map/ppermute | solution.py:157
  36.2 9.2 %collective-permute-start.23 = (f32[48,768]{1,0:T(8,128)S(1)}, f32[48,768]{1,0:T(8,128)S(1)}, u32[]{:S(2)}, u32[]{:S(2)}) collective-permute-start(f32[48,768]{1,0:T(8,128)S(1)} %get-tuple-element.115), channel_id=1, source_target_pairs={{0,1},{1,0},{2,3},{3,2},{4,5},{5,4},{6,7},{7,6},{8,9},{9,8},{10,11... | collective-permute-start | bytes 442376 | tf_op jit(solution)/shard_map/ppermute | solution.py:157
  36.8 17.9 %collective-permute-start.27 = (f32[48,768]{1,0:T(8,128)S(1)}, f32[48,768]{1,0:T(8,128)S(1)}, u32[]{:S(2)}, u32[]{:S(2)}) collective-permute-start(f32[48,768]{1,0:T(8,128)S(1)} %get-tuple-element.119), channel_id=1, source_target_pairs={{0,1},{1,0},{2,3},{3,2},{4,5},{5,4},{6,7},{7,6},{8,9},{9,8},{10,11... | collective-permute-start | bytes 442376 | tf_op jit(solution)/shard_map/ppermute | solution.py:157
  38.1 6.3 %collective-permute-start.21 = (f32[48,768]{1,0:T(8,128)S(1)}, f32[48,768]{1,0:T(8,128)S(1)}, u32[]{:S(2)}, u32[]{:S(2)}) collective-permute-start(f32[48,768]{1,0:T(8,128)S(1)} %add.76), channel_id=1, source_target_pairs={{0,2},{1,3},{2,0},{3,1},{4,6},{5,7},{6,4},{7,5},{8,10},{9,11},{10,... | collective-permute-start | bytes 442376 | tf_op jit(solution)/shard_map/ppermute | solution.py:157
  40.7 59.1 %collective-permute-start.45 = (f32[520,768]{1,0:T(8,128)S(1)}, f32[520,768]{1,0:T(8,128)S(1)}, u32[]{:S(2)}, u32[]{:S(2)}) collective-permute-start(f32[520,768]{1,0:T(8,128)S(1)} %shard_map.131), channel_id=1, source_target_pairs={{0,1},{1,2},{2,3},{3,4},{4,5},{5,6},{6,7},{7,8},{8,9},{9,10},{10,1... | collective-permute-start | bytes 4792328 | tf_op jit(solution)/shard_map/ppermute | solution.py:248
  40.8 6.2 %collective-permute-start.25 = (f32[48,768]{1,0:T(8,128)S(1)}, f32[48,768]{1,0:T(8,128)S(1)}, u32[]{:S(2)}, u32[]{:S(2)}) collective-permute-start(f32[48,768]{1,0:T(8,128)S(1)} %add.79), channel_id=1, source_target_pairs={{0,2},{1,3},{2,0},{3,1},{4,6},{5,7},{6,4},{7,5},{8,10},{9,11},{10,... | collective-permute-start | bytes 442376 | tf_op jit(solution)/shard_map/ppermute | solution.py:157
  44.4 22.5 %collective-permute-start.29 = (f32[48,768]{1,0:T(8,128)S(1)}, f32[48,768]{1,0:T(8,128)S(1)}, u32[]{:S(2)}, u32[]{:S(2)}) collective-permute-start(f32[48,768]{1,0:T(8,128)S(1)} %add.82), channel_id=1, source_target_pairs={{0,2},{1,3},{2,0},{3,1},{4,6},{5,7},{6,4},{7,5},{8,10},{9,11},{10,... | collective-permute-start | bytes 442376 | tf_op jit(solution)/shard_map/ppermute | solution.py:157
  45.4 21.4 %collective-permute-start.18 = (f32[48,768]{1,0:T(8,128)S(1)}, f32[48,768]{1,0:T(8,128)S(1)}, u32[]{:S(2)}, u32[]{:S(2)}) collective-permute-start(f32[48,768]{1,0:T(8,128)S(1)} %add_add_fusion.7), channel_id=1, source_target_pairs={{0,12},{1,13},{2,14},{3,15},{4,8},{5,9},{6,10},{7,11},{8,4},{9,5},... | collective-permute-start | bytes 442376 | tf_op jit(solution)/shard_map/ppermute | solution.py:157
  47.0 19.9 %collective-permute-start.22 = (f32[48,768]{1,0:T(8,128)S(1)}, f32[48,768]{1,0:T(8,128)S(1)}, u32[]{:S(2)}, u32[]{:S(2)}) collective-permute-start(f32[48,768]{1,0:T(8,128)S(1)} %add_add_fusion.6), channel_id=1, source_target_pairs={{0,8},{1,9},{2,10},{3,11},{4,12},{5,13},{6,14},{7,15},{8,0},{9,1},... | collective-permute-start | bytes 442376 | tf_op jit(solution)/shard_map/ppermute | solution.py:157
  54.8 15.1 %collective-permute-start.26 = (f32[48,768]{1,0:T(8,128)S(1)}, f32[48,768]{1,0:T(8,128)S(1)}, u32[]{:S(2)}, u32[]{:S(2)}) collective-permute-start(f32[48,768]{1,0:T(8,128)S(1)} %add_add_fusion.5), channel_id=1, source_target_pairs={{0,4},{1,5},{2,6},{3,7},{4,0},{5,1},{6,2},{7,3},{8,12},{9,13},{10,... | collective-permute-start | bytes 442376 | tf_op jit(solution)/shard_map/ppermute | solution.py:157
  70.0 7.2 %collective-permute-start.33 = (f32[48,768]{1,0:T(8,128)S(1)}, f32[48,768]{1,0:T(8,128)S(1)}, u32[]{:S(2)}, u32[]{:S(2)}) collective-permute-start(f32[48,768]{1,0:T(8,128)S(1)} %get-tuple-element.122.refs_0_.relation), channel_id=1, source_target_pairs={{0,4},{1,5},{2,6},{3,7},{4,0},{5,1},{6,2},{7,3},{8,12},{9,13},{10,... | collective-permute-start | bytes 442376 | tf_op jit(solution)/shard_map/ppermute | solution.py:157
  72.6 11.3 %collective-permute-start.31 = (f32[48,768]{1,0:T(8,128)S(1)}, f32[48,768]{1,0:T(8,128)S(1)}, u32[]{:S(2)}, u32[]{:S(2)}) collective-permute-start(f32[48,768]{1,0:T(8,128)S(1)} %get-tuple-element.122.refs_0_.relation), channel_id=1, source_target_pairs={{0,2},{1,3},{2,0},{3,1},{4,6},{5,7},{6,4},{7,5},{8,10},{9,11},{10,... | collective-permute-start | bytes 442376 | tf_op jit(solution)/shard_map/ppermute | solution.py:157
  77.0 9.9 %collective-permute-start.37 = (f32[48,768]{1,0:T(8,128)S(1)}, f32[48,768]{1,0:T(8,128)S(1)}, u32[]{:S(2)}, u32[]{:S(2)}) collective-permute-start(f32[48,768]{1,0:T(8,128)S(1)} %get-tuple-element.122.refs_0_.relation), channel_id=1, source_target_pairs={{0,8},{1,9},{2,10},{3,11},{4,12},{5,13},{6,14},{7,15},{8,0},{9,1},... | collective-permute-start | bytes 442376 | tf_op jit(solution)/shard_map/ppermute | solution.py:157
  77.0 6.8 %collective-permute-start.30 = (f32[48,768]{1,0:T(8,128)S(1)}, f32[48,768]{1,0:T(8,128)S(1)}, u32[]{:S(2)}, u32[]{:S(2)}) collective-permute-start(f32[48,768]{1,0:T(8,128)S(1)} %get-tuple-element.122.refs_0_.relation), channel_id=1, source_target_pairs={{0,1},{1,0},{2,3},{3,2},{4,5},{5,4},{6,7},{7,6},{8,9},{9,8},{10,11... | collective-permute-start | bytes 442376 | tf_op jit(solution)/shard_map/ppermute | solution.py:157
  77.2 9.8 %collective-permute-start.35 = (f32[48,768]{1,0:T(8,128)S(1)}, f32[48,768]{1,0:T(8,128)S(1)}, u32[]{:S(2)}, u32[]{:S(2)}) collective-permute-start(f32[48,768]{1,0:T(8,128)S(1)} %collective-permute-done.33.refs_4_), channel_id=1, source_target_pairs={{0,2},{1,3},{2,0},{3,1},{4,6},{5,7},{6,4},{7,5},{8,10},{9,11},{10,... | collective-permute-start | bytes 442376 | tf_op jit(solution)/shard_map/ppermute | solution.py:157
  83.8 3.2 %collective-permute-start.32 = (f32[48,768]{1,0:T(8,128)S(1)}, f32[48,768]{1,0:T(8,128)S(1)}, u32[]{:S(2)}, u32[]{:S(2)}) collective-permute-start(f32[48,768]{1,0:T(8,128)S(1)} %collective-permute-done.31.refs_2_), channel_id=1, source_target_pairs={{0,1},{1,0},{2,3},{3,2},{4,5},{5,4},{6,7},{7,6},{8,9},{9,8},{10,11... | collective-permute-start | bytes 442376 | tf_op jit(solution)/shard_map/ppermute | solution.py:157
  83.9 8.2 %collective-permute-start.41 = (f32[48,768]{1,0:T(8,128)S(1)}, f32[48,768]{1,0:T(8,128)S(1)}, u32[]{:S(2)}, u32[]{:S(2)}) collective-permute-start(f32[48,768]{1,0:T(8,128)S(1)} %get-tuple-element.122.refs_0_.relation), channel_id=1, source_target_pairs={{0,12},{1,13},{2,14},{3,15},{4,8},{5,9},{6,10},{7,11},{8,4},{9,5},... | collective-permute-start | bytes 442376 | tf_op jit(solution)/shard_map/ppermute | solution.py:157
  86.9 5.1 %collective-permute-start.39 = (f32[48,768]{1,0:T(8,128)S(1)}, f32[48,768]{1,0:T(8,128)S(1)}, u32[]{:S(2)}, u32[]{:S(2)}) collective-permute-start(f32[48,768]{1,0:T(8,128)S(1)} %collective-permute-done.37.refs_8_), channel_id=1, source_target_pairs={{0,2},{1,3},{2,0},{3,1},{4,6},{5,7},{6,4},{7,5},{8,10},{9,11},{10,... | collective-permute-start | bytes 442376 | tf_op jit(solution)/shard_map/ppermute | solution.py:157
  87.0 5.0 %collective-permute-start.34 = (f32[48,768]{1,0:T(8,128)S(1)}, f32[48,768]{1,0:T(8,128)S(1)}, u32[]{:S(2)}, u32[]{:S(2)}) collective-permute-start(f32[48,768]{1,0:T(8,128)S(1)} %collective-permute-done.33.refs_4_), channel_id=1, source_target_pairs={{0,1},{1,0},{2,3},{3,2},{4,5},{5,4},{6,7},{7,6},{8,9},{9,8},{10,11... | collective-permute-start | bytes 442376 | tf_op jit(solution)/shard_map/ppermute | solution.py:157
  87.0 5.0 %collective-permute-start.36 = (f32[48,768]{1,0:T(8,128)S(1)}, f32[48,768]{1,0:T(8,128)S(1)}, u32[]{:S(2)}, u32[]{:S(2)}) collective-permute-start(f32[48,768]{1,0:T(8,128)S(1)} %collective-permute-done.35.refs_6_), channel_id=1, source_target_pairs={{0,1},{1,0},{2,3},{3,2},{4,5},{5,4},{6,7},{7,6},{8,9},{9,8},{10,11... | collective-permute-start | bytes 442376 | tf_op jit(solution)/shard_map/ppermute | solution.py:157
  92.0 5.3 %collective-permute-start.43 = (f32[48,768]{1,0:T(8,128)S(1)}, f32[48,768]{1,0:T(8,128)S(1)}, u32[]{:S(2)}, u32[]{:S(2)}) collective-permute-start(f32[48,768]{1,0:T(8,128)S(1)} %collective-permute-done.41.refs_12_), channel_id=1, source_target_pairs={{0,2},{1,3},{2,0},{3,1},{4,6},{5,7},{6,4},{7,5},{8,10},{9,11},{10,... | collective-permute-start | bytes 442376 | tf_op jit(solution)/shard_map/ppermute | solution.py:157
  92.1 5.3 %collective-permute-start.38 = (f32[48,768]{1,0:T(8,128)S(1)}, f32[48,768]{1,0:T(8,128)S(1)}, u32[]{:S(2)}, u32[]{:S(2)}) collective-permute-start(f32[48,768]{1,0:T(8,128)S(1)} %collective-permute-done.37.refs_8_), channel_id=1, source_target_pairs={{0,1},{1,0},{2,3},{3,2},{4,5},{5,4},{6,7},{7,6},{8,9},{9,8},{10,11... | collective-permute-start | bytes 442376 | tf_op jit(solution)/shard_map/ppermute | solution.py:157
  92.1 5.2 %collective-permute-start.40 = (f32[48,768]{1,0:T(8,128)S(1)}, f32[48,768]{1,0:T(8,128)S(1)}, u32[]{:S(2)}, u32[]{:S(2)}) collective-permute-start(f32[48,768]{1,0:T(8,128)S(1)} %collective-permute-done.39.refs_10_), channel_id=1, source_target_pairs={{0,1},{1,0},{2,3},{3,2},{4,5},{5,4},{6,7},{7,6},{8,9},{9,8},{10,11... | collective-permute-start | bytes 442376 | tf_op jit(solution)/shard_map/ppermute | solution.py:157
  106.1 6.1 %collective-permute-start.50 = (f32[48,768]{1,0:T(8,128)S(1)}, f32[48,768]{1,0:T(8,128)S(1)}, u32[]{:S(2)}, u32[]{:S(2)}) collective-permute-start(f32[48,768]{1,0:T(8,128)S(1)} %get-tuple-element.169), channel_id=1, source_target_pairs={{0,1},{1,0},{2,3},{3,2},{4,5},{5,4},{6,7},{7,6},{8,9},{9,8},{10,11... | collective-permute-start | bytes 442376 | tf_op jit(solution)/shard_map/ppermute | solution.py:157
  106.5 7.4 %collective-permute-start.51 = (f32[48,768]{1,0:T(8,128)S(1)}, f32[48,768]{1,0:T(8,128)S(1)}, u32[]{:S(2)}, u32[]{:S(2)}) collective-permute-start(f32[48,768]{1,0:T(8,128)S(1)} %add.84), channel_id=1, source_target_pairs={{0,2},{1,3},{2,0},{3,1},{4,6},{5,7},{6,4},{7,5},{8,10},{9,11},{10,... | collective-permute-start | bytes 442376 | tf_op jit(solution)/shard_map/ppermute | solution.py:157
  106.8 7.5 %collective-permute-start.53 = (f32[48,768]{1,0:T(8,128)S(1)}, f32[48,768]{1,0:T(8,128)S(1)}, u32[]{:S(2)}, u32[]{:S(2)}) collective-permute-start(f32[48,768]{1,0:T(8,128)S(1)} %get-tuple-element.171), channel_id=1, source_target_pairs={{0,1},{1,0},{2,3},{3,2},{4,5},{5,4},{6,7},{7,6},{8,9},{9,8},{10,11... | collective-permute-start | bytes 442376 | tf_op jit(solution)/shard_map/ppermute | solution.py:157
  107.0 12.8 %collective-permute-start.56 = (f32[48,768]{1,0:T(8,128)S(1)}, f32[48,768]{1,0:T(8,128)S(1)}, u32[]{:S(2)}, u32[]{:S(2)}) collective-permute-start(f32[48,768]{1,0:T(8,128)S(1)} %get-tuple-element.173), channel_id=1, source_target_pairs={{0,1},{1,0},{2,3},{3,2},{4,5},{5,4},{6,7},{7,6},{8,9},{9,8},{10,11... | collective-permute-start | bytes 442376 | tf_op jit(solution)/shard_map/ppermute | solution.py:157
  107.4 16.3 %collective-permute-start.59 = (f32[48,768]{1,0:T(8,128)S(1)}, f32[48,768]{1,0:T(8,128)S(1)}, u32[]{:S(2)}, u32[]{:S(2)}) collective-permute-start(f32[48,768]{1,0:T(8,128)S(1)} %get-tuple-element.175), channel_id=1, source_target_pairs={{0,1},{1,0},{2,3},{3,2},{4,5},{5,4},{6,7},{7,6},{8,9},{9,8},{10,11... | collective-permute-start | bytes 442376 | tf_op jit(solution)/shard_map/ppermute | solution.py:157
  112.2 6.7 %collective-permute-start.54 = (f32[48,768]{1,0:T(8,128)S(1)}, f32[48,768]{1,0:T(8,128)S(1)}, u32[]{:S(2)}, u32[]{:S(2)}) collective-permute-start(f32[48,768]{1,0:T(8,128)S(1)} %add.85), channel_id=1, source_target_pairs={{0,2},{1,3},{2,0},{3,1},{4,6},{5,7},{6,4},{7,5},{8,10},{9,11},{10,... | collective-permute-start | bytes 442376 | tf_op jit(solution)/shard_map/ppermute | solution.py:157
  113.8 8.2 %collective-permute-start.57 = (f32[48,768]{1,0:T(8,128)S(1)}, f32[48,768]{1,0:T(8,128)S(1)}, u32[]{:S(2)}, u32[]{:S(2)}) collective-permute-start(f32[48,768]{1,0:T(8,128)S(1)} %add.86), channel_id=1, source_target_pairs={{0,2},{1,3},{2,0},{3,1},{4,6},{5,7},{6,4},{7,5},{8,10},{9,11},{10,... | collective-permute-start | bytes 442376 | tf_op jit(solution)/shard_map/ppermute | solution.py:157
  114.3 10.4 %collective-permute-start.60 = (f32[48,768]{1,0:T(8,128)S(1)}, f32[48,768]{1,0:T(8,128)S(1)}, u32[]{:S(2)}, u32[]{:S(2)}) collective-permute-start(f32[48,768]{1,0:T(8,128)S(1)} %add.87), channel_id=1, source_target_pairs={{0,2},{1,3},{2,0},{3,1},{4,6},{5,7},{6,4},{7,5},{8,10},{9,11},{10,... | collective-permute-start | bytes 442376 | tf_op jit(solution)/shard_map/ppermute | solution.py:157
  118.9 8.6 %collective-permute-start.52 = (f32[48,768]{1,0:T(8,128)S(1)}, f32[48,768]{1,0:T(8,128)S(1)}, u32[]{:S(2)}, u32[]{:S(2)}) collective-permute-start(f32[48,768]{1,0:T(8,128)S(1)} %add_add_fusion.3), channel_id=1, source_target_pairs={{0,12},{1,13},{2,14},{3,15},{4,8},{5,9},{6,10},{7,11},{8,4},{9,5},... | collective-permute-start | bytes 442376 | tf_op jit(solution)/shard_map/ppermute | solution.py:157
  119.8 14.6 %collective-permute-start.55 = (f32[48,768]{1,0:T(8,128)S(1)}, f32[48,768]{1,0:T(8,128)S(1)}, u32[]{:S(2)}, u32[]{:S(2)}) collective-permute-start(f32[48,768]{1,0:T(8,128)S(1)} %add_add_fusion.2), channel_id=1, source_target_pairs={{0,8},{1,9},{2,10},{3,11},{4,12},{5,13},{6,14},{7,15},{8,0},{9,1},... | collective-permute-start | bytes 442376 | tf_op jit(solution)/shard_map/ppermute | solution.py:157
  122.0 12.3 %collective-permute-start.58 = (f32[48,768]{1,0:T(8,128)S(1)}, f32[48,768]{1,0:T(8,128)S(1)}, u32[]{:S(2)}, u32[]{:S(2)}) collective-permute-start(f32[48,768]{1,0:T(8,128)S(1)} %add_add_fusion.1), channel_id=1, source_target_pairs={{0,4},{1,5},{2,6},{3,7},{4,0},{5,1},{6,2},{7,3},{8,12},{9,13},{10,... | collective-permute-start | bytes 442376 | tf_op jit(solution)/shard_map/ppermute | solution.py:157
  (23 other events, 192.2 us)

commit v3 on v1

v3 whole, which is shorter than its diff:
```python
import functools

import jax
import jax.numpy as jnp
from jax import lax
from jax.experimental import pallas as pl
from jax.experimental.pallas import tpu as pltpu
from jax.sharding import PartitionSpec as P

F32 = jnp.float32
BF16 = jnp.bfloat16
NN = (((1,), (0,)), ((), ()))
NT = (((1,), (1,)), ((), ()))
VMEM = pl.BlockSpec(memory_space=pltpu.VMEM)
SMEM = pl.BlockSpec(memory_space=pltpu.SMEM)
CHUNKS = 2


def split(x):
    high = x.astype(BF16)
    return high, (x - high.astype(F32)).astype(BF16)


def dot3(a, b, dims):
    def one(p, q):
        return lax.dot_general(p, q, dims, preferred_element_type=F32)

    return one(a[0], b[0]) + (one(a[0], b[1]) + one(a[1], b[0]))


def diagonal(n):
    return lax.broadcasted_iota(jnp.int32, (n, n), 0) == lax.broadcasted_iota(jnp.int32, (n, n), 1)


def adagrad(param, state_row, grad):
    n = param.shape[0]
    eye = diagonal(n)
    state = jnp.sum(jnp.where(eye, state_row, 0.0), axis=1, keepdims=True)
    state = state + jnp.sum(grad * grad, axis=1, keepdims=True) * (1.0 / grad.shape[1])
    back = jnp.sum(jnp.where(eye, state, 0.0), axis=0, keepdims=True)
    return param - grad * (0.1 / jnp.sqrt(state)), back


def to_slots(me, source, target, slots):
    rows = source.shape[0] // slots
    for r in range(slots):
        start = pl.multiple_of((me ^ r) * rows, rows)
        target[r * rows : (r + 1) * rows, :] = source[pl.ds(start, rows), :]


def from_slots(me, source, target, slots, first):
    rows = target.shape[0] // slots
    count = source.shape[0] // rows
    for r in range(count):
        start = pl.multiple_of((me ^ (first + r)) * rows, rows)
        target[pl.ds(start, rows), :] = source[r * rows : (r + 1) * rows, :]
    return first + count


def write_head_parts(me, heads, outs, normal, slotted, slots):
    normal[...] = heads.T
    to_slots(me, normal, slotted, slots)
    outs[0][...], outs[1][...] = split(slotted[...])
    at = 0
    for high, low in zip(outs[2::2], outs[3::2]):
        columns = high.shape[1]
        high[...], low[...] = split(slotted[at : at + columns, :].T)
        at += columns


def prepare_heads_kernel(slots, me_ref, heads, *rest):
    write_head_parts(me_ref[0], heads[...], rest[:-2], *rest[-2:], slots)


def prepare_tails_kernel(head_rows, tails, pos_head, pos_tail, high, low, marks):
    high[...], low[...] = split(tails[...])
    tail_rows, pairs = tails.shape[0], pos_head.shape[1]
    for bucket in range(2):
        in_head = lax.broadcasted_iota(jnp.int32, (head_rows, pairs), 0) == pos_head[bucket : bucket + 1, :]
        in_tail = lax.broadcasted_iota(jnp.int32, (tail_rows, pairs), 0) == pos_tail[bucket : bucket + 1, :]
        marks[bucket] = lax.dot_general(
            jnp.where(in_head, 1.0, 0.0).astype(BF16),
            jnp.where(in_tail, 1.0, 0.0).astype(BF16),
            NT,
            preferred_element_type=F32,
        )


def add_product(blocks, heads, parts):
    rows = blocks[0].shape[0]
    for r, block in enumerate(blocks):
        at = slice(r * rows, (r + 1) * rows)
        parts[0][at, :], parts[1][at, :] = split(block[...])
    return dot3((heads[0][...], heads[1][...]), (parts[0][...], parts[1][...]), NN)


def product_kernel(first, count, *refs):
    before, refs = (None, refs) if first else (refs[0], refs[1:])
    blocks, heads, product, parts = refs[:count], refs[count : count + 2], refs[count + 2], refs[count + 3 :]
    term = add_product(blocks, heads, parts)
    product[...] = term if first else before[...] + term


def bucket_kernel(bucket, first, count, picks, *refs):
    before, refs = (None, refs) if first else (refs[0], refs[1:])
    blocks, refs = refs[:count], refs[count:]
    heads, turned, tails, marks = refs[0:2], refs[2:4], refs[4:6], refs[6]
    relation, product, scores, grad, pieces = refs[7:9], refs[9:11], refs[11], refs[12:14], refs[14:]
    whole = add_product(blocks, heads, relation)
    prod = split(whole if first else before[...] + whole)
    product[0][...], product[1][...] = prod
    tail = (tails[0][...], tails[1][...])
    grad_scores = (jax.nn.sigmoid(dot3(prod, tail, NT)) - marks[bucket]) * 0.0625
    scores[...] = grad_scores
    grad_product = split(dot3(split(grad_scores), tail, NN))
    grad[0][...], grad[1][...] = grad_product
    whole = dot3((turned[0][...], turned[1][...]), grad_product, NN)
    rows = whole.shape[0] // sum(len(slots) for slots in picks)
    for piece, slots in zip(pieces, picks):
        for i, r in enumerate(slots):
            piece[i * rows : (i + 1) * rows, :] = whole[r * rows : (r + 1) * rows, :]


def tails_kernel(chunks, last, grad_scores, product_high, product_low, *refs):
    grad = dot3(split(grad_scores[...].T), (product_high[...], product_low[...]), NN)
    if last:
        tails, outs = refs[:chunks], refs[chunks:]
        rows = [outs[0].shape[0] // chunks] * chunks
        state = tails[-1][rows[-1] : rows[-1] + 1, : outs[0].shape[0]]
        held = [t[:n, :] for t, n in zip(tails, rows)]
        outs[0][...], outs[1][...] = adagrad(jnp.concatenate(held, axis=0), state, grad)
        return
    tails, state, outs = refs[0], refs[1], refs[2:]
    new, new_state = adagrad(tails[...], state[...], grad)
    rows = tails.shape[0] // chunks
    for c in range(chunks):
        outs[c][:rows, :] = new[c * rows : (c + 1) * rows, :]
    outs[-1][rows:, :] = jnp.zeros((outs[-1].shape[0] - rows, new.shape[1]), F32)
    outs[-1][rows : rows + 1, : tails.shape[0]] = new_state


def heads_kernel(slots, groups, last, me_ref, grad_high, grad_low, *rest):
    relation, (heads, state, heads_out, state_out), rest = rest[: 2 * groups], rest[2 * groups : 2 * groups + 4], rest[2 * groups + 4 :]
    outs, (high, low) = rest[: 2 + 2 * groups], (rest[:2] if last else rest[2 + 2 * groups : 4 + 2 * groups])
    at = 0
    for g in range(groups):
        from_slots(me_ref[0], relation[2 * g], high, slots, at)
        at = from_slots(me_ref[0], relation[2 * g + 1], low, slots, at)
    grad = dot3((grad_high[...], grad_low[...]), (high[...], low[...]), NT)
    new_heads, state_out[...] = adagrad(heads[...], state[...], grad)
    heads_out[...] = new_heads
    if not last:
        write_head_parts(me_ref[0], new_heads, outs, *rest[-2:], slots)


def split_kernel(*refs):
    chunks, (high, low) = refs[:-2], refs[-2:]
    rows = high.shape[0] // len(chunks)
    for c, chunk in enumerate(chunks):
        at = slice(c * rows, (c + 1) * rows)
        high[at, :], low[at, :] = split(chunk[:rows, :])


def sum_kernel(a, b, *totals):
    at = 0
    for total in totals:
        rows = slice(at, at + total.shape[0])
        total[...] = a[rows, :] + b[rows, :]
        at += total.shape[0]


def total_kernel(place, a, b, c, total):
    rows = slice(place * total.shape[0], (place + 1) * total.shape[0])
    total[...] = a[rows, :] + b[rows, :] + c[...]


def relation_kernel(relation, state, *rest):
    pieces, (relation_out, state_out) = rest[:-2], rest[-2:]
    grad = pieces[0][...]
    for piece in pieces[1:]:
        grad = grad + piece[...]
    relation_out[...], state_out[...] = adagrad(relation[...], state[...], grad)


def call(kernel, outs, args, scratch=(), smem_first=False, flops=0):
    specs = [VMEM] * len(args)
    if smem_first:
        specs[0] = SMEM
    moved = sum(a.size * a.dtype.itemsize for a in args)
    return pl.pallas_call(
        kernel,
        out_shape=[jax.ShapeDtypeStruct(s, t) for s, t in outs],
        in_specs=specs,
        out_specs=[VMEM] * len(outs),
        scratch_shapes=[pltpu.VMEM(s, t) for s, t in scratch],
        compiler_params=pltpu.CompilerParams(vmem_limit_bytes=20 * 1024 * 1024),
        cost_estimate=pl.CostEstimate(flops=flops, bytes_accessed=moved, transcendentals=0),
    )(*args)


def partner(value, mask):
    n = lax.axis_size("blk")
    return lax.ppermute(value, "blk", [(i, i ^ mask) for i in range(n)])


def after(value, *others):
    return lax.optimization_barrier((value, *others))[0]


def gather_groups(own, early, late, crowded, use):
    n = lax.axis_size("blk")
    far = list(range(4, n, 4))
    got = {0: own}
    step = n // 2
    while step >= 4:
        for k in [k for k in (0, *far) if k in got]:
            got[k ^ step] = partner(got[k], step)
        if step == n // 2:
            got[step] = after(got[step], *early)
        step //= 2
    for k in (0, *far):
        ready = after(got[k], got[k]) if crowded and k != far[-1] else got[k]
        got[k ^ 2] = partner(ready, 2)
    waited = late
    for k in (0, *far):
        first = after(got[k], *waited) if k == far[-1] else got[k]
        got[k ^ 1], got[k ^ 3] = partner(first, 1), partner(got[k ^ 2], 1)
        out = use([got[k ^ r] for r in range(4)], k == far[-1])
        if k == 0:
            waited = [*waited, out]
    return out


def pick_slots(n):
    order = (*range(n - 4, 0, -4), 0)
    return [[k ^ r for k in order] for r in (2, 3, 0, 1)]


def scatter_blocks(n, across, across_far, here, here_far):
    order = (*range(n - 4, 0, -4), 0)
    share = across.shape[0] // len(order)
    shape = ((share, across.shape[1]), F32)
    turned = partner(across_far, 1), partner(here_far, 1)
    sent = call(sum_kernel, [shape] * len(order), [across, turned[0]])
    crossed = [partner(value, 2) for value in sent]
    totals = {
        k: call(functools.partial(total_kernel, i), [shape], [here, turned[1], crossed[i]])[0]
        for i, k in enumerate(order)
    }
    step = 4
    while step < n // 2:
        for k in [k for k in totals if k & step]:
            (totals[k ^ step],) = call(sum_kernel, [shape], [totals[k ^ step], partner(totals.pop(k), step)])
        step *= 2
    return [totals[0], partner(totals[step], step)], crossed


def body(heads, head_state, tails, tail_state, relation, relation_state, pos_head, pos_tail):
    share, width = relation.shape
    n = lax.axis_size("blk")
    by_blocks = share % 16 == 0 and n & (n - 1) == 0 and n >= 16
    slots = n if by_blocks else 1
    me = (lax.axis_index("blk").astype(jnp.int32) if by_blocks else jnp.int32(0)).reshape(1)
    head_rows, tail_rows = heads.shape[0], tails.shape[0]
    head_state, tail_state, relation_state = (s.reshape(1, -1) for s in (head_state, tail_state, relation_state))

    def gathered(rows, early, late, crowded, use):
        if by_blocks:
            return gather_groups(rows, early, late, crowded, use)
        return use([lax.all_gather(rows, "blk", axis=0, tiled=True)], True)

    def scattered(pieces):
        if by_blocks:
            return scatter_blocks(n, *pieces)
        return [lax.psum_scatter(pieces[0], "blk", scatter_dimension=0, tiled=True)], []

    picks = pick_slots(n) if by_blocks else [[0]]
    sizes = [4 * share] * (n // 4) if by_blocks else [width]
    head_parts = [((width, head_rows), BF16)] * 2
    for size in sizes:
        head_parts += [((head_rows, size), BF16)] * 2
    turned = [((width, head_rows), F32)] * 2
    tail_parts = [((tail_rows, width), BF16)] * 2
    relation_parts = [[((size, width), BF16)] * 2 for size in sizes]
    row_parts = [((head_rows, width), BF16)] * 2
    held = [((len(pick) * (width // slots), width), F32) for pick in picks]
    table = ((head_rows, tail_rows), F32)

    head_half = call(
        functools.partial(prepare_heads_kernel, slots), head_parts, [me, heads], scratch=turned, smem_first=True
    )
    *tail_half, marks = call(
        functools.partial(prepare_tails_kernel, head_rows),
        [*tail_parts, ((2, *table[0]), F32)],
        [tails, pos_head, pos_tail],
    )
    for bucket in range(2):
        last = bucket == 1
        before, relation_half = [], []

        def use(blocks, closing):
            first, g = not before, len(relation_half) // 2
            halves, count = head_half[2 + 2 * g : 4 + 2 * g], len(blocks)
            if closing:
                out = call(
                    functools.partial(bucket_kernel, bucket, first, count, picks),
                    [*relation_parts[g], *row_parts, table, *row_parts, *held],
                    [*before[-1:], *blocks, *halves, *head_half[:2], *tail_half, marks],
                    flops=6 * head_rows * width * (2 * width + 2 * tail_rows),
                )
                relation_half.extend(out[:2])
                return out
            out = call(
                functools.partial(product_kernel, first, count),
                [((head_rows, width), F32), *relation_parts[g]],
                [*before[-1:], *blocks, *halves],
                flops=100000000,
            )
            relation_half.extend(out[1:])
            before.append(out[0])
            return out[0]

        out = gathered(relation, head_half, [] if bucket else [*tail_half, marks], bucket == 1, use)
        product, grad_scores, grad_product, pieces = out[2:4], out[4], out[5:7], out[7:]
        terms, crossed = scattered(pieces)
        tail_rest = {"flops": 6 * head_rows * width * tail_rows}
        if not last:
            rows = tail_rows // CHUNKS
            sent = call(
                functools.partial(tails_kernel, CHUNKS, last),
                [((rows, width), F32)] * (CHUNKS - 1) + [((rows + 8, width), F32)],
                [grad_scores, *product, tails, tail_state],
                **tail_rest,
            )
            sent = [after(v, *()) for v in sent]
            tails = [lax.ppermute(v, "blk", [(i, (i + 1) % n) for i in range(n)]) for v in sent]
            tail_half = call(split_kernel, tail_parts, tails)
        else:
            tails, tail_state = call(
                functools.partial(tails_kernel, CHUNKS, last),
                [((tail_rows, width), F32), (tail_state.shape, F32)],
                [after(grad_scores, *crossed[-1:]), *product, *tails],
                **tail_rest,
            )
        out = call(
            functools.partial(heads_kernel, slots, len(sizes), last),
            [(heads.shape, F32), (head_state.shape, F32), *([] if last else head_parts)],
            [me, after(grad_product[0], *crossed[-1:]), grad_product[1], *relation_half, heads, head_state],
            scratch=[((width, width), BF16)] * 2 + ([] if last else turned),
            smem_first=True,
        )
        heads, head_state, head_half = out[0], out[1], out[2:]
        relation, relation_state = call(
            relation_kernel,
            [(relation.shape, F32), (relation_state.shape, F32)],
            [relation, relation_state, *terms],
        )
    return (
        heads,
        head_state.reshape(-1),
        tails,
        tail_state.reshape(-1),
        relation,
        relation_state.reshape(-1),
    )


def solution(mesh):
    rows, flat, pairs = P(("grp", "blk"), None), P(("grp", "blk")), P(None, ("grp", "blk"))
    return jax.shard_map(
        body,
        mesh=mesh,
        in_specs=(rows, flat, rows, flat, rows, flat, pairs, pairs),
        out_specs=(rows, flat, rows, flat, rows, flat),
        check_vma=False,
    )
```

time: 167 us -> 124 us (0.74)
  waiting for transfers between devices: 85 us -> 55.3 us
  local copies, waits for them, and re-layouts: 12.4 us -> 3.94 us
  Pallas kernels: 27.8 us -> 20.2 us
  starting transfers between devices: 40 us -> 43.2 us
    ppermute x60 -> x48, waiting for transfers between devices: 80.7 us -> 55.3 us  [partner(): return lax.ppermute(value, 'blk', [(i, i ^ mask) for i in range(n)])]
    unnamed x58 -> x20, local copies, waits for them, and re-layouts: 12.4 us -> 3.94 us
    pallas_call x10 -> x31, Pallas kernels: 27.8 us -> 20.2 us  [call(): pl.pallas_call(kernel, out_shape=[jax.ShapeDtypeStruct(s, t) for s, t in...]
    ppermute x2, waiting for transfers between devices: 4.27 us -> 0.01 us  [body(): lax.ppermute(v, 'blk', [(i, (i + 1) % n) for i in range(n)])]
    ppermute x60 -> x48, starting transfers between devices: 38.8 us -> 41.2 us  [partner(): return lax.ppermute(value, 'blk', [(i, i ^ mask) for i in range(n)])]
  transfers between devices with their start and end apart: 62 -> 50, of which waited for: 22 -> 21; matrix products, arithmetic and copies ran while one was open for 0% -> 0% of each run, Pallas kernels for 7% -> 10%
where the time goes in v3:
time: 124 us
  waiting for transfers between devices  55.3 us (45%)
  starting transfers between devices  43.2 us (35%)
  Pallas kernels  20.2 us (16%)
  local copies, waits for them, and re-layouts  3.94 us (3%)
    ppermute x48, waiting for transfers between devices, partner(): return lax.ppermute(value, 'blk', [(i, i ^ mask) for i in range(n)])  55.3 us
    ppermute x48, starting transfers between devices, partner(): return lax.ppermute(value, 'blk', [(i, i ^ mask) for i in range(n)])  41.2 us
    pallas_call x31, Pallas kernels, call(): pl.pallas_call(kernel, out_shape=[jax.ShapeDtypeStruct(s, t) for s, t in...  20.2 us
    unnamed x20, local copies, waits for them, and re-layouts  3.94 us
  transfers between devices with their start and end apart: 50, of which 21 were waited for; matrix products, arithmetic and copies ran while one was open for 0% of the time, Pallas kernels for 10%

profile of v3, /device:TPU:0, one launch (start us, length us, event | category | flops | bytes accessed | tf_op | source)
XLA Modules:
  0.0 123.6 jit_solution(7623686403204636942)
XLA Ops:
  0.6 4.1 %collective-permute-start.7 = (f32[48,768]{1,0:T(8,128)}, f32[48,768]{1,0:T(8,128)S(1)}, u32[]{:S(2)}, u32[]{:S(2)}) collective-permute-start(f32[48,768]{1,0:T(8,128)} %relation.1), channel_id=1, source_target_pairs={{0,8},{1,9},{2,10},{3,11},{4,12},{5,13},{6,14},{7,15},{8,0},{9,1},... | collective-permute-start | bytes 442376 | tf_op jit(solution)/shard_map/ppermute | solution.py:203
  4.7 1.6 %collective-permute-start.3 = (f32[48,768]{1,0:T(8,128)}, f32[48,768]{1,0:T(8,128)S(1)}, u32[]{:S(2)}, u32[]{:S(2)}) collective-permute-start(f32[48,768]{1,0:T(8,128)} %relation.1), channel_id=1, source_target_pairs={{0,4},{1,5},{2,6},{3,7},{4,0},{5,1},{6,2},{7,3},{8,12},{9,13},{10,... | collective-permute-start | bytes 442376 | tf_op jit(solution)/shard_map/ppermute | solution.py:203
  6.3 1.5 %collective-permute-start.1 = (f32[48,768]{1,0:T(8,128)}, f32[48,768]{1,0:T(8,128)S(1)}, u32[]{:S(2)}, u32[]{:S(2)}) collective-permute-start(f32[48,768]{1,0:T(8,128)} %relation.1), channel_id=1, source_target_pairs={{0,2},{1,3},{2,0},{3,1},{4,6},{5,7},{6,4},{7,5},{8,10},{9,11},{10,... | collective-permute-start | bytes 442376 | tf_op jit(solution)/shard_map/ppermute | solution.py:203
  7.8 1.1 copy-done.2
  9.6 2.5 %collective-permute-done.7.refs_1_ = f32[48,768]{1,0:T(8,128)S(1)} collective-permute-done((f32[48,768]{1,0:T(8,128)}, f32[48,768]{1,0:T(8,128)S(1)}, u32[]{:S(2)}, u32[]{:S(2)}) %collective-permute-start.7) | collective-permute-done | bytes 147488 | tf_op jit(solution)/shard_map/ppermute | solution.py:203
  12.1 0.7 collective-permute-start.11
  12.8 1.5 %collective-permute-start.5 = (f32[48,768]{1,0:T(8,128)S(1)}, f32[48,768]{1,0:T(8,128)S(1)}, u32[]{:S(2)}, u32[]{:S(2)}) collective-permute-start(f32[48,768]{1,0:T(8,128)S(1)} %collective-permute-done.3.refs_1_), channel_id=1, source_target_pairs={{0,2},{1,3},{2,0},{3,1},{4,6},{5,7},{6,4},{7,5},{8,10},{9,11},{10,... | collective-permute-start | bytes 442376 | tf_op jit(solution)/shard_map/ppermute | solution.py:203
  15.0 2.2 %collective-permute-done.11.refs_1_ = f32[48,768]{1,0:T(8,128)S(1)} collective-permute-done((f32[48,768]{1,0:T(8,128)S(1)}, f32[48,768]{1,0:T(8,128)S(1)}, u32[]{:S(2)}, u32[]{:S(2)}) %collective-permute-start.11) | collective-permute-done | bytes 147488 | tf_op jit(solution)/shard_map/ppermute | solution.py:203
  17.2 1.6 %collective-permute-start.13 = (f32[48,768]{1,0:T(8,128)S(1)}, f32[48,768]{1,0:T(8,128)S(1)}, u32[]{:S(2)}, u32[]{:S(2)}) collective-permute-start(f32[48,768]{1,0:T(8,128)S(1)} %collective-permute-done.11.refs_1_), channel_id=1, source_target_pairs={{0,2},{1,3},{2,0},{3,1},{4,6},{5,7},{6,4},{7,5},{8,10},{9,11},{10,... | collective-permute-start | bytes 442376 | tf_op jit(solution)/shard_map/ppermute | solution.py:203
  19.1 1.4 %copy-done = f32[512,768]{1,0:T(8,128)S(1)} copy-done((f32[512,768]{1,0:T(8,128)S(1)}, f32[512,768]{1,0:T(8,128)}, u32[]{:S(2)}) %copy-start) | copy-done | bytes 1572888
  20.5 0.7 copy-done.5
  21.9 0.9 shard_map.131
  26.0 3.2 %shard_map.132 = (bf16[192,768]{1,0:T(8,128)(2,1)S(1)}, bf16[192,768]{1,0:T(8,128)(2,1)S(1)}, bf16[256,768]{1,0:T(8,128)(2,1)S(1)}, bf16[256,768]{1,0:T(8,128)(2...) custom-call(f32[256,768]{1,0:T(8,128)S(1)} %get-tuple-element.114.re, ...), custom_call_target="tpu_custom_call" | custom-call | flops 3019898880 | bytes 4980736 | tf_op jit(solution)/shard_map/pallas_call | solution.py:190
  29.8 1.1 shard_map.145
  31.1 1.7 %collective-permute-start.39 = (f32[256,768]{1,0:T(8,128)S(1)}, f32[256,768]{1,0:T(8,128)S(1)}, u32[]{:S(2)}, u32[]{:S(2)}) collective-permute-start(f32[256,768]{1,0:T(8,128)S(1)} %get-tuple-element.160), channel_id=1, source_target_pairs={{0,1},{1,2},{2,3},{3,4},{4,5},{5,6},{6,7},{7,8},{8,9},{9,10},{10,1... | collective-permute-start | bytes 2359304 | tf_op jit(solution)/shard_map/ppermute | solution.py:336
  33.6 1.4 %collective-permute-start.18 = (f32[48,768]{1,0:T(8,128)S(1)}, f32[48,768]{1,0:T(8,128)S(1)}, u32[]{:S(2)}, u32[]{:S(2)}) collective-permute-start(f32[48,768]{1,0:T(8,128)S(1)} %get-tuple-element.124), channel_id=1, source_target_pairs={{0,2},{1,3},{2,0},{3,1},{4,6},{5,7},{6,4},{7,5},{8,10},{9,11},{10,... | collective-permute-start | bytes 442376 | tf_op jit(solution)/shard_map/ppermute | solution.py:203
  35.6 21.2 %collective-permute-done.21.c = f32[48,768]{1,0:T(8,128)S(1)} collective-permute-done((f32[48,768]{1,0:T(8,128)S(1)}, f32[48,768]{1,0:T(8,128)S(1)}, u32[]{:S(2)}, u32[]{:S(2)}) %collective-permute-start.21) | collective-permute-done | bytes 147488 | tf_op jit(solution)/shard_map/ppermute | solution.py:203
  56.9 3.1 %collective-permute-done.18.c = f32[48,768]{1,0:T(8,128)S(1)} collective-permute-done((f32[48,768]{1,0:T(8,128)S(1)}, f32[48,768]{1,0:T(8,128)S(1)}, u32[]{:S(2)}, u32[]{:S(2)}) %collective-permute-start.18) | collective-permute-done | bytes 147488 | tf_op jit(solution)/shard_map/ppermute | solution.py:203
  60.0 3.1 %collective-permute-done.20.c = f32[48,768]{1,0:T(8,128)S(1)} collective-permute-done((f32[48,768]{1,0:T(8,128)S(1)}, f32[48,768]{1,0:T(8,128)S(1)}, u32[]{:S(2)}, u32[]{:S(2)}) %collective-permute-start.20) | collective-permute-done | bytes 147488 | tf_op jit(solution)/shard_map/ppermute | solution.py:203
  63.2 2.5 %collective-permute-start.23 = (f32[48,768]{1,0:T(8,128)S(1)}, f32[48,768]{1,0:T(8,128)S(1)}, u32[]{:S(2)}, u32[]{:S(2)}) collective-permute-start(f32[48,768]{1,0:T(8,128)S(1)} %shard_map.139), channel_id=1, source_target_pairs={{0,8},{1,9},{2,10},{3,11},{4,12},{5,13},{6,14},{7,15},{8,0},{9,1},... | collective-permute-start | bytes 442376 | tf_op jit(solution)/shard_map/ppermute | solution.py:203
  65.8 5.3 %collective-permute-done.19.b = f32[48,768]{1,0:T(8,128)S(1)} collective-permute-done((f32[48,768]{1,0:T(8,128)S(1)}, f32[48,768]{1,0:T(8,128)S(1)}, u32[]{:S(2)}, u32[]{:S(2)}) %collective-permute-start.19) | collective-permute-done | bytes 147488 | tf_op jit(solution)/shard_map/ppermute | solution.py:203
  71.2 1.4 %collective-permute-start.31 = (f32[48,768]{1,0:T(8,128)S(1)}, f32[48,768]{1,0:T(8,128)S(1)}, u32[]{:S(2)}, u32[]{:S(2)}) collective-permute-start(f32[48,768]{1,0:T(8,128)S(1)} %get-tuple-element.128.refs_0_.relation), channel_id=1, source_target_pairs={{0,8},{1,9},{2,10},{3,11},{4,12},{5,13},{6,14},{7,15},{8,0},{9,1},... | collective-permute-start | bytes 442376 | tf_op jit(solution)/shard_map/ppermute | solution.py:203
  72.6 4.0 %collective-permute-start.27 = (f32[48,768]{1,0:T(8,128)S(1)}, f32[48,768]{1,0:T(8,128)S(1)}, u32[]{:S(2)}, u32[]{:S(2)}) collective-permute-start(f32[48,768]{1,0:T(8,128)S(1)} %get-tuple-element.128.refs_0_.relation), channel_id=1, source_target_pairs={{0,4},{1,5},{2,6},{3,7},{4,0},{5,1},{6,2},{7,3},{8,12},{9,13},{10,... | collective-permute-start | bytes 442376 | tf_op jit(solution)/shard_map/ppermute | solution.py:203
  76.9 2.0 %shard_map.141 = (f32[256,768]{1,0:T(8,128)S(1)}, f32[1,256]{1,0:T(1,128)S(1)}, bf16[768,256]{1,0:T(8,128)(2,1)S(1)}, bf16[768,256]{1,0:T(8,128)(2,1)S(1)}, bf16...) custom-call(s32[1]{0:T(128)} %bitcast.me_ref, ...), custom_call_target="tpu_custom_call" | custom-call | bytes 3933188 | tf_op jit(solution)/shard_map/pallas_call | solution.py:190
  78.9 1.0 collective-permute-done.31.refs_1_
  80.0 0.7 collective-permute-done.27.refs_1_
  80.7 1.1 collective-permute-start.35
  81.8 1.2 collective-permute-start.29
  83.0 0.9 collective-permute-start.33
  84.1 2.2 %collective-permute-done.35.refs_1_ = f32[48,768]{1,0:T(8,128)S(1)} collective-permute-done((f32[48,768]{1,0:T(8,128)S(1)}, f32[48,768]{1,0:T(8,128)S(1)}, u32[]{:S(2)}, u32[]{:S(2)}) %collective-permute-start.35) | collective-permute-done | bytes 147488 | tf_op jit(solution)/shard_map/ppermute | solution.py:203
  86.2 2.2 %collective-permute-start.37 = (f32[48,768]{1,0:T(8,128)S(1)}, f32[48,768]{1,0:T(8,128)S(1)}, u32[]{:S(2)}, u32[]{:S(2)}) collective-permute-start(f32[48,768]{1,0:T(8,128)S(1)} %collective-permute-done.35.refs_1_), channel_id=1, source_target_pairs={{0,2},{1,3},{2,0},{3,1},{4,6},{5,7},{6,4},{7,5},{8,10},{9,11},{10,... | collective-permute-start | bytes 442376 | tf_op jit(solution)/shard_map/ppermute | solution.py:203
  89.0 2.6 %collective-permute-done.33.refs_3_ = f32[48,768]{1,0:T(8,128)S(1)} collective-permute-done((f32[48,768]{1,0:T(8,128)S(1)}, f32[48,768]{1,0:T(8,128)S(1)}, u32[]{:S(2)}, u32[]{:S(2)}) %collective-permute-start.33) | collective-permute-done | bytes 147488 | tf_op jit(solution)/shard_map/ppermute | solution.py:203
  92.7 1.2 collective-permute-done.37.refs_3_
  95.3 3.3 %shard_map.147 = (bf16[192,768]{1,0:T(8,128)(2,1)S(1)}, bf16[192,768]{1,0:T(8,128)(2,1)S(1)}, bf16[256,768]{1,0:T(8,128)(2,1)S(1)}, bf16[256,768]{1,0:T(8,128)(2...) custom-call(f32[256,768]{1,0:T(8,128)S(1)} %get-tuple-element.155.re, ...), custom_call_target="tpu_custom_call" | custom-call | flops 3019898880 | bytes 4980736 | tf_op jit(solution)/shard_map/pallas_call | solution.py:190
  99.1 1.6 %collective-permute-done.41.b = f32[192,768]{1,0:T(8,128)S(1)} collective-permute-done((f32[192,768]{1,0:T(8,128)S(1)}, f32[192,768]{1,0:T(8,128)S(1)}, u32[]{:S(2)}, u32[]{:S(2)}) %collective-permute-start.41) | collective-permute-done | bytes 589856 | tf_op jit(solution)/shard_map/ppermute | solution.py:203
  100.8 1.0 collective-permute-start.47
  101.8 1.1 collective-permute-start.44
  102.9 1.0 collective-permute-start.46
  103.8 3.7 %collective-permute-done.47.c = f32[48,768]{1,0:T(8,128)S(1)} collective-permute-done((f32[48,768]{1,0:T(8,128)S(1)}, f32[48,768]{1,0:T(8,128)S(1)}, u32[]{:S(2)}, u32[]{:S(2)}) %collective-permute-start.47) | collective-permute-done | bytes 147488 | tf_op jit(solution)/shard_map/ppermute | solution.py:203
  107.5 0.9 collective-permute-start.48
  108.5 1.8 %collective-permute-start.42 = (f32[48,768]{1,0:T(8,128)S(1)}, f32[48,768]{1,0:T(8,128)S(1)}, u32[]{:S(2)}, u32[]{:S(2)}) collective-permute-start(f32[48,768]{1,0:T(8,128)S(1)} %get-tuple-element.167), channel_id=1, source_target_pairs={{0,2},{1,3},{2,0},{3,1},{4,6},{5,7},{6,4},{7,5},{8,10},{9,11},{10,... | collective-permute-start | bytes 442376 | tf_op jit(solution)/shard_map/ppermute | solution.py:203
  110.7 0.9 collective-permute-start.45
  111.6 2.2 %collective-permute-done.46.c = f32[48,768]{1,0:T(8,128)S(1)} collective-permute-done((f32[48,768]{1,0:T(8,128)S(1)}, f32[48,768]{1,0:T(8,128)S(1)}, u32[]{:S(2)}, u32[]{:S(2)}) %collective-permute-start.46) | collective-permute-done | bytes 147488 | tf_op jit(solution)/shard_map/ppermute | solution.py:203
  113.9 2.7 %collective-permute-start.49 = (f32[48,768]{1,0:T(8,128)S(1)}, f32[48,768]{1,0:T(8,128)S(1)}, u32[]{:S(2)}, u32[]{:S(2)}) collective-permute-start(f32[48,768]{1,0:T(8,128)S(1)} %shard_map.156), channel_id=1, source_target_pairs={{0,8},{1,9},{2,10},{3,11},{4,12},{5,13},{6,14},{7,15},{8,0},{9,1},... | collective-permute-start | bytes 442376 | tf_op jit(solution)/shard_map/ppermute | solution.py:203
  116.7 2.3 %shard_map.149 = (f32[256,768]{1,0:T(8,128)}, f32[1,256]{1,0:T(1,128)}) custom-call(s32[1]{0:T(128)} %bitcast.me_ref, bf16[256,768]{1,0:T(8,128)(2,1)S(1)} %get-tuple-element.168.grad_high, bf16[256,768]{1,0:T(8,128)(2,1)S(1)} %get-tuple-element.169.grad_low, bf16[192,768]{1,0:T(8,128)(2,1)S(1)} %get-tuple-element.170.rest_0_, ...), custom_call_target="tpu_custom_call" | custom-call | bytes 3933188 | tf_op jit(solution)/shard_map/pallas_call | solution.py:190
  119.0 2.2 %shard_map.150 = (f32[512,768]{1,0:T(8,128)}, f32[1,512]{1,0:T(1,128)}) custom-call(f32[256,512]{1,0:T(8,128)S(1)} %get-tuple-element.183.grad_scores, bf16[256,768]{1,0:T(8,128)(2,1)S(1)} %get-tuple-element.184.product_high, bf16[256,768]{1,0:T(8,128)(2,1)S(1)} %get-tuple-element.185.product_low, f32[256,768]{1,0:T(8,128)S(1)} %collective-permute-done.39.refs_0_, ...), custom_call_target="tpu_custom_call" | custom-call | flops 603979776 | bytes 2908160 | tf_op jit(solution)/shard_map/pallas_call | solution.py:190
  121.3 1.6 %collective-permute-done.49.rest_1_ = f32[48,768]{1,0:T(8,128)S(1)} collective-permute-done((f32[48,768]{1,0:T(8,128)S(1)}, f32[48,768]{1,0:T(8,128)S(1)}, u32[]{:S(2)}, u32[]{:S(2)}) %collective-permute-start.49) | collective-permute-done | bytes 147488 | tf_op jit(solution)/shard_map/ppermute | solution.py:203
  122.8 0.8 shard_map.157
  (103 shorter events, 12.7 us)
Async XLA Ops:
  0.6 11.4 %collective-permute-start.7 = (f32[48,768]{1,0:T(8,128)}, f32[48,768]{1,0:T(8,128)S(1)}, u32[]{:S(2)}, u32[]{:S(2)}) collective-permute-start(f32[48,768]{1,0:T(8,128)} %relation.1), channel_id=1, source_target_pairs={{0,8},{1,9},{2,10},{3,11},{4,12},{5,13},{6,14},{7,15},{8,0},{9,1},... | collective-permute-start | bytes 442376 | tf_op jit(solution)/shard_map/ppermute | solution.py:203
  4.7 8.0 %collective-permute-start.3 = (f32[48,768]{1,0:T(8,128)}, f32[48,768]{1,0:T(8,128)S(1)}, u32[]{:S(2)}, u32[]{:S(2)}) collective-permute-start(f32[48,768]{1,0:T(8,128)} %relation.1), channel_id=1, source_target_pairs={{0,4},{1,5},{2,6},{3,7},{4,0},{5,1},{6,2},{7,3},{8,12},{9,13},{10,... | collective-permute-start | bytes 442376 | tf_op jit(solution)/shard_map/ppermute | solution.py:203
  6.3 8.0 %collective-permute-start.1 = (f32[48,768]{1,0:T(8,128)}, f32[48,768]{1,0:T(8,128)S(1)}, u32[]{:S(2)}, u32[]{:S(2)}) collective-permute-start(f32[48,768]{1,0:T(8,128)} %relation.1), channel_id=1, source_target_pairs={{0,2},{1,3},{2,0},{3,1},{4,6},{5,7},{6,4},{7,5},{8,10},{9,11},{10,... | collective-permute-start | bytes 442376 | tf_op jit(solution)/shard_map/ppermute | solution.py:203
  7.8 7.0 %collective-permute-start = (f32[48,768]{1,0:T(8,128)}, f32[48,768]{1,0:T(8,128)S(1)}, u32[]{:S(2)}, u32[]{:S(2)}) collective-permute-start(f32[48,768]{1,0:T(8,128)} %relation.1), channel_id=1, source_target_pairs={{0,1},{1,0},{2,3},{3,2},{4,5},{5,4},{6,7},{7,6},{8,9},{9,8},{10,11... | collective-permute-start | bytes 442376 | tf_op jit(solution)/shard_map/ppermute | solution.py:203
  12.1 5.1 %collective-permute-start.11 = (f32[48,768]{1,0:T(8,128)S(1)}, f32[48,768]{1,0:T(8,128)S(1)}, u32[]{:S(2)}, u32[]{:S(2)}) collective-permute-start(f32[48,768]{1,0:T(8,128)S(1)} %collective-permute-done.7.refs_1_), channel_id=1, source_target_pairs={{0,4},{1,5},{2,6},{3,7},{4,0},{5,1},{6,2},{7,3},{8,12},{9,13},{10,... | collective-permute-start | bytes 442376 | tf_op jit(solution)/shard_map/ppermute | solution.py:203
  12.8 6.3 %collective-permute-start.5 = (f32[48,768]{1,0:T(8,128)S(1)}, f32[48,768]{1,0:T(8,128)S(1)}, u32[]{:S(2)}, u32[]{:S(2)}) collective-permute-start(f32[48,768]{1,0:T(8,128)S(1)} %collective-permute-done.3.refs_1_), channel_id=1, source_target_pairs={{0,2},{1,3},{2,0},{3,1},{4,6},{5,7},{6,4},{7,5},{8,10},{9,11},{10,... | collective-permute-start | bytes 442376 | tf_op jit(solution)/shard_map/ppermute | solution.py:203
  14.3 8.5 %collective-permute-start.2 = (f32[48,768]{1,0:T(8,128)S(1)}, f32[48,768]{1,0:T(8,128)S(1)}, u32[]{:S(2)}, u32[]{:S(2)}) collective-permute-start(f32[48,768]{1,0:T(8,128)S(1)} %collective-permute-done.1.refs_2_), channel_id=1, source_target_pairs={{0,1},{1,0},{2,3},{3,2},{4,5},{5,4},{6,7},{7,6},{8,9},{9,8},{10,11... | collective-permute-start | bytes 442376 | tf_op jit(solution)/shard_map/ppermute | solution.py:203
  14.3 9.1 %collective-permute-start.9 = (f32[48,768]{1,0:T(8,128)S(1)}, f32[48,768]{1,0:T(8,128)S(1)}, u32[]{:S(2)}, u32[]{:S(2)}) collective-permute-start(f32[48,768]{1,0:T(8,128)S(1)} %collective-permute-done.7.refs_1_), channel_id=1, source_target_pairs={{0,2},{1,3},{2,0},{3,1},{4,6},{5,7},{6,4},{7,5},{8,10},{9,11},{10,... | collective-permute-start | bytes 442376 | tf_op jit(solution)/shard_map/ppermute | solution.py:203
  14.8 9.2 %collective-permute-start.4 = (f32[48,768]{1,0:T(8,128)S(1)}, f32[48,768]{1,0:T(8,128)S(1)}, u32[]{:S(2)}, u32[]{:S(2)}) collective-permute-start(f32[48,768]{1,0:T(8,128)S(1)} %collective-permute-done.3.refs_1_), channel_id=1, source_target_pairs={{0,1},{1,0},{2,3},{3,2},{4,5},{5,4},{6,7},{7,6},{8,9},{9,8},{10,11... | collective-permute-start | bytes 442376 | tf_op jit(solution)/shard_map/ppermute | solution.py:203
  17.2 7.4 %collective-permute-start.13 = (f32[48,768]{1,0:T(8,128)S(1)}, f32[48,768]{1,0:T(8,128)S(1)}, u32[]{:S(2)}, u32[]{:S(2)}) collective-permute-start(f32[48,768]{1,0:T(8,128)S(1)} %collective-permute-done.11.refs_1_), channel_id=1, source_target_pairs={{0,2},{1,3},{2,0},{3,1},{4,6},{5,7},{6,4},{7,5},{8,10},{9,11},{10,... | collective-permute-start | bytes 442376 | tf_op jit(solution)/shard_map/ppermute | solution.py:203
  19.1 5.5 %collective-permute-start.6 = (f32[48,768]{1,0:T(8,128)S(1)}, f32[48,768]{1,0:T(8,128)S(1)}, u32[]{:S(2)}, u32[]{:S(2)}) collective-permute-start(f32[48,768]{1,0:T(8,128)S(1)} %collective-permute-done.5.refs_3_), channel_id=1, source_target_pairs={{0,1},{1,0},{2,3},{3,2},{4,5},{5,4},{6,7},{7,6},{8,9},{9,8},{10,11... | collective-permute-start | bytes 442376 | tf_op jit(solution)/shard_map/ppermute | solution.py:203
  22.8 2.3 %collective-permute-start.8 = (f32[48,768]{1,0:T(8,128)S(1)}, f32[48,768]{1,0:T(8,128)S(1)}, u32[]{:S(2)}, u32[]{:S(2)}) collective-permute-start(f32[48,768]{1,0:T(8,128)S(1)} %collective-permute-done.7.refs_1_), channel_id=1, source_target_pairs={{0,1},{1,0},{2,3},{3,2},{4,5},{5,4},{6,7},{7,6},{8,9},{9,8},{10,11... | collective-permute-start | bytes 442376 | tf_op jit(solution)/shard_map/ppermute | solution.py:203
  23.4 1.7 %collective-permute-start.10 = (f32[48,768]{1,0:T(8,128)S(1)}, f32[48,768]{1,0:T(8,128)S(1)}, u32[]{:S(2)}, u32[]{:S(2)}) collective-permute-start(f32[48,768]{1,0:T(8,128)S(1)} %collective-permute-done.9.refs_3_), channel_id=1, source_target_pairs={{0,1},{1,0},{2,3},{3,2},{4,5},{5,4},{6,7},{7,6},{8,9},{9,8},{10,11... | collective-permute-start | bytes 442376 | tf_op jit(solution)/shard_map/ppermute | solution.py:203
  24.0 1.6 %collective-permute-start.12 = (f32[48,768]{1,0:T(8,128)S(1)}, f32[48,768]{1,0:T(8,128)S(1)}, u32[]{:S(2)}, u32[]{:S(2)}) collective-permute-start(f32[48,768]{1,0:T(8,128)S(1)} %collective-permute-done.11.refs_1_), channel_id=1, source_target_pairs={{0,1},{1,0},{2,3},{3,2},{4,5},{5,4},{6,7},{7,6},{8,9},{9,8},{10,11... | collective-permute-start | bytes 442376 | tf_op jit(solution)/shard_map/ppermute | solution.py:203
  29.2 3.7 %collective-permute-start.16 = (f32[192,768]{1,0:T(8,128)S(1)}, f32[192,768]{1,0:T(8,128)S(1)}, u32[]{:S(2)}, u32[]{:S(2)}) collective-permute-start(f32[192,768]{1,0:T(8,128)S(1)} %get-tuple-element.122), channel_id=1, source_target_pairs={{0,1},{1,0},{2,3},{3,2},{4,5},{5,4},{6,7},{7,6},{8,9},{9,8},{10,11... | collective-permute-start | bytes 1769480 | tf_op jit(solution)/shard_map/ppermute | solution.py:203
  29.5 5.5 %collective-permute-start.15 = (f32[192,768]{1,0:T(8,128)S(1)}, f32[192,768]{1,0:T(8,128)S(1)}, u32[]{:S(2)}, u32[]{:S(2)}) collective-permute-start(f32[192,768]{1,0:T(8,128)S(1)} %get-tuple-element.120), channel_id=1, source_target_pairs={{0,1},{1,0},{2,3},{3,2},{4,5},{5,4},{6,7},{7,6},{8,9},{9,8},{10,11... | collective-permute-start | bytes 1769480 | tf_op jit(solution)/shard_map/ppermute | solution.py:203
  30.9 52.1 %collective-permute-start.40 = (f32[264,768]{1,0:T(8,128)S(1)}, f32[264,768]{1,0:T(8,128)S(1)}, u32[]{:S(2)}, u32[]{:S(2)}) collective-permute-start(f32[264,768]{1,0:T(8,128)S(1)} %get-tuple-element.161), channel_id=1, source_target_pairs={{0,1},{1,2},{2,3},{3,4},{4,5},{5,6},{6,7},{7,8},{8,9},{9,10},{10,1... | collective-permute-start | bytes 2433032 | tf_op jit(solution)/shard_map/ppermute | solution.py:336
  31.1 50.7 %collective-permute-start.39 = (f32[256,768]{1,0:T(8,128)S(1)}, f32[256,768]{1,0:T(8,128)S(1)}, u32[]{:S(2)}, u32[]{:S(2)}) collective-permute-start(f32[256,768]{1,0:T(8,128)S(1)} %get-tuple-element.160), channel_id=1, source_target_pairs={{0,1},{1,2},{2,3},{3,4},{4,5},{5,6},{6,7},{7,8},{8,9},{9,10},{10,1... | collective-permute-start | bytes 2359304 | tf_op jit(solution)/shard_map/ppermute | solution.py:336
  32.9 23.9 %collective-permute-start.21 = (f32[48,768]{1,0:T(8,128)S(1)}, f32[48,768]{1,0:T(8,128)S(1)}, u32[]{:S(2)}, u32[]{:S(2)}) collective-permute-start(f32[48,768]{1,0:T(8,128)S(1)} %get-tuple-element.126), channel_id=1, source_target_pairs={{0,2},{1,3},{2,0},{3,1},{4,6},{5,7},{6,4},{7,5},{8,10},{9,11},{10,... | collective-permute-start | bytes 442376 | tf_op jit(solution)/shard_map/ppermute | solution.py:203
  33.6 26.4 %collective-permute-start.18 = (f32[48,768]{1,0:T(8,128)S(1)}, f32[48,768]{1,0:T(8,128)S(1)}, u32[]{:S(2)}, u32[]{:S(2)}) collective-permute-start(f32[48,768]{1,0:T(8,128)S(1)} %get-tuple-element.124), channel_id=1, source_target_pairs={{0,2},{1,3},{2,0},{3,1},{4,6},{5,7},{6,4},{7,5},{8,10},{9,11},{10,... | collective-permute-start | bytes 442376 | tf_op jit(solution)/shard_map/ppermute | solution.py:203
  35.0 28.1 %collective-permute-start.20 = (f32[48,768]{1,0:T(8,128)S(1)}, f32[48,768]{1,0:T(8,128)S(1)}, u32[]{:S(2)}, u32[]{:S(2)}) collective-permute-start(f32[48,768]{1,0:T(8,128)S(1)} %get-tuple-element.125), channel_id=1, source_target_pairs={{0,2},{1,3},{2,0},{3,1},{4,6},{5,7},{6,4},{7,5},{8,10},{9,11},{10,... | collective-permute-start | bytes 442376 | tf_op jit(solution)/shard_map/ppermute | solution.py:203
  56.8 6.3 %collective-permute-start.22 = (f32[48,768]{1,0:T(8,128)S(1)}, f32[48,768]{1,0:T(8,128)S(1)}, u32[]{:S(2)}, u32[]{:S(2)}) collective-permute-start(f32[48,768]{1,0:T(8,128)S(1)} %shard_map.138), channel_id=1, source_target_pairs={{0,4},{1,5},{2,6},{3,7},{4,0},{5,1},{6,2},{7,3},{8,12},{9,13},{10,... | collective-permute-start | bytes 442376 | tf_op jit(solution)/shard_map/ppermute | solution.py:203
  60.0 5.8 %collective-permute-start.17 = (f32[48,768]{1,0:T(8,128)S(1)}, f32[48,768]{1,0:T(8,128)S(1)}, u32[]{:S(2)}, u32[]{:S(2)}) collective-permute-start(f32[48,768]{1,0:T(8,128)S(1)} %get-tuple-element.123), channel_id=1, source_target_pairs={{0,2},{1,3},{2,0},{3,1},{4,6},{5,7},{6,4},{7,5},{8,10},{9,11},{10,... | collective-permute-start | bytes 442376 | tf_op jit(solution)/shard_map/ppermute | solution.py:203
  63.1 7.9 %collective-permute-start.19 = (f32[48,768]{1,0:T(8,128)S(1)}, f32[48,768]{1,0:T(8,128)S(1)}, u32[]{:S(2)}, u32[]{:S(2)}) collective-permute-start(f32[48,768]{1,0:T(8,128)S(1)} %shard_map.135), channel_id=1, source_target_pairs={{0,4},{1,5},{2,6},{3,7},{4,0},{5,1},{6,2},{7,3},{8,12},{9,13},{10,... | collective-permute-start | bytes 442376 | tf_op jit(solution)/shard_map/ppermute | solution.py:203
  63.2 7.9 %collective-permute-start.23 = (f32[48,768]{1,0:T(8,128)S(1)}, f32[48,768]{1,0:T(8,128)S(1)}, u32[]{:S(2)}, u32[]{:S(2)}) collective-permute-start(f32[48,768]{1,0:T(8,128)S(1)} %shard_map.139), channel_id=1, source_target_pairs={{0,8},{1,9},{2,10},{3,11},{4,12},{5,13},{6,14},{7,15},{8,0},{9,1},... | collective-permute-start | bytes 442376 | tf_op jit(solution)/shard_map/ppermute | solution.py:203
  71.2 8.7 %collective-permute-start.31 = (f32[48,768]{1,0:T(8,128)S(1)}, f32[48,768]{1,0:T(8,128)S(1)}, u32[]{:S(2)}, u32[]{:S(2)}) collective-permute-start(f32[48,768]{1,0:T(8,128)S(1)} %get-tuple-element.128.refs_0_.relation), channel_id=1, source_target_pairs={{0,8},{1,9},{2,10},{3,11},{4,12},{5,13},{6,14},{7,15},{8,0},{9,1},... | collective-permute-start | bytes 442376 | tf_op jit(solution)/shard_map/ppermute | solution.py:203
  72.6 8.0 %collective-permute-start.27 = (f32[48,768]{1,0:T(8,128)S(1)}, f32[48,768]{1,0:T(8,128)S(1)}, u32[]{:S(2)}, u32[]{:S(2)}) collective-permute-start(f32[48,768]{1,0:T(8,128)S(1)} %get-tuple-element.128.refs_0_.relation), channel_id=1, source_target_pairs={{0,4},{1,5},{2,6},{3,7},{4,0},{5,1},{6,2},{7,3},{8,12},{9,13},{10,... | collective-permute-start | bytes 442376 | tf_op jit(solution)/shard_map/ppermute | solution.py:203
  76.6 6.3 %collective-permute-start.25 = (f32[48,768]{1,0:T(8,128)S(1)}, f32[48,768]{1,0:T(8,128)S(1)}, u32[]{:S(2)}, u32[]{:S(2)}) collective-permute-start(f32[48,768]{1,0:T(8,128)S(1)} %get-tuple-element.128.refs_0_.relation), channel_id=1, source_target_pairs={{0,2},{1,3},{2,0},{3,1},{4,6},{5,7},{6,4},{7,5},{8,10},{9,11},{10,... | collective-permute-start | bytes 442376 | tf_op jit(solution)/shard_map/ppermute | solution.py:203
  80.0 3.9 %collective-permute-start.24 = (f32[48,768]{1,0:T(8,128)S(1)}, f32[48,768]{1,0:T(8,128)S(1)}, u32[]{:S(2)}, u32[]{:S(2)}) collective-permute-start(f32[48,768]{1,0:T(8,128)S(1)} %get-tuple-element.128.refs_0_.relation), channel_id=1, source_target_pairs={{0,1},{1,0},{2,3},{3,2},{4,5},{5,4},{6,7},{7,6},{8,9},{9,8},{10,11... | collective-permute-start | bytes 442376 | tf_op jit(solution)/shard_map/ppermute | solution.py:203
  80.7 5.6 %collective-permute-start.35 = (f32[48,768]{1,0:T(8,128)S(1)}, f32[48,768]{1,0:T(8,128)S(1)}, u32[]{:S(2)}, u32[]{:S(2)}) collective-permute-start(f32[48,768]{1,0:T(8,128)S(1)} %collective-permute-done.31.refs_1_), channel_id=1, source_target_pairs={{0,4},{1,5},{2,6},{3,7},{4,0},{5,1},{6,2},{7,3},{8,12},{9,13},{10,... | collective-permute-start | bytes 442376 | tf_op jit(solution)/shard_map/ppermute | solution.py:203
  81.8 6.7 %collective-permute-start.29 = (f32[48,768]{1,0:T(8,128)S(1)}, f32[48,768]{1,0:T(8,128)S(1)}, u32[]{:S(2)}, u32[]{:S(2)}) collective-permute-start(f32[48,768]{1,0:T(8,128)S(1)} %collective-permute-done.27.refs_1_), channel_id=1, source_target_pairs={{0,2},{1,3},{2,0},{3,1},{4,6},{5,7},{6,4},{7,5},{8,10},{9,11},{10,... | collective-permute-start | bytes 442376 | tf_op jit(solution)/shard_map/ppermute | solution.py:203
  82.9 5.6 %collective-permute-start.26 = (f32[48,768]{1,0:T(8,128)S(1)}, f32[48,768]{1,0:T(8,128)S(1)}, u32[]{:S(2)}, u32[]{:S(2)}) collective-permute-start(f32[48,768]{1,0:T(8,128)S(1)} %collective-permute-done.25.refs_2_), channel_id=1, source_target_pairs={{0,1},{1,0},{2,3},{3,2},{4,5},{5,4},{6,7},{7,6},{8,9},{9,8},{10,11... | collective-permute-start | bytes 442376 | tf_op jit(solution)/shard_map/ppermute | solution.py:203
  83.0 8.7 %collective-permute-start.33 = (f32[48,768]{1,0:T(8,128)S(1)}, f32[48,768]{1,0:T(8,128)S(1)}, u32[]{:S(2)}, u32[]{:S(2)}) collective-permute-start(f32[48,768]{1,0:T(8,128)S(1)} %collective-permute-done.31.refs_1_), channel_id=1, source_target_pairs={{0,2},{1,3},{2,0},{3,1},{4,6},{5,7},{6,4},{7,5},{8,10},{9,11},{10,... | collective-permute-start | bytes 442376 | tf_op jit(solution)/shard_map/ppermute | solution.py:203
  83.9 8.3 %collective-permute-start.28 = (f32[48,768]{1,0:T(8,128)S(1)}, f32[48,768]{1,0:T(8,128)S(1)}, u32[]{:S(2)}, u32[]{:S(2)}) collective-permute-start(f32[48,768]{1,0:T(8,128)S(1)} %collective-permute-done.27.refs_1_), channel_id=1, source_target_pairs={{0,1},{1,0},{2,3},{3,2},{4,5},{5,4},{6,7},{7,6},{8,9},{9,8},{10,11... | collective-permute-start | bytes 442376 | tf_op jit(solution)/shard_map/ppermute | solution.py:203
  86.2 7.7 %collective-permute-start.37 = (f32[48,768]{1,0:T(8,128)S(1)}, f32[48,768]{1,0:T(8,128)S(1)}, u32[]{:S(2)}, u32[]{:S(2)}) collective-permute-start(f32[48,768]{1,0:T(8,128)S(1)} %collective-permute-done.35.refs_1_), channel_id=1, source_target_pairs={{0,2},{1,3},{2,0},{3,1},{4,6},{5,7},{6,4},{7,5},{8,10},{9,11},{10,... | collective-permute-start | bytes 442376 | tf_op jit(solution)/shard_map/ppermute | solution.py:203
  88.5 5.6 %collective-permute-start.30 = (f32[48,768]{1,0:T(8,128)S(1)}, f32[48,768]{1,0:T(8,128)S(1)}, u32[]{:S(2)}, u32[]{:S(2)}) collective-permute-start(f32[48,768]{1,0:T(8,128)S(1)} %collective-permute-done.29.refs_3_), channel_id=1, source_target_pairs={{0,1},{1,0},{2,3},{3,2},{4,5},{5,4},{6,7},{7,6},{8,9},{9,8},{10,11... | collective-permute-start | bytes 442376 | tf_op jit(solution)/shard_map/ppermute | solution.py:203
  88.5 6.2 %collective-permute-start.32 = (f32[48,768]{1,0:T(8,128)S(1)}, f32[48,768]{1,0:T(8,128)S(1)}, u32[]{:S(2)}, u32[]{:S(2)}) collective-permute-start(f32[48,768]{1,0:T(8,128)S(1)} %collective-permute-done.31.refs_1_), channel_id=1, source_target_pairs={{0,1},{1,0},{2,3},{3,2},{4,5},{5,4},{6,7},{7,6},{8,9},{9,8},{10,11... | collective-permute-start | bytes 442376 | tf_op jit(solution)/shard_map/ppermute | solution.py:203
  91.7 3.0 %collective-permute-start.34 = (f32[48,768]{1,0:T(8,128)S(1)}, f32[48,768]{1,0:T(8,128)S(1)}, u32[]{:S(2)}, u32[]{:S(2)}) collective-permute-start(f32[48,768]{1,0:T(8,128)S(1)} %collective-permute-done.33.refs_3_), channel_id=1, source_target_pairs={{0,1},{1,0},{2,3},{3,2},{4,5},{5,4},{6,7},{7,6},{8,9},{9,8},{10,11... | collective-permute-start | bytes 442376 | tf_op jit(solution)/shard_map/ppermute | solution.py:203
  92.2 3.0 %collective-permute-start.36 = (f32[48,768]{1,0:T(8,128)S(1)}, f32[48,768]{1,0:T(8,128)S(1)}, u32[]{:S(2)}, u32[]{:S(2)}) collective-permute-start(f32[48,768]{1,0:T(8,128)S(1)} %collective-permute-done.35.refs_1_), channel_id=1, source_target_pairs={{0,1},{1,0},{2,3},{3,2},{4,5},{5,4},{6,7},{7,6},{8,9},{9,8},{10,11... | collective-permute-start | bytes 442376 | tf_op jit(solution)/shard_map/ppermute | solution.py:203
  98.6 2.1 %collective-permute-start.41 = (f32[192,768]{1,0:T(8,128)S(1)}, f32[192,768]{1,0:T(8,128)S(1)}, u32[]{:S(2)}, u32[]{:S(2)}) collective-permute-start(f32[192,768]{1,0:T(8,128)S(1)} %get-tuple-element.166), channel_id=1, source_target_pairs={{0,1},{1,0},{2,3},{3,2},{4,5},{5,4},{6,7},{7,6},{8,9},{9,8},{10,11... | collective-permute-start | bytes 1769480 | tf_op jit(solution)/shard_map/ppermute | solution.py:203
  99.1 4.8 %collective-permute-start.43 = (f32[192,768]{1,0:T(8,128)S(1)}, f32[192,768]{1,0:T(8,128)S(1)}, u32[]{:S(2)}, u32[]{:S(2)}) collective-permute-start(f32[192,768]{1,0:T(8,128)S(1)} %get-tuple-element.190), channel_id=1, source_target_pairs={{0,1},{1,0},{2,3},{3,2},{4,5},{5,4},{6,7},{7,6},{8,9},{9,8},{10,11... | collective-permute-start | bytes 1769480 | tf_op jit(solution)/shard_map/ppermute | solution.py:203
  100.8 6.7 %collective-permute-start.47 = (f32[48,768]{1,0:T(8,128)S(1)}, f32[48,768]{1,0:T(8,128)S(1)}, u32[]{:S(2)}, u32[]{:S(2)}) collective-permute-start(f32[48,768]{1,0:T(8,128)S(1)} %get-tuple-element.193), channel_id=1, source_target_pairs={{0,2},{1,3},{2,0},{3,1},{4,6},{5,7},{6,4},{7,5},{8,10},{9,11},{10,... | collective-permute-start | bytes 442376 | tf_op jit(solution)/shard_map/ppermute | solution.py:203
  101.8 8.9 %collective-permute-start.44 = (f32[48,768]{1,0:T(8,128)S(1)}, f32[48,768]{1,0:T(8,128)S(1)}, u32[]{:S(2)}, u32[]{:S(2)}) collective-permute-start(f32[48,768]{1,0:T(8,128)S(1)} %get-tuple-element.191), channel_id=1, source_target_pairs={{0,2},{1,3},{2,0},{3,1},{4,6},{5,7},{6,4},{7,5},{8,10},{9,11},{10,... | collective-permute-start | bytes 442376 | tf_op jit(solution)/shard_map/ppermute | solution.py:203
  102.9 11.0 %collective-permute-start.46 = (f32[48,768]{1,0:T(8,128)S(1)}, f32[48,768]{1,0:T(8,128)S(1)}, u32[]{:S(2)}, u32[]{:S(2)}) collective-permute-start(f32[48,768]{1,0:T(8,128)S(1)} %get-tuple-element.192), channel_id=1, source_target_pairs={{0,2},{1,3},{2,0},{3,1},{4,6},{5,7},{6,4},{7,5},{8,10},{9,11},{10,... | collective-permute-start | bytes 442376 | tf_op jit(solution)/shard_map/ppermute | solution.py:203
  107.5 6.3 %collective-permute-start.48 = (f32[48,768]{1,0:T(8,128)S(1)}, f32[48,768]{1,0:T(8,128)S(1)}, u32[]{:S(2)}, u32[]{:S(2)}) collective-permute-start(f32[48,768]{1,0:T(8,128)S(1)} %shard_map.155), channel_id=1, source_target_pairs={{0,4},{1,5},{2,6},{3,7},{4,0},{5,1},{6,2},{7,3},{8,12},{9,13},{10,... | collective-permute-start | bytes 442376 | tf_op jit(solution)/shard_map/ppermute | solution.py:203
  108.5 8.2 %collective-permute-start.42 = (f32[48,768]{1,0:T(8,128)S(1)}, f32[48,768]{1,0:T(8,128)S(1)}, u32[]{:S(2)}, u32[]{:S(2)}) collective-permute-start(f32[48,768]{1,0:T(8,128)S(1)} %get-tuple-element.167), channel_id=1, source_target_pairs={{0,2},{1,3},{2,0},{3,1},{4,6},{5,7},{6,4},{7,5},{8,10},{9,11},{10,... | collective-permute-start | bytes 442376 | tf_op jit(solution)/shard_map/ppermute | solution.py:203
  110.7 10.5 %collective-permute-start.45 = (f32[48,768]{1,0:T(8,128)S(1)}, f32[48,768]{1,0:T(8,128)S(1)}, u32[]{:S(2)}, u32[]{:S(2)}) collective-permute-start(f32[48,768]{1,0:T(8,128)S(1)} %shard_map.152), channel_id=1, source_target_pairs={{0,4},{1,5},{2,6},{3,7},{4,0},{5,1},{6,2},{7,3},{8,12},{9,13},{10,... | collective-permute-start | bytes 442376 | tf_op jit(solution)/shard_map/ppermute | solution.py:203
  113.9 8.9 %collective-permute-start.49 = (f32[48,768]{1,0:T(8,128)S(1)}, f32[48,768]{1,0:T(8,128)S(1)}, u32[]{:S(2)}, u32[]{:S(2)}) collective-permute-start(f32[48,768]{1,0:T(8,128)S(1)} %shard_map.156), channel_id=1, source_target_pairs={{0,8},{1,9},{2,10},{3,11},{4,12},{5,13},{6,14},{7,15},{8,0},{9,1},... | collective-permute-start | bytes 442376 | tf_op jit(solution)/shard_map/ppermute | solution.py:203
  (12 other events, 67.5 us)

commit v4 on v3

--- a/solution.py
+++ b/solution.py
@@ -13,7 +13,7 @@
 NT = (((1,), (1,)), ((), ()))
 VMEM = pl.BlockSpec(memory_space=pltpu.VMEM)
 SMEM = pl.BlockSpec(memory_space=pltpu.SMEM)
-CHUNKS = 2
+CHUNKS = 1
 
 
 def split(x):
@@ -101,42 +101,50 @@
     product[...] = term if first else before[...] + term
 
 
-def bucket_kernel(bucket, first, count, picks, *refs):
+def scores_kernel(bucket, first, count, rows, *refs):
     before, refs = (None, refs) if first else (refs[0], refs[1:])
     blocks, refs = refs[:count], refs[count:]
-    heads, turned, tails, marks = refs[0:2], refs[2:4], refs[4:6], refs[6]
-    relation, product, scores, grad, pieces = refs[7:9], refs[9:11], refs[11], refs[12:14], refs[14:]
+    heads, halves, marks, refs = refs[0:2], refs[2:4], refs[4], refs[5:]
+    if rows:
+        tails, state, refs = refs[0], refs[1], refs[2:]
+    relation, product, scores, chunks = refs[0:2], refs[2:4], refs[4], refs[5:]
     whole = add_product(blocks, heads, relation)
     prod = split(whole if first else before[...] + whole)
     product[0][...], product[1][...] = prod
-    tail = (tails[0][...], tails[1][...])
-    grad_scores = (jax.nn.sigmoid(dot3(prod, tail, NT)) - marks[bucket]) * 0.0625
+    grad_scores = (jax.nn.sigmoid(dot3(prod, (halves[0][...], halves[1][...]), NT)) - marks[bucket]) * 0.0625
     scores[...] = grad_scores
-    grad_product = split(dot3(split(grad_scores), tail, NN))
-    grad[0][...], grad[1][...] = grad_product
-    whole = dot3((turned[0][...], turned[1][...]), grad_product, NN)
-    rows = whole.shape[0] // sum(len(slots) for slots in picks)
-    for piece, slots in zip(pieces, picks):
-        for i, r in enumerate(slots):
-            piece[i * rows : (i + 1) * rows, :] = whole[r * rows : (r + 1) * rows, :]
-
-
-def tails_kernel(chunks, last, grad_scores, product_high, product_low, *refs):
+    if rows:
+        grad = dot3(split(grad_scores.T), prod, NN)
+        new, new_state = adagrad(tails[...], state[...], grad)
+        at = 0
+        for chunk, n in zip(chunks, rows):
+            chunk[:n, :] = new[at : at + n, :]
+            at += n
+        chunks[-1][rows[-1] :, :] = jnp.zeros((chunks[-1].shape[0] - rows[-1], new.shape[1]), F32)
+        chunks[-1][rows[-1] : rows[-1] + 1, : tails.shape[0]] = new_state
+
+
+def grads_kernel(picks, turned_high, turned_low, scores, high, low, *refs):
+    grad = split(dot3(split(scores[...]), (high[...], low[...]), NN))
+    refs[0][...], refs[1][...] = grad
+    relation_term_kernel(picks, turned_high, turned_low, *refs)
+
+
+def relation_term_kernel(picks, turned_high, turned_low, grad_high, grad_low, *pieces):
+    rows = turned_high.shape[0] // picks[0]
+    grad = grad_high[...], grad_low[...]
+    for piece, slots in zip(pieces, picks[1:]):
+        high = jnp.concatenate([turned_high[r * rows : (r + 1) * rows, :] for r in slots], axis=0)
+        low = jnp.concatenate([turned_low[r * rows : (r + 1) * rows, :] for r in slots], axis=0)
+        piece[...] = dot3((high, low), grad, NN)
+
+
+def tails_kernel(rows, grad_scores, product_high, product_low, *refs):
     grad = dot3(split(grad_scores[...].T), (product_high[...], product_low[...]), NN)
-    if last:
-        tails, outs = refs[:chunks], refs[chunks:]
-        rows = [outs[0].shape[0] // chunks] * chunks
-        state = tails[-1][rows[-1] : rows[-1] + 1, : outs[0].shape[0]]
-        held = [t[:n, :] for t, n in zip(tails, rows)]
-        outs[0][...], outs[1][...] = adagrad(jnp.concatenate(held, axis=0), state, grad)
-        return
-    tails, state, outs = refs[0], refs[1], refs[2:]
-    new, new_state = adagrad(tails[...], state[...], grad)
-    rows = tails.shape[0] // chunks
-    for c in range(chunks):
-        outs[c][:rows, :] = new[c * rows : (c + 1) * rows, :]
-    outs[-1][rows:, :] = jnp.zeros((outs[-1].shape[0] - rows, new.shape[1]), F32)
-    outs[-1][rows : rows + 1, : tails.shape[0]] = new_state
+    tails, outs = refs[: len(rows)], refs[len(rows) :]
+    state = tails[-1][rows[-1] : rows[-1] + 1, : outs[0].shape[0]]
+    held = [t[:n, :] for t, n in zip(tails, rows)]
+    outs[0][...], outs[1][...] = adagrad(jnp.concatenate(held, axis=0), state, grad)
 
 
 def heads_kernel(slots, groups, last, me_ref, grad_high, grad_low, *rest):
@@ -153,12 +161,12 @@
         write_head_parts(me_ref[0], new_heads, outs, *rest[-2:], slots)
 
 
-def split_kernel(*refs):
+def split_kernel(rows, *refs):
     chunks, (high, low) = refs[:-2], refs[-2:]
-    rows = high.shape[0] // len(chunks)
-    for c, chunk in enumerate(chunks):
-        at = slice(c * rows, (c + 1) * rows)
-        high[at, :], low[at, :] = split(chunk[:rows, :])
+    at = 0
+    for chunk, n in zip(chunks, rows):
+        high[at : at + n, :], low[at : at + n, :] = split(chunk[:n, :])
+        at += n
 
 
 def sum_kernel(a, b, *totals):
@@ -294,6 +302,8 @@
         [*tail_parts, ((2, *table[0]), F32)],
         [tails, pos_head, pos_tail],
     )
+    rows = [tail_rows // CHUNKS] * CHUNKS
+    sent_shapes = [((r + 8 * (i == CHUNKS - 1), width), F32) for i, r in enumerate(rows)]
     for bucket in range(2):
         last = bucket == 1
         before, relation_half = [], []
@@ -303,10 +313,10 @@
             halves, count = head_half[2 + 2 * g : 4 + 2 * g], len(blocks)
             if closing:
                 out = call(
-                    functools.partial(bucket_kernel, bucket, first, count, picks),
-                    [*relation_parts[g], *row_parts, table, *row_parts, *held],
-                    [*before[-1:], *blocks, *halves, *head_half[:2], *tail_half, marks],
-                    flops=6 * head_rows * width * (2 * width + 2 * tail_rows),
+                    functools.partial(scores_kernel, bucket, first, count, [] if last else rows),
+                    [*relation_parts[g], *row_parts, table, *([] if last else sent_shapes)],
+                    [*before[-1:], *blocks, *halves, *tail_half, marks, *([] if last else [tails, tail_state])],
+                    flops=6 * head_rows * width * (width // len(sizes) + 2 * tail_rows),
                 )
                 relation_half.extend(out[:2])
                 return out
@@ -321,31 +331,43 @@
             return out[0]
 
         out = gathered(relation, head_half, [] if bucket else [*tail_half, marks], bucket == 1, use)
-        product, grad_scores, grad_product, pieces = out[2:4], out[4], out[5:7], out[7:]
+        product, grad_scores, sent = out[2:4], out[4], out[5:]
+        if not last:
+            moves = [(i, (i + 1) % n) for i in range(n)]
+            arrived = [lax.ppermute(v, "blk", moves) for v in sent]
+        pieces = {}
+        for chosen in ((1, 3), (0, 2)) if by_blocks else [(0,)]:
+            wanted = [slots, *[picks[c] for c in chosen]]
+            shapes = [held[c] for c in chosen]
+            if pieces:
+                out = call(
+                    functools.partial(relation_term_kernel, wanted), shapes, [*head_half[:2], *grad_product], flops=6 * head_rows * width * width // 2
+                )
+            else:
+                out = call(
+                    functools.partial(grads_kernel, wanted),
+                    [*row_parts, *shapes],
+                    [*head_half[:2], grad_scores, *tail_half],
+                    flops=6 * head_rows * width * width // 2,
+                )
+                grad_product, out = out[:2], out[2:]
+            pieces.update(zip(chosen, out))
+        pieces = [pieces[c] for c in range(len(picks))]
         terms, crossed = scattered(pieces)
-        tail_rest = {"flops": 6 * head_rows * width * tail_rows}
-        if not last:
-            rows = tail_rows // CHUNKS
-            sent = call(
-                functools.partial(tails_kernel, CHUNKS, last),
-                [((rows, width), F32)] * (CHUNKS - 1) + [((rows + 8, width), F32)],
-                [grad_scores, *product, tails, tail_state],
-                **tail_rest,
-            )
-            sent = [after(v, *()) for v in sent]
-            tails = [lax.ppermute(v, "blk", [(i, (i + 1) % n) for i in range(n)]) for v in sent]
-            tail_half = call(split_kernel, tail_parts, tails)
-        else:
+        if last:
             tails, tail_state = call(
-                functools.partial(tails_kernel, CHUNKS, last),
+                functools.partial(tails_kernel, rows),
                 [((tail_rows, width), F32), (tail_state.shape, F32)],
                 [after(grad_scores, *crossed[-1:]), *product, *tails],
-                **tail_rest,
+                flops=6 * head_rows * width * tail_rows,
             )
+        else:
+            tails = arrived
+            tail_half = call(functools.partial(split_kernel, rows), tail_parts, tails)
         out = call(
             functools.partial(heads_kernel, slots, len(sizes), last),
             [(heads.shape, F32), (head_state.shape, F32), *([] if last else head_parts)],
-            [me, after(grad_product[0], *crossed[-1:]), grad_product[1], *relation_half, heads, head_state],
+            [me, after(grad_product[0], *(crossed[-1:] if last else arrived)), grad_product[1], *relation_half, heads, head_state],
             scratch=[((width, width), BF16)] * 2 + ([] if last else turned),
             smem_first=True,
         )

time: 124 us -> 122 us (0.984)
  starting transfers between devices: 43.2 us -> 35.2 us
  waiting for transfers between devices: 55.3 us -> 60.5 us
    ppermute x48, starting transfers between devices: 41.2 us -> 34.7 us  [partner(): return lax.ppermute(value, 'blk', [(i, i ^ mask) for i in range(n)])]
    ppermute x48, waiting for transfers between devices: 55.3 us -> 60.5 us  [partner(): return lax.ppermute(value, 'blk', [(i, i ^ mask) for i in range(n)])]
    ppermute x2 -> x1, starting transfers between devices: 2 us -> 0.42 us  [body(): arrived = [lax.ppermute(v, 'blk', moves) for v in sent]]
    pallas_call x31 -> x34, Pallas kernels: 20.2 us -> 20.7 us  [call(): pl.pallas_call(kernel, out_shape=[jax.ShapeDtypeStruct(s, t) for s, t in...]
  transfers between devices with their start and end apart: 50 -> 49, of which waited for: 21 -> 24; matrix products, arithmetic and copies ran while one was open for 0% -> 0% of each run, Pallas kernels for 10% -> 12%
where the time goes in v4:
time: 122 us; the launch traced here: 121 us
  waiting for transfers between devices  60.5 us (50%)
  starting transfers between devices  35.2 us (29%)
  Pallas kernels  20.7 us (17%)
  local copies, waits for them, and re-layouts  3.95 us (3%)
    ppermute x48, waiting for transfers between devices, partner(): return lax.ppermute(value, 'blk', [(i, i ^ mask) for i in range(n)])  60.5 us
    ppermute x48, starting transfers between devices, partner(): return lax.ppermute(value, 'blk', [(i, i ^ mask) for i in range(n)])  34.7 us
    pallas_call x34, Pallas kernels, call(): pl.pallas_call(kernel, out_shape=[jax.ShapeDtypeStruct(s, t) for s, t in...  20.7 us
    unnamed x20, local copies, waits for them, and re-layouts  3.95 us
  transfers between devices with their start and end apart: 49, of which 24 were waited for; matrix products, arithmetic and copies ran while one was open for 0% of the time, Pallas kernels for 12%

profile of v4, /device:TPU:0, one launch (start us, length us, event | category | flops | bytes accessed | tf_op | source)
XLA Modules:
  0.0 121.4 jit_solution(14988236125883791611)
XLA Ops:
  0.6 4.1 %collective-permute-start.7 = (f32[48,768]{1,0:T(8,128)}, f32[48,768]{1,0:T(8,128)S(1)}, u32[]{:S(2)}, u32[]{:S(2)}) collective-permute-start(f32[48,768]{1,0:T(8,128)} %relation.1), channel_id=1, source_target_pairs={{0,8},{1,9},{2,10},{3,11},{4,12},{5,13},{6,14},{7,15},{8,0},{9,1},... | collective-permute-start | bytes 442376 | tf_op jit(solution)/shard_map/ppermute | solution.py:211
  4.7 1.6 %collective-permute-start.3 = (f32[48,768]{1,0:T(8,128)}, f32[48,768]{1,0:T(8,128)S(1)}, u32[]{:S(2)}, u32[]{:S(2)}) collective-permute-start(f32[48,768]{1,0:T(8,128)} %relation.1), channel_id=1, source_target_pairs={{0,4},{1,5},{2,6},{3,7},{4,0},{5,1},{6,2},{7,3},{8,12},{9,13},{10,... | collective-permute-start | bytes 442376 | tf_op jit(solution)/shard_map/ppermute | solution.py:211
  6.3 1.5 %collective-permute-start.1 = (f32[48,768]{1,0:T(8,128)}, f32[48,768]{1,0:T(8,128)S(1)}, u32[]{:S(2)}, u32[]{:S(2)}) collective-permute-start(f32[48,768]{1,0:T(8,128)} %relation.1), channel_id=1, source_target_pairs={{0,2},{1,3},{2,0},{3,1},{4,6},{5,7},{6,4},{7,5},{8,10},{9,11},{10,... | collective-permute-start | bytes 442376 | tf_op jit(solution)/shard_map/ppermute | solution.py:211
  7.8 1.1 copy-done.2
  9.6 2.5 %collective-permute-done.7.refs_1_ = f32[48,768]{1,0:T(8,128)S(1)} collective-permute-done((f32[48,768]{1,0:T(8,128)}, f32[48,768]{1,0:T(8,128)S(1)}, u32[]{:S(2)}, u32[]{:S(2)}) %collective-permute-start.7) | collective-permute-done | bytes 147488 | tf_op jit(solution)/shard_map/ppermute | solution.py:211
  12.1 0.7 collective-permute-start.11
  12.8 1.5 %collective-permute-start.5 = (f32[48,768]{1,0:T(8,128)S(1)}, f32[48,768]{1,0:T(8,128)S(1)}, u32[]{:S(2)}, u32[]{:S(2)}) collective-permute-start(f32[48,768]{1,0:T(8,128)S(1)} %collective-permute-done.3.refs_1_), channel_id=1, source_target_pairs={{0,2},{1,3},{2,0},{3,1},{4,6},{5,7},{6,4},{7,5},{8,10},{9,11},{10,... | collective-permute-start | bytes 442376 | tf_op jit(solution)/shard_map/ppermute | solution.py:211
  15.0 2.2 %collective-permute-done.11.refs_1_ = f32[48,768]{1,0:T(8,128)S(1)} collective-permute-done((f32[48,768]{1,0:T(8,128)S(1)}, f32[48,768]{1,0:T(8,128)S(1)}, u32[]{:S(2)}, u32[]{:S(2)}) %collective-permute-start.11) | collective-permute-done | bytes 147488 | tf_op jit(solution)/shard_map/ppermute | solution.py:211
  17.2 1.6 %collective-permute-start.13 = (f32[48,768]{1,0:T(8,128)S(1)}, f32[48,768]{1,0:T(8,128)S(1)}, u32[]{:S(2)}, u32[]{:S(2)}) collective-permute-start(f32[48,768]{1,0:T(8,128)S(1)} %collective-permute-done.11.refs_1_), channel_id=1, source_target_pairs={{0,2},{1,3},{2,0},{3,1},{4,6},{5,7},{6,4},{7,5},{8,10},{9,11},{10,... | collective-permute-start | bytes 442376 | tf_op jit(solution)/shard_map/ppermute | solution.py:211
  19.1 1.4 %copy-done = f32[512,768]{1,0:T(8,128)S(1)} copy-done((f32[512,768]{1,0:T(8,128)S(1)}, f32[512,768]{1,0:T(8,128)}, u32[]{:S(2)}) %copy-start) | copy-done | bytes 1572888
  20.5 0.7 copy-done.5
  21.2 0.7 copy-done.6
  21.9 0.9 shard_map.131
  26.0 2.4 %shard_map.132 = (bf16[192,768]{1,0:T(8,128)(2,1)S(1)}, bf16[192,768]{1,0:T(8,128)(2,1)S(1)}, bf16[256,768]{1,0:T(8,128)(2,1)}, bf16[256,768]{1,0:T(8,128)(2,1)}...) custom-call(f32[256,768]{1,0:T(8,128)S(1)} %get-tuple-element.111.refs_0_, ...), custom_call_target="tpu_custom_call" | custom-call | flops 1434451968 | bytes 5769216 | tf_op jit(solution)/shard_map/pallas_call | solution.py:198
  28.8 1.7 %shard_map.133 = (bf16[256,768]{1,0:T(8,128)(2,1)S(1)}, bf16[256,768]{1,0:T(8,128)(2,1)S(1)}, f32[192,768]{1,0:T(8,128)S(1)}, f32[192,768]{1,0:T(8,128)S(1)}) custom-call(bf16[768,256]{1,0:T(8,128)(2,1)S(1)} %get-tuple-element.98.turned_high, bf16[768,256]{1,0:T(8,128)(2,1)S(1)} %get-tuple-element.99.turned_low, f32[256,512]{1,0:T(8,128)S(1)} %get-tuple-element.116.scores, ...), custom_call_target="tpu_custom_call" | custom-call | flops 452984832 | bytes 2883584 | tf_op jit(solution)/shard_map/pallas_call | solution.py:198
  30.4 1.8 %collective-permute-start.17 = (f32[192,768]{1,0:T(8,128)S(1)}, f32[192,768]{1,0:T(8,128)S(1)}, u32[]{:S(2)}, u32[]{:S(2)}) collective-permute-start(f32[192,768]{1,0:T(8,128)S(1)} %get-tuple-element.134), channel_id=1, source_target_pairs={{0,1},{1,0},{2,3},{3,2},{4,5},{5,4},{6,7},{7,6},{8,9},{9,8},{10,11... | collective-permute-start | bytes 1769480 | tf_op jit(solution)/shard_map/ppermute | solution.py:211
  33.0 0.9 collective-permute-done.17.b
  34.0 0.7 collective-permute-start.22
  34.7 1.4 %collective-permute-start.19 = (f32[48,768]{1,0:T(8,128)S(1)}, f32[48,768]{1,0:T(8,128)S(1)}, u32[]{:S(2)}, u32[]{:S(2)}) collective-permute-start(f32[48,768]{1,0:T(8,128)S(1)} %get-tuple-element.136), channel_id=1, source_target_pairs={{0,2},{1,3},{2,0},{3,1},{4,6},{5,7},{6,4},{7,5},{8,10},{9,11},{10,... | collective-permute-start | bytes 442376 | tf_op jit(solution)/shard_map/ppermute | solution.py:211
  36.7 17.9 %collective-permute-done.22.c = f32[48,768]{1,0:T(8,128)S(1)} collective-permute-done((f32[48,768]{1,0:T(8,128)S(1)}, f32[48,768]{1,0:T(8,128)S(1)}, u32[]{:S(2)}, u32[]{:S(2)}) %collective-permute-start.22) | collective-permute-done | bytes 147488 | tf_op jit(solution)/shard_map/ppermute | solution.py:211
  54.8 3.0 %collective-permute-done.19.c = f32[48,768]{1,0:T(8,128)S(1)} collective-permute-done((f32[48,768]{1,0:T(8,128)S(1)}, f32[48,768]{1,0:T(8,128)S(1)}, u32[]{:S(2)}, u32[]{:S(2)}) %collective-permute-start.19) | collective-permute-done | bytes 147488 | tf_op jit(solution)/shard_map/ppermute | solution.py:211
  57.9 3.0 %collective-permute-done.21.c = f32[48,768]{1,0:T(8,128)S(1)} collective-permute-done((f32[48,768]{1,0:T(8,128)S(1)}, f32[48,768]{1,0:T(8,128)S(1)}, u32[]{:S(2)}, u32[]{:S(2)}) %collective-permute-start.21) | collective-permute-done | bytes 147488 | tf_op jit(solution)/shard_map/ppermute | solution.py:211
  61.0 1.5 %collective-permute-start.24 = (f32[48,768]{1,0:T(8,128)S(1)}, f32[48,768]{1,0:T(8,128)S(1)}, u32[]{:S(2)}, u32[]{:S(2)}) collective-permute-start(f32[48,768]{1,0:T(8,128)S(1)} %shard_map.142), channel_id=1, source_target_pairs={{0,8},{1,9},{2,10},{3,11},{4,12},{5,13},{6,14},{7,15},{8,0},{9,1},... | collective-permute-start | bytes 442376 | tf_op jit(solution)/shard_map/ppermute | solution.py:211
  62.5 1.5 %collective-permute-done.18.c = f32[48,768]{1,0:T(8,128)S(1)} collective-permute-done((f32[48,768]{1,0:T(8,128)S(1)}, f32[48,768]{1,0:T(8,128)S(1)}, u32[]{:S(2)}, u32[]{:S(2)}) %collective-permute-start.18) | collective-permute-done | bytes 147488 | tf_op jit(solution)/shard_map/ppermute | solution.py:211
  64.1 6.8 %collective-permute-done.24.rest_1_ = f32[48,768]{1,0:T(8,128)S(1)} collective-permute-done((f32[48,768]{1,0:T(8,128)S(1)}, f32[48,768]{1,0:T(8,128)S(1)}, u32[]{:S(2)}, u32[]{:S(2)}) %collective-permute-start.24) | collective-permute-done | bytes 147488 | tf_op jit(solution)/shard_map/ppermute | solution.py:211
  71.1 2.9 %collective-permute-start.28 = (f32[48,768]{1,0:T(8,128)S(1)}, f32[48,768]{1,0:T(8,128)S(1)}, u32[]{:S(2)}, u32[]{:S(2)}) collective-permute-start(f32[48,768]{1,0:T(8,128)S(1)} %get-tuple-element.140.refs_0_.relation), channel_id=1, source_target_pairs={{0,4},{1,5},{2,6},{3,7},{4,0},{5,1},{6,2},{7,3},{8,12},{9,13},{10,... | collective-permute-start | bytes 442376 | tf_op jit(solution)/shard_map/ppermute | solution.py:211
  74.0 2.0 %shard_map.134 = (f32[256,768]{1,0:T(8,128)S(1)}, f32[1,256]{1,0:T(1,128)S(1)}, bf16[768,256]{1,0:T(8,128)(2,1)S(1)}, bf16[768,256]{1,0:T(8,128)(2,1)S(1)}, bf16...) custom-call(s32[1]{0:T(128)} %bitcast.me_ref, ...), custom_call_target="tpu_custom_call" | custom-call | bytes 3933188 | tf_op jit(solution)/shard_map/pallas_call | solution.py:198
  76.1 4.1 %collective-permute-done.32.refs_1_ = f32[48,768]{1,0:T(8,128)S(1)} collective-permute-done((f32[48,768]{1,0:T(8,128)S(1)}, f32[48,768]{1,0:T(8,128)S(1)}, u32[]{:S(2)}, u32[]{:S(2)}) %collective-permute-start.32) | collective-permute-done | bytes 147488 | tf_op jit(solution)/shard_map/ppermute | solution.py:211
  80.7 1.7 %collective-permute-start.34 = (f32[48,768]{1,0:T(8,128)S(1)}, f32[48,768]{1,0:T(8,128)S(1)}, u32[]{:S(2)}, u32[]{:S(2)}) collective-permute-start(f32[48,768]{1,0:T(8,128)S(1)} %collective-permute-done.32.refs_1_), channel_id=1, source_target_pairs={{0,2},{1,3},{2,0},{3,1},{4,6},{5,7},{6,4},{7,5},{8,10},{9,11},{10,... | collective-permute-start | bytes 442376 | tf_op jit(solution)/shard_map/ppermute | solution.py:211
  82.6 3.3 %collective-permute-done.36.refs_1_ = f32[48,768]{1,0:T(8,128)S(1)} collective-permute-done((f32[48,768]{1,0:T(8,128)S(1)}, f32[48,768]{1,0:T(8,128)S(1)}, u32[]{:S(2)}, u32[]{:S(2)}) %collective-permute-start.36) | collective-permute-done | bytes 147488 | tf_op jit(solution)/shard_map/ppermute | solution.py:211
  86.3 0.8 collective-permute-done.30.refs_3_
  87.6 2.6 %collective-permute-done.34.refs_3_ = f32[48,768]{1,0:T(8,128)S(1)} collective-permute-done((f32[48,768]{1,0:T(8,128)S(1)}, f32[48,768]{1,0:T(8,128)S(1)}, u32[]{:S(2)}, u32[]{:S(2)}) %collective-permute-start.34) | collective-permute-done | bytes 147488 | tf_op jit(solution)/shard_map/ppermute | solution.py:211
  91.3 0.9 collective-permute-done.38.refs_3_
  93.6 1.1 shard_map.148
  94.7 1.7 %shard_map.149 = (bf16[256,768]{1,0:T(8,128)(2,1)S(1)}, bf16[256,768]{1,0:T(8,128)(2,1)S(1)}, f32[192,768]{1,0:T(8,128)S(1)}, f32[192,768]{1,0:T(8,128)S(1)}) custom-call(bf16[768,256]{1,0:T(8,128)(2,1)S(1)} %get-tuple-element.129.turned_high, bf16[768,256]{1,0:T(8,128)(2,1)S(1)} %get-tuple-element.130.turned_low, ...), custom_call_target="tpu_custom_call" | custom-call | flops 452984832 | bytes 2883584 | tf_op jit(solution)/shard_map/pallas_call | solution.py:198
  97.6 0.9 collective-permute-done.40.b
  99.1 1.6 %collective-permute-start.43 = (f32[48,768]{1,0:T(8,128)S(1)}, f32[48,768]{1,0:T(8,128)S(1)}, u32[]{:S(2)}, u32[]{:S(2)}) collective-permute-start(f32[48,768]{1,0:T(8,128)S(1)} %get-tuple-element.185), channel_id=1, source_target_pairs={{0,2},{1,3},{2,0},{3,1},{4,6},{5,7},{6,4},{7,5},{8,10},{9,11},{10,... | collective-permute-start | bytes 442376 | tf_op jit(solution)/shard_map/ppermute | solution.py:211
  101.1 4.2 %collective-permute-done.46.c = f32[48,768]{1,0:T(8,128)S(1)} collective-permute-done((f32[48,768]{1,0:T(8,128)S(1)}, f32[48,768]{1,0:T(8,128)S(1)}, u32[]{:S(2)}, u32[]{:S(2)}) %collective-permute-start.46) | collective-permute-done | bytes 147488 | tf_op jit(solution)/shard_map/ppermute | solution.py:211
  105.4 1.8 %collective-permute-start.47 = (f32[48,768]{1,0:T(8,128)S(1)}, f32[48,768]{1,0:T(8,128)S(1)}, u32[]{:S(2)}, u32[]{:S(2)}) collective-permute-start(f32[48,768]{1,0:T(8,128)S(1)} %shard_map.158), channel_id=1, source_target_pairs={{0,4},{1,5},{2,6},{3,7},{4,0},{5,1},{6,2},{7,3},{8,12},{9,13},{10,... | collective-permute-start | bytes 442376 | tf_op jit(solution)/shard_map/ppermute | solution.py:211
  107.6 0.9 collective-permute-done.43.c
  108.6 1.8 %collective-permute-start.44 = (f32[48,768]{1,0:T(8,128)S(1)}, f32[48,768]{1,0:T(8,128)S(1)}, u32[]{:S(2)}, u32[]{:S(2)}) collective-permute-start(f32[48,768]{1,0:T(8,128)S(1)} %shard_map.155), channel_id=1, source_target_pairs={{0,4},{1,5},{2,6},{3,7},{4,0},{5,1},{6,2},{7,3},{8,12},{9,13},{10,... | collective-permute-start | bytes 442376 | tf_op jit(solution)/shard_map/ppermute | solution.py:211
  110.4 1.3 %collective-permute-done.45.c = f32[48,768]{1,0:T(8,128)S(1)} collective-permute-done((f32[48,768]{1,0:T(8,128)S(1)}, f32[48,768]{1,0:T(8,128)S(1)}, u32[]{:S(2)}, u32[]{:S(2)}) %collective-permute-start.45) | collective-permute-done | bytes 147488 | tf_op jit(solution)/shard_map/ppermute | solution.py:211
  111.8 1.6 %collective-permute-start.48 = (f32[48,768]{1,0:T(8,128)S(1)}, f32[48,768]{1,0:T(8,128)S(1)}, u32[]{:S(2)}, u32[]{:S(2)}) collective-permute-start(f32[48,768]{1,0:T(8,128)S(1)} %shard_map.159), channel_id=1, source_target_pairs={{0,8},{1,9},{2,10},{3,11},{4,12},{5,13},{6,14},{7,15},{8,0},{9,1},... | collective-permute-start | bytes 442376 | tf_op jit(solution)/shard_map/ppermute | solution.py:211
  113.3 1.0 collective-permute-done.41.c
  114.3 2.3 %shard_map.152 = (f32[256,768]{1,0:T(8,128)}, f32[1,256]{1,0:T(1,128)}) custom-call(s32[1]{0:T(128)} %bitcast.me_ref, bf16[256,768]{1,0:T(8,128)(2,1)S(1)} %get-tuple-element.164.grad_high, bf16[256,768]{1,0:T(8,128)(2,1)S(1)} %get-tuple-element.160.grad_low, bf16[192,768]{1,0:T(8,128)(2,1)S(1)} %get-tuple-element.165.rest_0_, ...), custom_call_target="tpu_custom_call" | custom-call | bytes 3933188 | tf_op jit(solution)/shard_map/pallas_call | solution.py:198
  116.6 2.3 %shard_map.153 = (f32[512,768]{1,0:T(8,128)}, f32[1,512]{1,0:T(1,128)}) custom-call(f32[256,512]{1,0:T(8,128)S(1)} %get-tuple-element.177.scores.grad_scores, bf16[256,768]{1,0:T(8,128)(2,1)S(1)} %get-tuple-element.178.product_high, bf16[256,768]{1,0:T(8,128)(2,1)S(1)} %get-tuple-element.179.product_low, f32[520,768]{1,0:T(8,128)S(1)} %collective-permute-done.15.refs_0_), custom_call_target="tpu_custom_call" | custom-call | flops 603979776 | bytes 2908160 | tf_op jit(solution)/shard_map/pallas_call | solution.py:198
  118.9 1.7 %collective-permute-done.48.rest_1_ = f32[48,768]{1,0:T(8,128)S(1)} collective-permute-done((f32[48,768]{1,0:T(8,128)S(1)}, f32[48,768]{1,0:T(8,128)S(1)}, u32[]{:S(2)}, u32[]{:S(2)}) %collective-permute-start.48) | collective-permute-done | bytes 147488 | tf_op jit(solution)/shard_map/ppermute | solution.py:211
  120.6 0.8 shard_map.160
  (104 shorter events, 13.9 us)
Async XLA Ops:
  0.6 11.4 %collective-permute-start.7 = (f32[48,768]{1,0:T(8,128)}, f32[48,768]{1,0:T(8,128)S(1)}, u32[]{:S(2)}, u32[]{:S(2)}) collective-permute-start(f32[48,768]{1,0:T(8,128)} %relation.1), channel_id=1, source_target_pairs={{0,8},{1,9},{2,10},{3,11},{4,12},{5,13},{6,14},{7,15},{8,0},{9,1},... | collective-permute-start | bytes 442376 | tf_op jit(solution)/shard_map/ppermute | solution.py:211
  4.7 8.0 %collective-permute-start.3 = (f32[48,768]{1,0:T(8,128)}, f32[48,768]{1,0:T(8,128)S(1)}, u32[]{:S(2)}, u32[]{:S(2)}) collective-permute-start(f32[48,768]{1,0:T(8,128)} %relation.1), channel_id=1, source_target_pairs={{0,4},{1,5},{2,6},{3,7},{4,0},{5,1},{6,2},{7,3},{8,12},{9,13},{10,... | collective-permute-start | bytes 442376 | tf_op jit(solution)/shard_map/ppermute | solution.py:211
  6.3 8.0 %collective-permute-start.1 = (f32[48,768]{1,0:T(8,128)}, f32[48,768]{1,0:T(8,128)S(1)}, u32[]{:S(2)}, u32[]{:S(2)}) collective-permute-start(f32[48,768]{1,0:T(8,128)} %relation.1), channel_id=1, source_target_pairs={{0,2},{1,3},{2,0},{3,1},{4,6},{5,7},{6,4},{7,5},{8,10},{9,11},{10,... | collective-permute-start | bytes 442376 | tf_op jit(solution)/shard_map/ppermute | solution.py:211
  7.8 7.0 %collective-permute-start = (f32[48,768]{1,0:T(8,128)}, f32[48,768]{1,0:T(8,128)S(1)}, u32[]{:S(2)}, u32[]{:S(2)}) collective-permute-start(f32[48,768]{1,0:T(8,128)} %relation.1), channel_id=1, source_target_pairs={{0,1},{1,0},{2,3},{3,2},{4,5},{5,4},{6,7},{7,6},{8,9},{9,8},{10,11... | collective-permute-start | bytes 442376 | tf_op jit(solution)/shard_map/ppermute | solution.py:211
  12.1 5.1 %collective-permute-start.11 = (f32[48,768]{1,0:T(8,128)S(1)}, f32[48,768]{1,0:T(8,128)S(1)}, u32[]{:S(2)}, u32[]{:S(2)}) collective-permute-start(f32[48,768]{1,0:T(8,128)S(1)} %collective-permute-done.7.refs_1_), channel_id=1, source_target_pairs={{0,4},{1,5},{2,6},{3,7},{4,0},{5,1},{6,2},{7,3},{8,12},{9,13},{10,... | collective-permute-start | bytes 442376 | tf_op jit(solution)/shard_map/ppermute | solution.py:211
  12.8 6.3 %collective-permute-start.5 = (f32[48,768]{1,0:T(8,128)S(1)}, f32[48,768]{1,0:T(8,128)S(1)}, u32[]{:S(2)}, u32[]{:S(2)}) collective-permute-start(f32[48,768]{1,0:T(8,128)S(1)} %collective-permute-done.3.refs_1_), channel_id=1, source_target_pairs={{0,2},{1,3},{2,0},{3,1},{4,6},{5,7},{6,4},{7,5},{8,10},{9,11},{10,... | collective-permute-start | bytes 442376 | tf_op jit(solution)/shard_map/ppermute | solution.py:211
  14.3 8.5 %collective-permute-start.2 = (f32[48,768]{1,0:T(8,128)S(1)}, f32[48,768]{1,0:T(8,128)S(1)}, u32[]{:S(2)}, u32[]{:S(2)}) collective-permute-start(f32[48,768]{1,0:T(8,128)S(1)} %collective-permute-done.1.refs_2_), channel_id=1, source_target_pairs={{0,1},{1,0},{2,3},{3,2},{4,5},{5,4},{6,7},{7,6},{8,9},{9,8},{10,11... | collective-permute-start | bytes 442376 | tf_op jit(solution)/shard_map/ppermute | solution.py:211
  14.3 9.1 %collective-permute-start.9 = (f32[48,768]{1,0:T(8,128)S(1)}, f32[48,768]{1,0:T(8,128)S(1)}, u32[]{:S(2)}, u32[]{:S(2)}) collective-permute-start(f32[48,768]{1,0:T(8,128)S(1)} %collective-permute-done.7.refs_1_), channel_id=1, source_target_pairs={{0,2},{1,3},{2,0},{3,1},{4,6},{5,7},{6,4},{7,5},{8,10},{9,11},{10,... | collective-permute-start | bytes 442376 | tf_op jit(solution)/shard_map/ppermute | solution.py:211
  14.8 9.2 %collective-permute-start.4 = (f32[48,768]{1,0:T(8,128)S(1)}, f32[48,768]{1,0:T(8,128)S(1)}, u32[]{:S(2)}, u32[]{:S(2)}) collective-permute-start(f32[48,768]{1,0:T(8,128)S(1)} %collective-permute-done.3.refs_1_), channel_id=1, source_target_pairs={{0,1},{1,0},{2,3},{3,2},{4,5},{5,4},{6,7},{7,6},{8,9},{9,8},{10,11... | collective-permute-start | bytes 442376 | tf_op jit(solution)/shard_map/ppermute | solution.py:211
  17.2 7.4 %collective-permute-start.13 = (f32[48,768]{1,0:T(8,128)S(1)}, f32[48,768]{1,0:T(8,128)S(1)}, u32[]{:S(2)}, u32[]{:S(2)}) collective-permute-start(f32[48,768]{1,0:T(8,128)S(1)} %collective-permute-done.11.refs_1_), channel_id=1, source_target_pairs={{0,2},{1,3},{2,0},{3,1},{4,6},{5,7},{6,4},{7,5},{8,10},{9,11},{10,... | collective-permute-start | bytes 442376 | tf_op jit(solution)/shard_map/ppermute | solution.py:211
  19.1 5.5 %collective-permute-start.6 = (f32[48,768]{1,0:T(8,128)S(1)}, f32[48,768]{1,0:T(8,128)S(1)}, u32[]{:S(2)}, u32[]{:S(2)}) collective-permute-start(f32[48,768]{1,0:T(8,128)S(1)} %collective-permute-done.5.refs_3_), channel_id=1, source_target_pairs={{0,1},{1,0},{2,3},{3,2},{4,5},{5,4},{6,7},{7,6},{8,9},{9,8},{10,11... | collective-permute-start | bytes 442376 | tf_op jit(solution)/shard_map/ppermute | solution.py:211
  22.8 2.3 %collective-permute-start.8 = (f32[48,768]{1,0:T(8,128)S(1)}, f32[48,768]{1,0:T(8,128)S(1)}, u32[]{:S(2)}, u32[]{:S(2)}) collective-permute-start(f32[48,768]{1,0:T(8,128)S(1)} %collective-permute-done.7.refs_1_), channel_id=1, source_target_pairs={{0,1},{1,0},{2,3},{3,2},{4,5},{5,4},{6,7},{7,6},{8,9},{9,8},{10,11... | collective-permute-start | bytes 442376 | tf_op jit(solution)/shard_map/ppermute | solution.py:211
  23.4 1.7 %collective-permute-start.10 = (f32[48,768]{1,0:T(8,128)S(1)}, f32[48,768]{1,0:T(8,128)S(1)}, u32[]{:S(2)}, u32[]{:S(2)}) collective-permute-start(f32[48,768]{1,0:T(8,128)S(1)} %collective-permute-done.9.refs_3_), channel_id=1, source_target_pairs={{0,1},{1,0},{2,3},{3,2},{4,5},{5,4},{6,7},{7,6},{8,9},{9,8},{10,11... | collective-permute-start | bytes 442376 | tf_op jit(solution)/shard_map/ppermute | solution.py:211
  24.0 1.6 %collective-permute-start.12 = (f32[48,768]{1,0:T(8,128)S(1)}, f32[48,768]{1,0:T(8,128)S(1)}, u32[]{:S(2)}, u32[]{:S(2)}) collective-permute-start(f32[48,768]{1,0:T(8,128)S(1)} %collective-permute-done.11.refs_1_), channel_id=1, source_target_pairs={{0,1},{1,0},{2,3},{3,2},{4,5},{5,4},{6,7},{7,6},{8,9},{9,8},{10,11... | collective-permute-start | bytes 442376 | tf_op jit(solution)/shard_map/ppermute | solution.py:211
  24.6 1.4 %collective-permute-start.14 = (f32[48,768]{1,0:T(8,128)S(1)}, f32[48,768]{1,0:T(8,128)S(1)}, u32[]{:S(2)}, u32[]{:S(2)}) collective-permute-start(f32[48,768]{1,0:T(8,128)S(1)} %collective-permute-done.13.refs_3_), channel_id=1, source_target_pairs={{0,1},{1,0},{2,3},{3,2},{4,5},{5,4},{6,7},{7,6},{8,9},{9,8},{10,11... | collective-permute-start | bytes 442376 | tf_op jit(solution)/shard_map/ppermute | solution.py:211
  28.3 45.6 %collective-permute-start.15 = (f32[520,768]{1,0:T(8,128)S(1)}, f32[520,768]{1,0:T(8,128)S(1)}, u32[]{:S(2)}, u32[]{:S(2)}) collective-permute-start(f32[520,768]{1,0:T(8,128)S(1)} %get-tuple-element.118), channel_id=1, source_target_pairs={{0,1},{1,2},{2,3},{3,4},{4,5},{5,6},{6,7},{7,8},{8,9},{9,10},{10,1... | collective-permute-start | bytes 4792328 | tf_op jit(solution)/shard_map/ppermute | solution.py:337
  30.4 3.5 %collective-permute-start.17 = (f32[192,768]{1,0:T(8,128)S(1)}, f32[192,768]{1,0:T(8,128)S(1)}, u32[]{:S(2)}, u32[]{:S(2)}) collective-permute-start(f32[192,768]{1,0:T(8,128)S(1)} %get-tuple-element.134), channel_id=1, source_target_pairs={{0,1},{1,0},{2,3},{3,2},{4,5},{5,4},{6,7},{7,6},{8,9},{9,8},{10,11... | collective-permute-start | bytes 1769480 | tf_op jit(solution)/shard_map/ppermute | solution.py:211
  32.3 4.4 %collective-permute-start.16 = (f32[192,768]{1,0:T(8,128)S(1)}, f32[192,768]{1,0:T(8,128)S(1)}, u32[]{:S(2)}, u32[]{:S(2)}) collective-permute-start(f32[192,768]{1,0:T(8,128)S(1)} %get-tuple-element.132), channel_id=1, source_target_pairs={{0,1},{1,0},{2,3},{3,2},{4,5},{5,4},{6,7},{7,6},{8,9},{9,8},{10,11... | collective-permute-start | bytes 1769480 | tf_op jit(solution)/shard_map/ppermute | solution.py:211
  34.0 20.6 %collective-permute-start.22 = (f32[48,768]{1,0:T(8,128)S(1)}, f32[48,768]{1,0:T(8,128)S(1)}, u32[]{:S(2)}, u32[]{:S(2)}) collective-permute-start(f32[48,768]{1,0:T(8,128)S(1)} %get-tuple-element.138), channel_id=1, source_target_pairs={{0,2},{1,3},{2,0},{3,1},{4,6},{5,7},{6,4},{7,5},{8,10},{9,11},{10,... | collective-permute-start | bytes 442376 | tf_op jit(solution)/shard_map/ppermute | solution.py:211
  34.7 23.1 %collective-permute-start.19 = (f32[48,768]{1,0:T(8,128)S(1)}, f32[48,768]{1,0:T(8,128)S(1)}, u32[]{:S(2)}, u32[]{:S(2)}) collective-permute-start(f32[48,768]{1,0:T(8,128)S(1)} %get-tuple-element.136), channel_id=1, source_target_pairs={{0,2},{1,3},{2,0},{3,1},{4,6},{5,7},{6,4},{7,5},{8,10},{9,11},{10,... | collective-permute-start | bytes 442376 | tf_op jit(solution)/shard_map/ppermute | solution.py:211
  36.1 24.8 %collective-permute-start.21 = (f32[48,768]{1,0:T(8,128)S(1)}, f32[48,768]{1,0:T(8,128)S(1)}, u32[]{:S(2)}, u32[]{:S(2)}) collective-permute-start(f32[48,768]{1,0:T(8,128)S(1)} %get-tuple-element.137), channel_id=1, source_target_pairs={{0,2},{1,3},{2,0},{3,1},{4,6},{5,7},{6,4},{7,5},{8,10},{9,11},{10,... | collective-permute-start | bytes 442376 | tf_op jit(solution)/shard_map/ppermute | solution.py:211
  54.6 6.3 %collective-permute-start.23 = (f32[48,768]{1,0:T(8,128)S(1)}, f32[48,768]{1,0:T(8,128)S(1)}, u32[]{:S(2)}, u32[]{:S(2)}) collective-permute-start(f32[48,768]{1,0:T(8,128)S(1)} %shard_map.141), channel_id=1, source_target_pairs={{0,4},{1,5},{2,6},{3,7},{4,0},{5,1},{6,2},{7,3},{8,12},{9,13},{10,... | collective-permute-start | bytes 442376 | tf_op jit(solution)/shard_map/ppermute | solution.py:211
  54.7 9.3 %collective-permute-start.18 = (f32[48,768]{1,0:T(8,128)S(1)}, f32[48,768]{1,0:T(8,128)S(1)}, u32[]{:S(2)}, u32[]{:S(2)}) collective-permute-start(f32[48,768]{1,0:T(8,128)S(1)} %get-tuple-element.135), channel_id=1, source_target_pairs={{0,2},{1,3},{2,0},{3,1},{4,6},{5,7},{6,4},{7,5},{8,10},{9,11},{10,... | collective-permute-start | bytes 442376 | tf_op jit(solution)/shard_map/ppermute | solution.py:211
  57.8 6.3 %collective-permute-start.20 = (f32[48,768]{1,0:T(8,128)S(1)}, f32[48,768]{1,0:T(8,128)S(1)}, u32[]{:S(2)}, u32[]{:S(2)}) collective-permute-start(f32[48,768]{1,0:T(8,128)S(1)} %shard_map.138), channel_id=1, source_target_pairs={{0,4},{1,5},{2,6},{3,7},{4,0},{5,1},{6,2},{7,3},{8,12},{9,13},{10,... | collective-permute-start | bytes 442376 | tf_op jit(solution)/shard_map/ppermute | solution.py:211
  61.0 9.9 %collective-permute-start.24 = (f32[48,768]{1,0:T(8,128)S(1)}, f32[48,768]{1,0:T(8,128)S(1)}, u32[]{:S(2)}, u32[]{:S(2)}) collective-permute-start(f32[48,768]{1,0:T(8,128)S(1)} %shard_map.142), channel_id=1, source_target_pairs={{0,8},{1,9},{2,10},{3,11},{4,12},{5,13},{6,14},{7,15},{8,0},{9,1},... | collective-permute-start | bytes 442376 | tf_op jit(solution)/shard_map/ppermute | solution.py:211
  71.0 9.2 %collective-permute-start.32 = (f32[48,768]{1,0:T(8,128)S(1)}, f32[48,768]{1,0:T(8,128)S(1)}, u32[]{:S(2)}, u32[]{:S(2)}) collective-permute-start(f32[48,768]{1,0:T(8,128)S(1)} %get-tuple-element.140.refs_0_.relation), channel_id=1, source_target_pairs={{0,8},{1,9},{2,10},{3,11},{4,12},{5,13},{6,14},{7,15},{8,0},{9,1},... | collective-permute-start | bytes 442376 | tf_op jit(solution)/shard_map/ppermute | solution.py:211
  71.1 9.2 %collective-permute-start.28 = (f32[48,768]{1,0:T(8,128)S(1)}, f32[48,768]{1,0:T(8,128)S(1)}, u32[]{:S(2)}, u32[]{:S(2)}) collective-permute-start(f32[48,768]{1,0:T(8,128)S(1)} %get-tuple-element.140.refs_0_.relation), channel_id=1, source_target_pairs={{0,4},{1,5},{2,6},{3,7},{4,0},{5,1},{6,2},{7,3},{8,12},{9,13},{10,... | collective-permute-start | bytes 442376 | tf_op jit(solution)/shard_map/ppermute | solution.py:211
  74.0 6.7 %collective-permute-start.26 = (f32[48,768]{1,0:T(8,128)S(1)}, f32[48,768]{1,0:T(8,128)S(1)}, u32[]{:S(2)}, u32[]{:S(2)}) collective-permute-start(f32[48,768]{1,0:T(8,128)S(1)} %get-tuple-element.140.refs_0_.relation), channel_id=1, source_target_pairs={{0,2},{1,3},{2,0},{3,1},{4,6},{5,7},{6,4},{7,5},{8,10},{9,11},{10,... | collective-permute-start | bytes 442376 | tf_op jit(solution)/shard_map/ppermute | solution.py:211
  74.0 8.4 %collective-permute-start.25 = (f32[48,768]{1,0:T(8,128)S(1)}, f32[48,768]{1,0:T(8,128)S(1)}, u32[]{:S(2)}, u32[]{:S(2)}) collective-permute-start(f32[48,768]{1,0:T(8,128)S(1)} %get-tuple-element.140.refs_0_.relation), channel_id=1, source_target_pairs={{0,1},{1,0},{2,3},{3,2},{4,5},{5,4},{6,7},{7,6},{8,9},{9,8},{10,11... | collective-permute-start | bytes 442376 | tf_op jit(solution)/shard_map/ppermute | solution.py:211
  80.2 5.7 %collective-permute-start.36 = (f32[48,768]{1,0:T(8,128)S(1)}, f32[48,768]{1,0:T(8,128)S(1)}, u32[]{:S(2)}, u32[]{:S(2)}) collective-permute-start(f32[48,768]{1,0:T(8,128)S(1)} %collective-permute-done.32.refs_1_), channel_id=1, source_target_pairs={{0,4},{1,5},{2,6},{3,7},{4,0},{5,1},{6,2},{7,3},{8,12},{9,13},{10,... | collective-permute-start | bytes 442376 | tf_op jit(solution)/shard_map/ppermute | solution.py:211
  80.3 6.7 %collective-permute-start.30 = (f32[48,768]{1,0:T(8,128)S(1)}, f32[48,768]{1,0:T(8,128)S(1)}, u32[]{:S(2)}, u32[]{:S(2)}) collective-permute-start(f32[48,768]{1,0:T(8,128)S(1)} %collective-permute-done.28.refs_1_), channel_id=1, source_target_pairs={{0,2},{1,3},{2,0},{3,1},{4,6},{5,7},{6,4},{7,5},{8,10},{9,11},{10,... | collective-permute-start | bytes 442376 | tf_op jit(solution)/shard_map/ppermute | solution.py:211
  80.7 6.4 %collective-permute-start.27 = (f32[48,768]{1,0:T(8,128)S(1)}, f32[48,768]{1,0:T(8,128)S(1)}, u32[]{:S(2)}, u32[]{:S(2)}) collective-permute-start(f32[48,768]{1,0:T(8,128)S(1)} %collective-permute-done.26.refs_2_), channel_id=1, source_target_pairs={{0,1},{1,0},{2,3},{3,2},{4,5},{5,4},{6,7},{7,6},{8,9},{9,8},{10,11... | collective-permute-start | bytes 442376 | tf_op jit(solution)/shard_map/ppermute | solution.py:211
  80.7 9.6 %collective-permute-start.34 = (f32[48,768]{1,0:T(8,128)S(1)}, f32[48,768]{1,0:T(8,128)S(1)}, u32[]{:S(2)}, u32[]{:S(2)}) collective-permute-start(f32[48,768]{1,0:T(8,128)S(1)} %collective-permute-done.32.refs_1_), channel_id=1, source_target_pairs={{0,2},{1,3},{2,0},{3,1},{4,6},{5,7},{6,4},{7,5},{8,10},{9,11},{10,... | collective-permute-start | bytes 442376 | tf_op jit(solution)/shard_map/ppermute | solution.py:211
  82.4 8.4 %collective-permute-start.29 = (f32[48,768]{1,0:T(8,128)S(1)}, f32[48,768]{1,0:T(8,128)S(1)}, u32[]{:S(2)}, u32[]{:S(2)}) collective-permute-start(f32[48,768]{1,0:T(8,128)S(1)} %collective-permute-done.28.refs_1_), channel_id=1, source_target_pairs={{0,1},{1,0},{2,3},{3,2},{4,5},{5,4},{6,7},{7,6},{8,9},{9,8},{10,11... | collective-permute-start | bytes 442376 | tf_op jit(solution)/shard_map/ppermute | solution.py:211
  85.9 6.3 %collective-permute-start.38 = (f32[48,768]{1,0:T(8,128)S(1)}, f32[48,768]{1,0:T(8,128)S(1)}, u32[]{:S(2)}, u32[]{:S(2)}) collective-permute-start(f32[48,768]{1,0:T(8,128)S(1)} %collective-permute-done.36.refs_1_), channel_id=1, source_target_pairs={{0,2},{1,3},{2,0},{3,1},{4,6},{5,7},{6,4},{7,5},{8,10},{9,11},{10,... | collective-permute-start | bytes 442376 | tf_op jit(solution)/shard_map/ppermute | solution.py:211
  87.1 5.4 %collective-permute-start.31 = (f32[48,768]{1,0:T(8,128)S(1)}, f32[48,768]{1,0:T(8,128)S(1)}, u32[]{:S(2)}, u32[]{:S(2)}) collective-permute-start(f32[48,768]{1,0:T(8,128)S(1)} %collective-permute-done.30.refs_3_), channel_id=1, source_target_pairs={{0,1},{1,0},{2,3},{3,2},{4,5},{5,4},{6,7},{7,6},{8,9},{9,8},{10,11... | collective-permute-start | bytes 442376 | tf_op jit(solution)/shard_map/ppermute | solution.py:211
  87.1 5.9 %collective-permute-start.33 = (f32[48,768]{1,0:T(8,128)S(1)}, f32[48,768]{1,0:T(8,128)S(1)}, u32[]{:S(2)}, u32[]{:S(2)}) collective-permute-start(f32[48,768]{1,0:T(8,128)S(1)} %collective-permute-done.32.refs_1_), channel_id=1, source_target_pairs={{0,1},{1,0},{2,3},{3,2},{4,5},{5,4},{6,7},{7,6},{8,9},{9,8},{10,11... | collective-permute-start | bytes 442376 | tf_op jit(solution)/shard_map/ppermute | solution.py:211
  90.2 2.8 %collective-permute-start.35 = (f32[48,768]{1,0:T(8,128)S(1)}, f32[48,768]{1,0:T(8,128)S(1)}, u32[]{:S(2)}, u32[]{:S(2)}) collective-permute-start(f32[48,768]{1,0:T(8,128)S(1)} %collective-permute-done.34.refs_3_), channel_id=1, source_target_pairs={{0,1},{1,0},{2,3},{3,2},{4,5},{5,4},{6,7},{7,6},{8,9},{9,8},{10,11... | collective-permute-start | bytes 442376 | tf_op jit(solution)/shard_map/ppermute | solution.py:211
  90.7 2.8 %collective-permute-start.37 = (f32[48,768]{1,0:T(8,128)S(1)}, f32[48,768]{1,0:T(8,128)S(1)}, u32[]{:S(2)}, u32[]{:S(2)}) collective-permute-start(f32[48,768]{1,0:T(8,128)S(1)} %collective-permute-done.36.refs_1_), channel_id=1, source_target_pairs={{0,1},{1,0},{2,3},{3,2},{4,5},{5,4},{6,7},{7,6},{8,9},{9,8},{10,11... | collective-permute-start | bytes 442376 | tf_op jit(solution)/shard_map/ppermute | solution.py:211
  96.4 2.1 %collective-permute-start.40 = (f32[192,768]{1,0:T(8,128)S(1)}, f32[192,768]{1,0:T(8,128)S(1)}, u32[]{:S(2)}, u32[]{:S(2)}) collective-permute-start(f32[192,768]{1,0:T(8,128)S(1)} %get-tuple-element.162), channel_id=1, source_target_pairs={{0,1},{1,0},{2,3},{3,2},{4,5},{5,4},{6,7},{7,6},{8,9},{9,8},{10,11... | collective-permute-start | bytes 1769480 | tf_op jit(solution)/shard_map/ppermute | solution.py:211
  96.9 4.2 %collective-permute-start.42 = (f32[192,768]{1,0:T(8,128)S(1)}, f32[192,768]{1,0:T(8,128)S(1)}, u32[]{:S(2)}, u32[]{:S(2)}) collective-permute-start(f32[192,768]{1,0:T(8,128)S(1)} %get-tuple-element.184), channel_id=1, source_target_pairs={{0,1},{1,0},{2,3},{3,2},{4,5},{5,4},{6,7},{7,6},{8,9},{9,8},{10,11... | collective-permute-start | bytes 1769480 | tf_op jit(solution)/shard_map/ppermute | solution.py:211
  98.6 6.7 %collective-permute-start.46 = (f32[48,768]{1,0:T(8,128)S(1)}, f32[48,768]{1,0:T(8,128)S(1)}, u32[]{:S(2)}, u32[]{:S(2)}) collective-permute-start(f32[48,768]{1,0:T(8,128)S(1)} %get-tuple-element.187), channel_id=1, source_target_pairs={{0,2},{1,3},{2,0},{3,1},{4,6},{5,7},{6,4},{7,5},{8,10},{9,11},{10,... | collective-permute-start | bytes 442376 | tf_op jit(solution)/shard_map/ppermute | solution.py:211
  99.1 9.4 %collective-permute-start.43 = (f32[48,768]{1,0:T(8,128)S(1)}, f32[48,768]{1,0:T(8,128)S(1)}, u32[]{:S(2)}, u32[]{:S(2)}) collective-permute-start(f32[48,768]{1,0:T(8,128)S(1)} %get-tuple-element.185), channel_id=1, source_target_pairs={{0,2},{1,3},{2,0},{3,1},{4,6},{5,7},{6,4},{7,5},{8,10},{9,11},{10,... | collective-permute-start | bytes 442376 | tf_op jit(solution)/shard_map/ppermute | solution.py:211
  100.7 11.0 %collective-permute-start.45 = (f32[48,768]{1,0:T(8,128)S(1)}, f32[48,768]{1,0:T(8,128)S(1)}, u32[]{:S(2)}, u32[]{:S(2)}) collective-permute-start(f32[48,768]{1,0:T(8,128)S(1)} %get-tuple-element.186), channel_id=1, source_target_pairs={{0,2},{1,3},{2,0},{3,1},{4,6},{5,7},{6,4},{7,5},{8,10},{9,11},{10,... | collective-permute-start | bytes 442376 | tf_op jit(solution)/shard_map/ppermute | solution.py:211
  105.4 6.3 %collective-permute-start.47 = (f32[48,768]{1,0:T(8,128)S(1)}, f32[48,768]{1,0:T(8,128)S(1)}, u32[]{:S(2)}, u32[]{:S(2)}) collective-permute-start(f32[48,768]{1,0:T(8,128)S(1)} %shard_map.158), channel_id=1, source_target_pairs={{0,4},{1,5},{2,6},{3,7},{4,0},{5,1},{6,2},{7,3},{8,12},{9,13},{10,... | collective-permute-start | bytes 442376 | tf_op jit(solution)/shard_map/ppermute | solution.py:211
  107.2 7.1 %collective-permute-start.41 = (f32[48,768]{1,0:T(8,128)S(1)}, f32[48,768]{1,0:T(8,128)S(1)}, u32[]{:S(2)}, u32[]{:S(2)}) collective-permute-start(f32[48,768]{1,0:T(8,128)S(1)} %get-tuple-element.163), channel_id=1, source_target_pairs={{0,2},{1,3},{2,0},{3,1},{4,6},{5,7},{6,4},{7,5},{8,10},{9,11},{10,... | collective-permute-start | bytes 442376 | tf_op jit(solution)/shard_map/ppermute | solution.py:211
  108.6 10.3 %collective-permute-start.44 = (f32[48,768]{1,0:T(8,128)S(1)}, f32[48,768]{1,0:T(8,128)S(1)}, u32[]{:S(2)}, u32[]{:S(2)}) collective-permute-start(f32[48,768]{1,0:T(8,128)S(1)} %shard_map.155), channel_id=1, source_target_pairs={{0,4},{1,5},{2,6},{3,7},{4,0},{5,1},{6,2},{7,3},{8,12},{9,13},{10,... | collective-permute-start | bytes 442376 | tf_op jit(solution)/shard_map/ppermute | solution.py:211
  111.8 8.9 %collective-permute-start.48 = (f32[48,768]{1,0:T(8,128)S(1)}, f32[48,768]{1,0:T(8,128)S(1)}, u32[]{:S(2)}, u32[]{:S(2)}) collective-permute-start(f32[48,768]{1,0:T(8,128)S(1)} %shard_map.159), channel_id=1, source_target_pairs={{0,8},{1,9},{2,10},{3,11},{4,12},{5,13},{6,14},{7,15},{8,0},{9,1},... | collective-permute-start | bytes 442376 | tf_op jit(solution)/shard_map/ppermute | solution.py:211
  (11 other events, 63.0 us)

commit v5 on v4

--- a/solution.py
+++ b/solution.py
@@ -22,10 +22,10 @@
 
 
 def dot3(a, b, dims):
-    def one(p, q):
-        return lax.dot_general(p, q, dims, preferred_element_type=F32)
-
-    return one(a[0], b[0]) + (one(a[0], b[1]) + one(a[1], b[0]))
+    (((i,), (j,)), _) = dims
+    left = jnp.concatenate([a[1], a[0], a[0]], axis=i)
+    right = jnp.concatenate([b[0], b[1], b[0]], axis=j)
+    return lax.dot_general(left, right, dims, preferred_element_type=F32)
 
 
 def diagonal(n):
@@ -139,6 +139,13 @@
         piece[...] = dot3((high, low), grad, NN)
 
 
+def scores_and_grads_kernel(bucket, first, count, picks, *refs):
+    held = count + (not first)
+    inputs, (turned_high, turned_low), outs = refs[: held + 5], refs[held + 5 : held + 7], refs[held + 7 :]
+    scores_kernel(bucket, first, count, [], *inputs, *outs[:5])
+    grads_kernel(picks, turned_high, turned_low, outs[4], *inputs[held + 2 : held + 4], *outs[5:])
+
+
 def tails_kernel(rows, grad_scores, product_high, product_low, *refs):
     grad = dot3(split(grad_scores[...].T), (product_high[...], product_low[...]), NN)
     tails, outs = refs[: len(rows)], refs[len(rows) :]
@@ -215,7 +222,7 @@
     return lax.optimization_barrier((value, *others))[0]
 
 
-def gather_groups(own, early, late, crowded, use):
+def gather_groups(own, early, late, use):
     n = lax.axis_size("blk")
     far = list(range(4, n, 4))
     got = {0: own}
@@ -224,11 +231,11 @@
         for k in [k for k in (0, *far) if k in got]:
             got[k ^ step] = partner(got[k], step)
         if step == n // 2:
-            got[step] = after(got[step], *early)
+            got[2] = partner(own, 2)
+            got[step] = after(got[step], *early, *([] if late else [got[2]]))
         step //= 2
-    for k in (0, *far):
-        ready = after(got[k], got[k]) if crowded and k != far[-1] else got[k]
-        got[k ^ 2] = partner(ready, 2)
+    for k in far:
+        got[k ^ 2] = partner(got[k], 2)
     waited = late
     for k in (0, *far):
         first = after(got[k], *waited) if k == far[-1] else got[k]
@@ -272,9 +279,9 @@
     head_rows, tail_rows = heads.shape[0], tails.shape[0]
     head_state, tail_state, relation_state = (s.reshape(1, -1) for s in (head_state, tail_state, relation_state))
 
-    def gathered(rows, early, late, crowded, use):
+    def gathered(rows, early, late, use):
         if by_blocks:
-            return gather_groups(rows, early, late, crowded, use)
+            return gather_groups(rows, early, late, use)
         return use([lax.all_gather(rows, "blk", axis=0, tiled=True)], True)
 
     def scattered(pieces):
@@ -304,6 +311,7 @@
     )
     rows = [tail_rows // CHUNKS] * CHUNKS
     sent_shapes = [((r + 8 * (i == CHUNKS - 1), width), F32) for i, r in enumerate(rows)]
+    calls = ((1,), (0, 2, 3)) if by_blocks else ((0,),)
     for bucket in range(2):
         last = bucket == 1
         before, relation_half = [], []
@@ -311,6 +319,15 @@
         def use(blocks, closing):
             first, g = not before, len(relation_half) // 2
             halves, count = head_half[2 + 2 * g : 4 + 2 * g], len(blocks)
+            if closing and last:
+                out = call(
+                    functools.partial(scores_and_grads_kernel, bucket, first, count, [slots, *[picks[c] for c in calls[0]]]),
+                    [*relation_parts[g], *row_parts, table, *row_parts, *[held[c] for c in calls[0]]],
+                    [*before[-1:], *blocks, *halves, *tail_half, marks, *head_half[:2]],
+                    flops=6 * head_rows * width * (width // len(sizes) + 2 * tail_rows),
+                )
+                relation_half.extend(out[:2])
+                return out
             if closing:
                 out = call(
                     functools.partial(scores_kernel, bucket, first, count, [] if last else rows),
@@ -330,13 +347,14 @@
             before.append(out[0])
             return out[0]
 
-        out = gathered(relation, head_half, [] if bucket else [*tail_half, marks], bucket == 1, use)
+        out = gathered(relation, head_half, [] if bucket else [*tail_half, marks], use)
         product, grad_scores, sent = out[2:4], out[4], out[5:]
         if not last:
             moves = [(i, (i + 1) % n) for i in range(n)]
             arrived = [lax.ppermute(v, "blk", moves) for v in sent]
-        pieces = {}
-        for chosen in ((1, 3), (0, 2)) if by_blocks else [(0,)]:
+        pieces = dict(zip(calls[0], sent[2:])) if last else {}
+        grad_product = sent[:2]
+        for chosen in calls[len(pieces) > 0 :]:
             wanted = [slots, *[picks[c] for c in chosen]]
             shapes = [held[c] for c in chosen]
             if pieces:

time: 122 us -> 121 us (level)
    pallas_call x34 -> x33, Pallas kernels: 20.7 us -> 20.5 us  [call(): pl.pallas_call(kernel, out_shape=[jax.ShapeDtypeStruct(s, t) for s, t in...]
  transfers between devices with their start and end apart: 49 -> 49, of which waited for: 24 -> 22; matrix products, arithmetic and copies ran while one was open for 0% -> 0% of each run, Pallas kernels for 12% -> 12%
where the time goes in v5:
time: 121 us
  waiting for transfers between devices  59.5 us (49%)
  starting transfers between devices  36.2 us (30%)
  Pallas kernels  20.5 us (17%)
  local copies, waits for them, and re-layouts  3.95 us (3%)
    ppermute x48, waiting for transfers between devices, partner(): return lax.ppermute(value, 'blk', [(i, i ^ mask) for i in range(n)])  59.5 us
    ppermute x48, starting transfers between devices, partner(): return lax.ppermute(value, 'blk', [(i, i ^ mask) for i in range(n)])  35.7 us
    pallas_call x33, Pallas kernels, call(): pl.pallas_call(kernel, out_shape=[jax.ShapeDtypeStruct(s, t) for s, t in...  20.5 us
    unnamed x20, local copies, waits for them, and re-layouts  3.95 us
  transfers between devices with their start and end apart: 49, of which 22 were waited for; matrix products, arithmetic and copies ran while one was open for 0% of the time, Pallas kernels for 12%

profile of v5, /device:TPU:0, one launch (start us, length us, event | category | flops | bytes accessed | tf_op | source)
XLA Modules:
  0.0 121.1 jit_solution(895476951370399242)
XLA Ops:
  0.6 4.1 %collective-permute-start.7 = (f32[48,768]{1,0:T(8,128)}, f32[48,768]{1,0:T(8,128)S(1)}, u32[]{:S(2)}, u32[]{:S(2)}) collective-permute-start(f32[48,768]{1,0:T(8,128)} %relation.1), channel_id=1, source_target_pairs={{0,8},{1,9},{2,10},{3,11},{4,12},{5,13},{6,14},{7,15},{8,0},{9,1},... | collective-permute-start | bytes 442376 | tf_op jit(solution)/shard_map/ppermute | solution.py:218
  4.7 1.6 %collective-permute-start.3 = (f32[48,768]{1,0:T(8,128)}, f32[48,768]{1,0:T(8,128)S(1)}, u32[]{:S(2)}, u32[]{:S(2)}) collective-permute-start(f32[48,768]{1,0:T(8,128)} %relation.1), channel_id=1, source_target_pairs={{0,4},{1,5},{2,6},{3,7},{4,0},{5,1},{6,2},{7,3},{8,12},{9,13},{10,... | collective-permute-start | bytes 442376 | tf_op jit(solution)/shard_map/ppermute | solution.py:218
  6.3 1.5 %collective-permute-start.1 = (f32[48,768]{1,0:T(8,128)}, f32[48,768]{1,0:T(8,128)S(1)}, u32[]{:S(2)}, u32[]{:S(2)}) collective-permute-start(f32[48,768]{1,0:T(8,128)} %relation.1), channel_id=1, source_target_pairs={{0,2},{1,3},{2,0},{3,1},{4,6},{5,7},{6,4},{7,5},{8,10},{9,11},{10,... | collective-permute-start | bytes 442376 | tf_op jit(solution)/shard_map/ppermute | solution.py:218
  7.8 1.1 copy-done.2
  9.6 2.5 %collective-permute-done.7.refs_1_ = f32[48,768]{1,0:T(8,128)S(1)} collective-permute-done((f32[48,768]{1,0:T(8,128)}, f32[48,768]{1,0:T(8,128)S(1)}, u32[]{:S(2)}, u32[]{:S(2)}) %collective-permute-start.7) | collective-permute-done | bytes 147488 | tf_op jit(solution)/shard_map/ppermute | solution.py:218
  12.1 0.7 collective-permute-start.11
  12.8 1.5 %collective-permute-start.5 = (f32[48,768]{1,0:T(8,128)S(1)}, f32[48,768]{1,0:T(8,128)S(1)}, u32[]{:S(2)}, u32[]{:S(2)}) collective-permute-start(f32[48,768]{1,0:T(8,128)S(1)} %collective-permute-done.3.refs_1_), channel_id=1, source_target_pairs={{0,2},{1,3},{2,0},{3,1},{4,6},{5,7},{6,4},{7,5},{8,10},{9,11},{10,... | collective-permute-start | bytes 442376 | tf_op jit(solution)/shard_map/ppermute | solution.py:218
  15.0 2.2 %collective-permute-done.11.refs_1_ = f32[48,768]{1,0:T(8,128)S(1)} collective-permute-done((f32[48,768]{1,0:T(8,128)S(1)}, f32[48,768]{1,0:T(8,128)S(1)}, u32[]{:S(2)}, u32[]{:S(2)}) %collective-permute-start.11) | collective-permute-done | bytes 147488 | tf_op jit(solution)/shard_map/ppermute | solution.py:218
  17.2 1.6 %collective-permute-start.13 = (f32[48,768]{1,0:T(8,128)S(1)}, f32[48,768]{1,0:T(8,128)S(1)}, u32[]{:S(2)}, u32[]{:S(2)}) collective-permute-start(f32[48,768]{1,0:T(8,128)S(1)} %collective-permute-done.11.refs_1_), channel_id=1, source_target_pairs={{0,2},{1,3},{2,0},{3,1},{4,6},{5,7},{6,4},{7,5},{8,10},{9,11},{10,... | collective-permute-start | bytes 442376 | tf_op jit(solution)/shard_map/ppermute | solution.py:218
  19.1 1.4 %copy-done = f32[512,768]{1,0:T(8,128)S(1)} copy-done((f32[512,768]{1,0:T(8,128)S(1)}, f32[512,768]{1,0:T(8,128)}, u32[]{:S(2)}) %copy-start) | copy-done | bytes 1572888
  20.5 0.7 copy-done.5
  21.9 0.9 shard_map.131
  26.0 2.4 %shard_map.132 = (bf16[192,768]{1,0:T(8,128)(2,1)S(1)}, bf16[192,768]{1,0:T(8,128)(2,1)S(1)}, bf16[256,768]{1,0:T(8,128)(2,1)}, bf16[256,768]{1,0:T(8,128)(2,1)}...) custom-call(f32[256,768]{1,0:T(8,128)S(1)} %get-tuple-element.108.refs_0_, ...), custom_call_target="tpu_custom_call" | custom-call | flops 1434451968 | bytes 5769216 | tf_op jit(solution)/shard_map/pallas_call | solution.py:205
  28.9 1.3 %shard_map.133 = (bf16[256,768]{1,0:T(8,128)(2,1)S(1)}, bf16[256,768]{1,0:T(8,128)(2,1)S(1)}, f32[192,768]{1,0:T(8,128)S(1)}) custom-call(bf16[768,256]{1,0:T(8,128)(2,1)S(1)} %get-tuple-element.95.turned_high, bf16[768,256]{1,0:T(8,128)(2,1)S(1)} %get-tuple-element.96.turned_low, f32[256,512]{1,0:T(8,128)S(1)} %get-tuple-element.113.scores, ...), custom_call_target="tpu_custom_call" | custom-call | flops 452984832 | bytes 2883584 | tf_op jit(solution)/shard_map/pallas_call | solution.py:205
  30.1 1.8 %collective-permute-start.16 = (f32[192,768]{1,0:T(8,128)S(1)}, f32[192,768]{1,0:T(8,128)S(1)}, u32[]{:S(2)}, u32[]{:S(2)}) collective-permute-start(f32[192,768]{1,0:T(8,128)S(1)} %get-tuple-element.119), channel_id=1, source_target_pairs={{0,1},{1,0},{2,3},{3,2},{4,5},{5,4},{6,7},{7,6},{8,9},{9,8},{10,11... | collective-permute-start | bytes 1769480 | tf_op jit(solution)/shard_map/ppermute | solution.py:218
  31.9 0.9 shard_map.134
  33.6 1.2 collective-permute-start.21
  34.8 0.9 collective-permute-start.18
  35.7 1.1 collective-permute-start.20
  36.8 17.8 %collective-permute-done.21.c = f32[48,768]{1,0:T(8,128)S(1)} collective-permute-done((f32[48,768]{1,0:T(8,128)S(1)}, f32[48,768]{1,0:T(8,128)S(1)}, u32[]{:S(2)}, u32[]{:S(2)}) %collective-permute-start.21) | collective-permute-done | bytes 147488 | tf_op jit(solution)/shard_map/ppermute | solution.py:218
  54.8 3.0 %collective-permute-done.18.c = f32[48,768]{1,0:T(8,128)S(1)} collective-permute-done((f32[48,768]{1,0:T(8,128)S(1)}, f32[48,768]{1,0:T(8,128)S(1)}, u32[]{:S(2)}, u32[]{:S(2)}) %collective-permute-start.18) | collective-permute-done | bytes 147488 | tf_op jit(solution)/shard_map/ppermute | solution.py:218
  57.9 3.0 %collective-permute-done.20.c = f32[48,768]{1,0:T(8,128)S(1)} collective-permute-done((f32[48,768]{1,0:T(8,128)S(1)}, f32[48,768]{1,0:T(8,128)S(1)}, u32[]{:S(2)}, u32[]{:S(2)}) %collective-permute-start.20) | collective-permute-done | bytes 147488 | tf_op jit(solution)/shard_map/ppermute | solution.py:218
  61.0 1.5 %collective-permute-start.23 = (f32[48,768]{1,0:T(8,128)S(1)}, f32[48,768]{1,0:T(8,128)S(1)}, u32[]{:S(2)}, u32[]{:S(2)}) collective-permute-start(f32[48,768]{1,0:T(8,128)S(1)} %shard_map.141), channel_id=1, source_target_pairs={{0,8},{1,9},{2,10},{3,11},{4,12},{5,13},{6,14},{7,15},{8,0},{9,1},... | collective-permute-start | bytes 442376 | tf_op jit(solution)/shard_map/ppermute | solution.py:218
  62.6 1.5 %collective-permute-done.17.c = f32[48,768]{1,0:T(8,128)S(1)} collective-permute-done((f32[48,768]{1,0:T(8,128)S(1)}, f32[48,768]{1,0:T(8,128)S(1)}, u32[]{:S(2)}, u32[]{:S(2)}) %collective-permute-start.17) | collective-permute-done | bytes 147488 | tf_op jit(solution)/shard_map/ppermute | solution.py:218
  64.1 6.8 %collective-permute-done.23.rest_1_ = f32[48,768]{1,0:T(8,128)S(1)} collective-permute-done((f32[48,768]{1,0:T(8,128)S(1)}, f32[48,768]{1,0:T(8,128)S(1)}, u32[]{:S(2)}, u32[]{:S(2)}) %collective-permute-start.23) | collective-permute-done | bytes 147488 | tf_op jit(solution)/shard_map/ppermute | solution.py:218
  71.2 2.8 %collective-permute-start.28 = (f32[48,768]{1,0:T(8,128)S(1)}, f32[48,768]{1,0:T(8,128)S(1)}, u32[]{:S(2)}, u32[]{:S(2)}) collective-permute-start(f32[48,768]{1,0:T(8,128)S(1)} %get-tuple-element.124.refs_0_.relation), channel_id=1, source_target_pairs={{0,4},{1,5},{2,6},{3,7},{4,0},{5,1},{6,2},{7,3},{8,12},{9,13},{10,... | collective-permute-start | bytes 442376 | tf_op jit(solution)/shard_map/ppermute | solution.py:218
  74.1 2.1 %shard_map.143 = (f32[256,768]{1,0:T(8,128)S(1)}, f32[1,256]{1,0:T(1,128)S(1)}, bf16[768,256]{1,0:T(8,128)(2,1)S(1)}, bf16[768,256]{1,0:T(8,128)(2,1)S(1)}, bf16...) custom-call(s32[1]{0:T(128)} %bitcast.me_ref, ...), custom_call_target="tpu_custom_call" | custom-call | bytes 3933188 | tf_op jit(solution)/shard_map/pallas_call | solution.py:205
  76.1 4.1 %collective-permute-done.32.refs_1_ = f32[48,768]{1,0:T(8,128)S(1)} collective-permute-done((f32[48,768]{1,0:T(8,128)S(1)}, f32[48,768]{1,0:T(8,128)S(1)}, u32[]{:S(2)}, u32[]{:S(2)}) %collective-permute-start.32) | collective-permute-done | bytes 147488 | tf_op jit(solution)/shard_map/ppermute | solution.py:218
  80.4 1.7 %collective-permute-start.30 = (f32[48,768]{1,0:T(8,128)S(1)}, f32[48,768]{1,0:T(8,128)S(1)}, u32[]{:S(2)}, u32[]{:S(2)}) collective-permute-start(f32[48,768]{1,0:T(8,128)S(1)} %collective-permute-done.28.refs_1_), channel_id=1, source_target_pairs={{0,2},{1,3},{2,0},{3,1},{4,6},{5,7},{6,4},{7,5},{8,10},{9,11},{10,... | collective-permute-start | bytes 442376 | tf_op jit(solution)/shard_map/ppermute | solution.py:218
  82.7 3.3 %collective-permute-done.36.refs_1_ = f32[48,768]{1,0:T(8,128)S(1)} collective-permute-done((f32[48,768]{1,0:T(8,128)S(1)}, f32[48,768]{1,0:T(8,128)S(1)}, u32[]{:S(2)}, u32[]{:S(2)}) %collective-permute-start.36) | collective-permute-done | bytes 147488 | tf_op jit(solution)/shard_map/ppermute | solution.py:218
  87.4 2.6 %collective-permute-done.34.refs_3_ = f32[48,768]{1,0:T(8,128)S(1)} collective-permute-done((f32[48,768]{1,0:T(8,128)S(1)}, f32[48,768]{1,0:T(8,128)S(1)}, u32[]{:S(2)}, u32[]{:S(2)}) %collective-permute-start.34) | collective-permute-done | bytes 147488 | tf_op jit(solution)/shard_map/ppermute | solution.py:218
  91.1 1.2 %collective-permute-done.38.refs_3_ = f32[48,768]{1,0:T(8,128)S(1)} collective-permute-done((f32[48,768]{1,0:T(8,128)S(1)}, f32[48,768]{1,0:T(8,128)S(1)}, u32[]{:S(2)}, u32[]{:S(2)}) %collective-permute-start.38) | collective-permute-done | bytes 147488 | tf_op jit(solution)/shard_map/ppermute | solution.py:218
  93.7 2.3 %shard_map.148 = (bf16[192,768]{1,0:T(8,128)(2,1)S(1)}, bf16[192,768]{1,0:T(8,128)(2,1)S(1)}, bf16[256,768]{1,0:T(8,128)(2,1)S(1)}, bf16[256,768]{1,0:T(8,128)(2...) custom-call(f32[256,768]{1,0:T(8,128)S(1)} %get-tuple-element.148.re, ...), custom_call_target="tpu_custom_call" | custom-call | flops 1434451968 | bytes 4980736 | tf_op jit(solution)/shard_map/pallas_call | solution.py:205
  96.6 0.9 shard_map.149
  98.3 1.2 collective-permute-start.46
  99.5 0.9 collective-permute-start.43
  100.4 1.1 collective-permute-start.45
  101.5 3.6 %collective-permute-done.46.c = f32[48,768]{1,0:T(8,128)S(1)} collective-permute-done((f32[48,768]{1,0:T(8,128)S(1)}, f32[48,768]{1,0:T(8,128)S(1)}, u32[]{:S(2)}, u32[]{:S(2)}) %collective-permute-start.46) | collective-permute-done | bytes 147488 | tf_op jit(solution)/shard_map/ppermute | solution.py:218
  105.1 1.7 %collective-permute-start.47 = (f32[48,768]{1,0:T(8,128)S(1)}, f32[48,768]{1,0:T(8,128)S(1)}, u32[]{:S(2)}, u32[]{:S(2)}) collective-permute-start(f32[48,768]{1,0:T(8,128)S(1)} %shard_map.157), channel_id=1, source_target_pairs={{0,4},{1,5},{2,6},{3,7},{4,0},{5,1},{6,2},{7,3},{8,12},{9,13},{10,... | collective-permute-start | bytes 442376 | tf_op jit(solution)/shard_map/ppermute | solution.py:218
  107.2 1.0 collective-permute-done.43.c
  108.3 1.7 %collective-permute-start.44 = (f32[48,768]{1,0:T(8,128)S(1)}, f32[48,768]{1,0:T(8,128)S(1)}, u32[]{:S(2)}, u32[]{:S(2)}) collective-permute-start(f32[48,768]{1,0:T(8,128)S(1)} %shard_map.154), channel_id=1, source_target_pairs={{0,4},{1,5},{2,6},{3,7},{4,0},{5,1},{6,2},{7,3},{8,12},{9,13},{10,... | collective-permute-start | bytes 442376 | tf_op jit(solution)/shard_map/ppermute | solution.py:218
  110.0 1.4 %collective-permute-done.45.c = f32[48,768]{1,0:T(8,128)S(1)} collective-permute-done((f32[48,768]{1,0:T(8,128)S(1)}, f32[48,768]{1,0:T(8,128)S(1)}, u32[]{:S(2)}, u32[]{:S(2)}) %collective-permute-start.45) | collective-permute-done | bytes 147488 | tf_op jit(solution)/shard_map/ppermute | solution.py:218
  111.5 1.5 %collective-permute-start.48 = (f32[48,768]{1,0:T(8,128)S(1)}, f32[48,768]{1,0:T(8,128)S(1)}, u32[]{:S(2)}, u32[]{:S(2)}) collective-permute-start(f32[48,768]{1,0:T(8,128)S(1)} %shard_map.158), channel_id=1, source_target_pairs={{0,8},{1,9},{2,10},{3,11},{4,12},{5,13},{6,14},{7,15},{8,0},{9,1},... | collective-permute-start | bytes 442376 | tf_op jit(solution)/shard_map/ppermute | solution.py:218
  113.0 1.1 collective-permute-done.41.c
  114.0 2.4 %shard_map.151 = (f32[256,768]{1,0:T(8,128)}, f32[1,256]{1,0:T(1,128)}) custom-call(s32[1]{0:T(128)} %bitcast.me_ref, bf16[256,768]{1,0:T(8,128)(2,1)S(1)} %get-tuple-element.157.grad_high, bf16[256,768]{1,0:T(8,128)(2,1)S(1)} %get-tuple-element.153.grad_low, bf16[192,768]{1,0:T(8,128)(2,1)S(1)} %get-tuple-element.158.rest_0_, ...), custom_call_target="tpu_custom_call" | custom-call | bytes 3933188 | tf_op jit(solution)/shard_map/pallas_call | solution.py:205
  116.4 2.2 %shard_map.152 = (f32[512,768]{1,0:T(8,128)}, f32[1,512]{1,0:T(1,128)}) custom-call(f32[256,512]{1,0:T(8,128)S(1)} %get-tuple-element.171.grad_scores, bf16[256,768]{1,0:T(8,128)(2,1)S(1)} %get-tuple-element.172.product_high, bf16[256,768]{1,0:T(8,128)(2,1)S(1)} %get-tuple-element.173.product_low, f32[520,768]{1,0:T(8,128)S(1)} %collective-permute-done.27.refs_0_), custom_call_target="tpu_custom_call" | custom-call | flops 603979776 | bytes 2908160 | tf_op jit(solution)/shard_map/pallas_call | solution.py:205
  118.6 1.7 %collective-permute-done.48.rest_1_ = f32[48,768]{1,0:T(8,128)S(1)} collective-permute-done((f32[48,768]{1,0:T(8,128)S(1)}, f32[48,768]{1,0:T(8,128)S(1)}, u32[]{:S(2)}, u32[]{:S(2)}) %collective-permute-start.48) | collective-permute-done | bytes 147488 | tf_op jit(solution)/shard_map/ppermute | solution.py:218
  120.4 0.8 shard_map.159
  (103 shorter events, 13.9 us)
Async XLA Ops:
  0.6 11.4 %collective-permute-start.7 = (f32[48,768]{1,0:T(8,128)}, f32[48,768]{1,0:T(8,128)S(1)}, u32[]{:S(2)}, u32[]{:S(2)}) collective-permute-start(f32[48,768]{1,0:T(8,128)} %relation.1), channel_id=1, source_target_pairs={{0,8},{1,9},{2,10},{3,11},{4,12},{5,13},{6,14},{7,15},{8,0},{9,1},... | collective-permute-start | bytes 442376 | tf_op jit(solution)/shard_map/ppermute | solution.py:218
  4.7 8.0 %collective-permute-start.3 = (f32[48,768]{1,0:T(8,128)}, f32[48,768]{1,0:T(8,128)S(1)}, u32[]{:S(2)}, u32[]{:S(2)}) collective-permute-start(f32[48,768]{1,0:T(8,128)} %relation.1), channel_id=1, source_target_pairs={{0,4},{1,5},{2,6},{3,7},{4,0},{5,1},{6,2},{7,3},{8,12},{9,13},{10,... | collective-permute-start | bytes 442376 | tf_op jit(solution)/shard_map/ppermute | solution.py:218
  6.3 8.0 %collective-permute-start.1 = (f32[48,768]{1,0:T(8,128)}, f32[48,768]{1,0:T(8,128)S(1)}, u32[]{:S(2)}, u32[]{:S(2)}) collective-permute-start(f32[48,768]{1,0:T(8,128)} %relation.1), channel_id=1, source_target_pairs={{0,2},{1,3},{2,0},{3,1},{4,6},{5,7},{6,4},{7,5},{8,10},{9,11},{10,... | collective-permute-start | bytes 442376 | tf_op jit(solution)/shard_map/ppermute | solution.py:218
  7.8 7.0 %collective-permute-start = (f32[48,768]{1,0:T(8,128)}, f32[48,768]{1,0:T(8,128)S(1)}, u32[]{:S(2)}, u32[]{:S(2)}) collective-permute-start(f32[48,768]{1,0:T(8,128)} %relation.1), channel_id=1, source_target_pairs={{0,1},{1,0},{2,3},{3,2},{4,5},{5,4},{6,7},{7,6},{8,9},{9,8},{10,11... | collective-permute-start | bytes 442376 | tf_op jit(solution)/shard_map/ppermute | solution.py:218
  12.1 5.1 %collective-permute-start.11 = (f32[48,768]{1,0:T(8,128)S(1)}, f32[48,768]{1,0:T(8,128)S(1)}, u32[]{:S(2)}, u32[]{:S(2)}) collective-permute-start(f32[48,768]{1,0:T(8,128)S(1)} %collective-permute-done.7.refs_1_), channel_id=1, source_target_pairs={{0,4},{1,5},{2,6},{3,7},{4,0},{5,1},{6,2},{7,3},{8,12},{9,13},{10,... | collective-permute-start | bytes 442376 | tf_op jit(solution)/shard_map/ppermute | solution.py:218
  12.8 6.3 %collective-permute-start.5 = (f32[48,768]{1,0:T(8,128)S(1)}, f32[48,768]{1,0:T(8,128)S(1)}, u32[]{:S(2)}, u32[]{:S(2)}) collective-permute-start(f32[48,768]{1,0:T(8,128)S(1)} %collective-permute-done.3.refs_1_), channel_id=1, source_target_pairs={{0,2},{1,3},{2,0},{3,1},{4,6},{5,7},{6,4},{7,5},{8,10},{9,11},{10,... | collective-permute-start | bytes 442376 | tf_op jit(solution)/shard_map/ppermute | solution.py:218
  14.3 8.5 %collective-permute-start.2 = (f32[48,768]{1,0:T(8,128)S(1)}, f32[48,768]{1,0:T(8,128)S(1)}, u32[]{:S(2)}, u32[]{:S(2)}) collective-permute-start(f32[48,768]{1,0:T(8,128)S(1)} %collective-permute-done.1.refs_2_), channel_id=1, source_target_pairs={{0,1},{1,0},{2,3},{3,2},{4,5},{5,4},{6,7},{7,6},{8,9},{9,8},{10,11... | collective-permute-start | bytes 442376 | tf_op jit(solution)/shard_map/ppermute | solution.py:218
  14.3 9.1 %collective-permute-start.9 = (f32[48,768]{1,0:T(8,128)S(1)}, f32[48,768]{1,0:T(8,128)S(1)}, u32[]{:S(2)}, u32[]{:S(2)}) collective-permute-start(f32[48,768]{1,0:T(8,128)S(1)} %collective-permute-done.7.refs_1_), channel_id=1, source_target_pairs={{0,2},{1,3},{2,0},{3,1},{4,6},{5,7},{6,4},{7,5},{8,10},{9,11},{10,... | collective-permute-start | bytes 442376 | tf_op jit(solution)/shard_map/ppermute | solution.py:218
  14.8 9.2 %collective-permute-start.4 = (f32[48,768]{1,0:T(8,128)S(1)}, f32[48,768]{1,0:T(8,128)S(1)}, u32[]{:S(2)}, u32[]{:S(2)}) collective-permute-start(f32[48,768]{1,0:T(8,128)S(1)} %collective-permute-done.3.refs_1_), channel_id=1, source_target_pairs={{0,1},{1,0},{2,3},{3,2},{4,5},{5,4},{6,7},{7,6},{8,9},{9,8},{10,11... | collective-permute-start | bytes 442376 | tf_op jit(solution)/shard_map/ppermute | solution.py:218
  17.2 7.4 %collective-permute-start.13 = (f32[48,768]{1,0:T(8,128)S(1)}, f32[48,768]{1,0:T(8,128)S(1)}, u32[]{:S(2)}, u32[]{:S(2)}) collective-permute-start(f32[48,768]{1,0:T(8,128)S(1)} %collective-permute-done.11.refs_1_), channel_id=1, source_target_pairs={{0,2},{1,3},{2,0},{3,1},{4,6},{5,7},{6,4},{7,5},{8,10},{9,11},{10,... | collective-permute-start | bytes 442376 | tf_op jit(solution)/shard_map/ppermute | solution.py:218
  19.1 5.5 %collective-permute-start.6 = (f32[48,768]{1,0:T(8,128)S(1)}, f32[48,768]{1,0:T(8,128)S(1)}, u32[]{:S(2)}, u32[]{:S(2)}) collective-permute-start(f32[48,768]{1,0:T(8,128)S(1)} %collective-permute-done.5.refs_3_), channel_id=1, source_target_pairs={{0,1},{1,0},{2,3},{3,2},{4,5},{5,4},{6,7},{7,6},{8,9},{9,8},{10,11... | collective-permute-start | bytes 442376 | tf_op jit(solution)/shard_map/ppermute | solution.py:218
  22.8 2.3 %collective-permute-start.8 = (f32[48,768]{1,0:T(8,128)S(1)}, f32[48,768]{1,0:T(8,128)S(1)}, u32[]{:S(2)}, u32[]{:S(2)}) collective-permute-start(f32[48,768]{1,0:T(8,128)S(1)} %collective-permute-done.7.refs_1_), channel_id=1, source_target_pairs={{0,1},{1,0},{2,3},{3,2},{4,5},{5,4},{6,7},{7,6},{8,9},{9,8},{10,11... | collective-permute-start | bytes 442376 | tf_op jit(solution)/shard_map/ppermute | solution.py:218
  23.4 1.8 %collective-permute-start.10 = (f32[48,768]{1,0:T(8,128)S(1)}, f32[48,768]{1,0:T(8,128)S(1)}, u32[]{:S(2)}, u32[]{:S(2)}) collective-permute-start(f32[48,768]{1,0:T(8,128)S(1)} %collective-permute-done.9.refs_3_), channel_id=1, source_target_pairs={{0,1},{1,0},{2,3},{3,2},{4,5},{5,4},{6,7},{7,6},{8,9},{9,8},{10,11... | collective-permute-start | bytes 442376 | tf_op jit(solution)/shard_map/ppermute | solution.py:218
  24.1 1.7 %collective-permute-start.12 = (f32[48,768]{1,0:T(8,128)S(1)}, f32[48,768]{1,0:T(8,128)S(1)}, u32[]{:S(2)}, u32[]{:S(2)}) collective-permute-start(f32[48,768]{1,0:T(8,128)S(1)} %collective-permute-done.11.refs_1_), channel_id=1, source_target_pairs={{0,1},{1,0},{2,3},{3,2},{4,5},{5,4},{6,7},{7,6},{8,9},{9,8},{10,11... | collective-permute-start | bytes 442376 | tf_op jit(solution)/shard_map/ppermute | solution.py:218
  24.6 1.4 %collective-permute-start.14 = (f32[48,768]{1,0:T(8,128)S(1)}, f32[48,768]{1,0:T(8,128)S(1)}, u32[]{:S(2)}, u32[]{:S(2)}) collective-permute-start(f32[48,768]{1,0:T(8,128)S(1)} %collective-permute-done.13.refs_3_), channel_id=1, source_target_pairs={{0,1},{1,0},{2,3},{3,2},{4,5},{5,4},{6,7},{7,6},{8,9},{9,8},{10,11... | collective-permute-start | bytes 442376 | tf_op jit(solution)/shard_map/ppermute | solution.py:218
  28.4 45.7 %collective-permute-start.27 = (f32[520,768]{1,0:T(8,128)S(1)}, f32[520,768]{1,0:T(8,128)S(1)}, u32[]{:S(2)}, u32[]{:S(2)}) collective-permute-start(f32[520,768]{1,0:T(8,128)S(1)} %get-tuple-element.125), channel_id=1, source_target_pairs={{0,1},{1,2},{2,3},{3,4},{4,5},{5,6},{6,7},{7,8},{8,9},{9,10},{10,1... | collective-permute-start | bytes 4792328 | tf_op jit(solution)/shard_map/ppermute | solution.py:354
  30.1 3.4 %collective-permute-start.16 = (f32[192,768]{1,0:T(8,128)S(1)}, f32[192,768]{1,0:T(8,128)S(1)}, u32[]{:S(2)}, u32[]{:S(2)}) collective-permute-start(f32[192,768]{1,0:T(8,128)S(1)} %get-tuple-element.119), channel_id=1, source_target_pairs={{0,1},{1,0},{2,3},{3,2},{4,5},{5,4},{6,7},{7,6},{8,9},{9,8},{10,11... | collective-permute-start | bytes 1769480 | tf_op jit(solution)/shard_map/ppermute | solution.py:218
  32.8 4.0 %collective-permute-start.15 = (f32[192,768]{1,0:T(8,128)S(1)}, f32[192,768]{1,0:T(8,128)S(1)}, u32[]{:S(2)}, u32[]{:S(2)}) collective-permute-start(f32[192,768]{1,0:T(8,128)S(1)} %get-tuple-element.117), channel_id=1, source_target_pairs={{0,1},{1,0},{2,3},{3,2},{4,5},{5,4},{6,7},{7,6},{8,9},{9,8},{10,11... | collective-permute-start | bytes 1769480 | tf_op jit(solution)/shard_map/ppermute | solution.py:218
  33.6 21.0 %collective-permute-start.21 = (f32[48,768]{1,0:T(8,128)S(1)}, f32[48,768]{1,0:T(8,128)S(1)}, u32[]{:S(2)}, u32[]{:S(2)}) collective-permute-start(f32[48,768]{1,0:T(8,128)S(1)} %get-tuple-element.123), channel_id=1, source_target_pairs={{0,2},{1,3},{2,0},{3,1},{4,6},{5,7},{6,4},{7,5},{8,10},{9,11},{10,... | collective-permute-start | bytes 442376 | tf_op jit(solution)/shard_map/ppermute | solution.py:218
  34.8 23.0 %collective-permute-start.18 = (f32[48,768]{1,0:T(8,128)S(1)}, f32[48,768]{1,0:T(8,128)S(1)}, u32[]{:S(2)}, u32[]{:S(2)}) collective-permute-start(f32[48,768]{1,0:T(8,128)S(1)} %get-tuple-element.121), channel_id=1, source_target_pairs={{0,2},{1,3},{2,0},{3,1},{4,6},{5,7},{6,4},{7,5},{8,10},{9,11},{10,... | collective-permute-start | bytes 442376 | tf_op jit(solution)/shard_map/ppermute | solution.py:218
  35.7 25.2 %collective-permute-start.20 = (f32[48,768]{1,0:T(8,128)S(1)}, f32[48,768]{1,0:T(8,128)S(1)}, u32[]{:S(2)}, u32[]{:S(2)}) collective-permute-start(f32[48,768]{1,0:T(8,128)S(1)} %get-tuple-element.122), channel_id=1, source_target_pairs={{0,2},{1,3},{2,0},{3,1},{4,6},{5,7},{6,4},{7,5},{8,10},{9,11},{10,... | collective-permute-start | bytes 442376 | tf_op jit(solution)/shard_map/ppermute | solution.py:218
  54.7 6.3 %collective-permute-start.22 = (f32[48,768]{1,0:T(8,128)S(1)}, f32[48,768]{1,0:T(8,128)S(1)}, u32[]{:S(2)}, u32[]{:S(2)}) collective-permute-start(f32[48,768]{1,0:T(8,128)S(1)} %shard_map.140), channel_id=1, source_target_pairs={{0,4},{1,5},{2,6},{3,7},{4,0},{5,1},{6,2},{7,3},{8,12},{9,13},{10,... | collective-permute-start | bytes 442376 | tf_op jit(solution)/shard_map/ppermute | solution.py:218
  54.7 9.3 %collective-permute-start.17 = (f32[48,768]{1,0:T(8,128)S(1)}, f32[48,768]{1,0:T(8,128)S(1)}, u32[]{:S(2)}, u32[]{:S(2)}) collective-permute-start(f32[48,768]{1,0:T(8,128)S(1)} %get-tuple-element.120), channel_id=1, source_target_pairs={{0,2},{1,3},{2,0},{3,1},{4,6},{5,7},{6,4},{7,5},{8,10},{9,11},{10,... | collective-permute-start | bytes 442376 | tf_op jit(solution)/shard_map/ppermute | solution.py:218
  57.8 6.3 %collective-permute-start.19 = (f32[48,768]{1,0:T(8,128)S(1)}, f32[48,768]{1,0:T(8,128)S(1)}, u32[]{:S(2)}, u32[]{:S(2)}) collective-permute-start(f32[48,768]{1,0:T(8,128)S(1)} %shard_map.137), channel_id=1, source_target_pairs={{0,4},{1,5},{2,6},{3,7},{4,0},{5,1},{6,2},{7,3},{8,12},{9,13},{10,... | collective-permute-start | bytes 442376 | tf_op jit(solution)/shard_map/ppermute | solution.py:218
  61.0 9.9 %collective-permute-start.23 = (f32[48,768]{1,0:T(8,128)S(1)}, f32[48,768]{1,0:T(8,128)S(1)}, u32[]{:S(2)}, u32[]{:S(2)}) collective-permute-start(f32[48,768]{1,0:T(8,128)S(1)} %shard_map.141), channel_id=1, source_target_pairs={{0,8},{1,9},{2,10},{3,11},{4,12},{5,13},{6,14},{7,15},{8,0},{9,1},... | collective-permute-start | bytes 442376 | tf_op jit(solution)/shard_map/ppermute | solution.py:218
  71.1 9.2 %collective-permute-start.32 = (f32[48,768]{1,0:T(8,128)S(1)}, f32[48,768]{1,0:T(8,128)S(1)}, u32[]{:S(2)}, u32[]{:S(2)}) collective-permute-start(f32[48,768]{1,0:T(8,128)S(1)} %get-tuple-element.124.refs_0_.relation), channel_id=1, source_target_pairs={{0,8},{1,9},{2,10},{3,11},{4,12},{5,13},{6,14},{7,15},{8,0},{9,1},... | collective-permute-start | bytes 442376 | tf_op jit(solution)/shard_map/ppermute | solution.py:218
  71.1 9.1 %collective-permute-start.25 = (f32[48,768]{1,0:T(8,128)S(1)}, f32[48,768]{1,0:T(8,128)S(1)}, u32[]{:S(2)}, u32[]{:S(2)}) collective-permute-start(f32[48,768]{1,0:T(8,128)S(1)} %get-tuple-element.124.refs_0_.relation), channel_id=1, source_target_pairs={{0,2},{1,3},{2,0},{3,1},{4,6},{5,7},{6,4},{7,5},{8,10},{9,11},{10,... | collective-permute-start | bytes 442376 | tf_op jit(solution)/shard_map/ppermute | solution.py:218
  71.2 9.2 %collective-permute-start.28 = (f32[48,768]{1,0:T(8,128)S(1)}, f32[48,768]{1,0:T(8,128)S(1)}, u32[]{:S(2)}, u32[]{:S(2)}) collective-permute-start(f32[48,768]{1,0:T(8,128)S(1)} %get-tuple-element.124.refs_0_.relation), channel_id=1, source_target_pairs={{0,4},{1,5},{2,6},{3,7},{4,0},{5,1},{6,2},{7,3},{8,12},{9,13},{10,... | collective-permute-start | bytes 442376 | tf_op jit(solution)/shard_map/ppermute | solution.py:218
  74.1 8.4 %collective-permute-start.24 = (f32[48,768]{1,0:T(8,128)S(1)}, f32[48,768]{1,0:T(8,128)S(1)}, u32[]{:S(2)}, u32[]{:S(2)}) collective-permute-start(f32[48,768]{1,0:T(8,128)S(1)} %get-tuple-element.124.refs_0_.relation), channel_id=1, source_target_pairs={{0,1},{1,0},{2,3},{3,2},{4,5},{5,4},{6,7},{7,6},{8,9},{9,8},{10,11... | collective-permute-start | bytes 442376 | tf_op jit(solution)/shard_map/ppermute | solution.py:218
  80.3 5.7 %collective-permute-start.36 = (f32[48,768]{1,0:T(8,128)S(1)}, f32[48,768]{1,0:T(8,128)S(1)}, u32[]{:S(2)}, u32[]{:S(2)}) collective-permute-start(f32[48,768]{1,0:T(8,128)S(1)} %collective-permute-done.32.refs_1_), channel_id=1, source_target_pairs={{0,4},{1,5},{2,6},{3,7},{4,0},{5,1},{6,2},{7,3},{8,12},{9,13},{10,... | collective-permute-start | bytes 442376 | tf_op jit(solution)/shard_map/ppermute | solution.py:218
  80.4 6.4 %collective-permute-start.30 = (f32[48,768]{1,0:T(8,128)S(1)}, f32[48,768]{1,0:T(8,128)S(1)}, u32[]{:S(2)}, u32[]{:S(2)}) collective-permute-start(f32[48,768]{1,0:T(8,128)S(1)} %collective-permute-done.28.refs_1_), channel_id=1, source_target_pairs={{0,2},{1,3},{2,0},{3,1},{4,6},{5,7},{6,4},{7,5},{8,10},{9,11},{10,... | collective-permute-start | bytes 442376 | tf_op jit(solution)/shard_map/ppermute | solution.py:218
  82.1 4.8 %collective-permute-start.26 = (f32[48,768]{1,0:T(8,128)S(1)}, f32[48,768]{1,0:T(8,128)S(1)}, u32[]{:S(2)}, u32[]{:S(2)}) collective-permute-start(f32[48,768]{1,0:T(8,128)S(1)} %collective-permute-done.25.refs_2_), channel_id=1, source_target_pairs={{0,1},{1,0},{2,3},{3,2},{4,5},{5,4},{6,7},{7,6},{8,9},{9,8},{10,11... | collective-permute-start | bytes 442376 | tf_op jit(solution)/shard_map/ppermute | solution.py:218
  82.1 7.9 %collective-permute-start.34 = (f32[48,768]{1,0:T(8,128)S(1)}, f32[48,768]{1,0:T(8,128)S(1)}, u32[]{:S(2)}, u32[]{:S(2)}) collective-permute-start(f32[48,768]{1,0:T(8,128)S(1)} %collective-permute-done.32.refs_1_), channel_id=1, source_target_pairs={{0,2},{1,3},{2,0},{3,1},{4,6},{5,7},{6,4},{7,5},{8,10},{9,11},{10,... | collective-permute-start | bytes 442376 | tf_op jit(solution)/shard_map/ppermute | solution.py:218
  82.5 8.1 %collective-permute-start.29 = (f32[48,768]{1,0:T(8,128)S(1)}, f32[48,768]{1,0:T(8,128)S(1)}, u32[]{:S(2)}, u32[]{:S(2)}) collective-permute-start(f32[48,768]{1,0:T(8,128)S(1)} %collective-permute-done.28.refs_1_), channel_id=1, source_target_pairs={{0,1},{1,0},{2,3},{3,2},{4,5},{5,4},{6,7},{7,6},{8,9},{9,8},{10,11... | collective-permute-start | bytes 442376 | tf_op jit(solution)/shard_map/ppermute | solution.py:218
  86.0 6.4 %collective-permute-start.38 = (f32[48,768]{1,0:T(8,128)S(1)}, f32[48,768]{1,0:T(8,128)S(1)}, u32[]{:S(2)}, u32[]{:S(2)}) collective-permute-start(f32[48,768]{1,0:T(8,128)S(1)} %collective-permute-done.36.refs_1_), channel_id=1, source_target_pairs={{0,2},{1,3},{2,0},{3,1},{4,6},{5,7},{6,4},{7,5},{8,10},{9,11},{10,... | collective-permute-start | bytes 442376 | tf_op jit(solution)/shard_map/ppermute | solution.py:218
  86.9 5.7 %collective-permute-start.31 = (f32[48,768]{1,0:T(8,128)S(1)}, f32[48,768]{1,0:T(8,128)S(1)}, u32[]{:S(2)}, u32[]{:S(2)}) collective-permute-start(f32[48,768]{1,0:T(8,128)S(1)} %collective-permute-done.30.refs_3_), channel_id=1, source_target_pairs={{0,1},{1,0},{2,3},{3,2},{4,5},{5,4},{6,7},{7,6},{8,9},{9,8},{10,11... | collective-permute-start | bytes 442376 | tf_op jit(solution)/shard_map/ppermute | solution.py:218
  86.9 6.3 %collective-permute-start.33 = (f32[48,768]{1,0:T(8,128)S(1)}, f32[48,768]{1,0:T(8,128)S(1)}, u32[]{:S(2)}, u32[]{:S(2)}) collective-permute-start(f32[48,768]{1,0:T(8,128)S(1)} %collective-permute-done.32.refs_1_), channel_id=1, source_target_pairs={{0,1},{1,0},{2,3},{3,2},{4,5},{5,4},{6,7},{7,6},{8,9},{9,8},{10,11... | collective-permute-start | bytes 442376 | tf_op jit(solution)/shard_map/ppermute | solution.py:218
  90.0 3.1 %collective-permute-start.35 = (f32[48,768]{1,0:T(8,128)S(1)}, f32[48,768]{1,0:T(8,128)S(1)}, u32[]{:S(2)}, u32[]{:S(2)}) collective-permute-start(f32[48,768]{1,0:T(8,128)S(1)} %collective-permute-done.34.refs_3_), channel_id=1, source_target_pairs={{0,1},{1,0},{2,3},{3,2},{4,5},{5,4},{6,7},{7,6},{8,9},{9,8},{10,11... | collective-permute-start | bytes 442376 | tf_op jit(solution)/shard_map/ppermute | solution.py:218
  90.6 3.1 %collective-permute-start.37 = (f32[48,768]{1,0:T(8,128)S(1)}, f32[48,768]{1,0:T(8,128)S(1)}, u32[]{:S(2)}, u32[]{:S(2)}) collective-permute-start(f32[48,768]{1,0:T(8,128)S(1)} %collective-permute-done.36.refs_1_), channel_id=1, source_target_pairs={{0,1},{1,0},{2,3},{3,2},{4,5},{5,4},{6,7},{7,6},{8,9},{9,8},{10,11... | collective-permute-start | bytes 442376 | tf_op jit(solution)/shard_map/ppermute | solution.py:218
  96.1 2.2 %collective-permute-start.40 = (f32[192,768]{1,0:T(8,128)S(1)}, f32[192,768]{1,0:T(8,128)S(1)}, u32[]{:S(2)}, u32[]{:S(2)}) collective-permute-start(f32[192,768]{1,0:T(8,128)S(1)} %get-tuple-element.155), channel_id=1, source_target_pairs={{0,1},{1,0},{2,3},{3,2},{4,5},{5,4},{6,7},{7,6},{8,9},{9,8},{10,11... | collective-permute-start | bytes 1769480 | tf_op jit(solution)/shard_map/ppermute | solution.py:218
  97.5 4.0 %collective-permute-start.42 = (f32[192,768]{1,0:T(8,128)S(1)}, f32[192,768]{1,0:T(8,128)S(1)}, u32[]{:S(2)}, u32[]{:S(2)}) collective-permute-start(f32[192,768]{1,0:T(8,128)S(1)} %get-tuple-element.178), channel_id=1, source_target_pairs={{0,1},{1,0},{2,3},{3,2},{4,5},{5,4},{6,7},{7,6},{8,9},{9,8},{10,11... | collective-permute-start | bytes 1769480 | tf_op jit(solution)/shard_map/ppermute | solution.py:218
  98.3 6.7 %collective-permute-start.46 = (f32[48,768]{1,0:T(8,128)S(1)}, f32[48,768]{1,0:T(8,128)S(1)}, u32[]{:S(2)}, u32[]{:S(2)}) collective-permute-start(f32[48,768]{1,0:T(8,128)S(1)} %get-tuple-element.181), channel_id=1, source_target_pairs={{0,2},{1,3},{2,0},{3,1},{4,6},{5,7},{6,4},{7,5},{8,10},{9,11},{10,... | collective-permute-start | bytes 442376 | tf_op jit(solution)/shard_map/ppermute | solution.py:218
  99.5 8.7 %collective-permute-start.43 = (f32[48,768]{1,0:T(8,128)S(1)}, f32[48,768]{1,0:T(8,128)S(1)}, u32[]{:S(2)}, u32[]{:S(2)}) collective-permute-start(f32[48,768]{1,0:T(8,128)S(1)} %get-tuple-element.179), channel_id=1, source_target_pairs={{0,2},{1,3},{2,0},{3,1},{4,6},{5,7},{6,4},{7,5},{8,10},{9,11},{10,... | collective-permute-start | bytes 442376 | tf_op jit(solution)/shard_map/ppermute | solution.py:218
  100.4 11.0 %collective-permute-start.45 = (f32[48,768]{1,0:T(8,128)S(1)}, f32[48,768]{1,0:T(8,128)S(1)}, u32[]{:S(2)}, u32[]{:S(2)}) collective-permute-start(f32[48,768]{1,0:T(8,128)S(1)} %get-tuple-element.180), channel_id=1, source_target_pairs={{0,2},{1,3},{2,0},{3,1},{4,6},{5,7},{6,4},{7,5},{8,10},{9,11},{10,... | collective-permute-start | bytes 442376 | tf_op jit(solution)/shard_map/ppermute | solution.py:218
  105.1 6.3 %collective-permute-start.47 = (f32[48,768]{1,0:T(8,128)S(1)}, f32[48,768]{1,0:T(8,128)S(1)}, u32[]{:S(2)}, u32[]{:S(2)}) collective-permute-start(f32[48,768]{1,0:T(8,128)S(1)} %shard_map.157), channel_id=1, source_target_pairs={{0,4},{1,5},{2,6},{3,7},{4,0},{5,1},{6,2},{7,3},{8,12},{9,13},{10,... | collective-permute-start | bytes 442376 | tf_op jit(solution)/shard_map/ppermute | solution.py:218
  106.9 7.2 %collective-permute-start.41 = (f32[48,768]{1,0:T(8,128)S(1)}, f32[48,768]{1,0:T(8,128)S(1)}, u32[]{:S(2)}, u32[]{:S(2)}) collective-permute-start(f32[48,768]{1,0:T(8,128)S(1)} %get-tuple-element.156), channel_id=1, source_target_pairs={{0,2},{1,3},{2,0},{3,1},{4,6},{5,7},{6,4},{7,5},{8,10},{9,11},{10,... | collective-permute-start | bytes 442376 | tf_op jit(solution)/shard_map/ppermute | solution.py:218
  108.3 10.3 %collective-permute-start.44 = (f32[48,768]{1,0:T(8,128)S(1)}, f32[48,768]{1,0:T(8,128)S(1)}, u32[]{:S(2)}, u32[]{:S(2)}) collective-permute-start(f32[48,768]{1,0:T(8,128)S(1)} %shard_map.154), channel_id=1, source_target_pairs={{0,4},{1,5},{2,6},{3,7},{4,0},{5,1},{6,2},{7,3},{8,12},{9,13},{10,... | collective-permute-start | bytes 442376 | tf_op jit(solution)/shard_map/ppermute | solution.py:218
  111.5 8.9 %collective-permute-start.48 = (f32[48,768]{1,0:T(8,128)S(1)}, f32[48,768]{1,0:T(8,128)S(1)}, u32[]{:S(2)}, u32[]{:S(2)}) collective-permute-start(f32[48,768]{1,0:T(8,128)S(1)} %shard_map.158), channel_id=1, source_target_pairs={{0,8},{1,9},{2,10},{3,11},{4,12},{5,13},{6,14},{7,15},{8,0},{9,1},... | collective-permute-start | bytes 442376 | tf_op jit(solution)/shard_map/ppermute | solution.py:218
  (11 other events, 63.0 us)

commit v6 on v5

--- a/solution.py
+++ b/solution.py
@@ -34,10 +34,13 @@
 
 def adagrad(param, state_row, grad):
     n = param.shape[0]
-    eye = diagonal(n)
-    state = jnp.sum(jnp.where(eye, state_row, 0.0), axis=1, keepdims=True)
+    step = 128 if n % 128 == 0 else n
+    eye, starts = diagonal(step), range(0, n, step)
+    parts = [jnp.sum(jnp.where(eye, state_row[:, i : i + step], 0.0), axis=1, keepdims=True) for i in starts]
+    state = jnp.concatenate(parts, axis=0)
     state = state + jnp.sum(grad * grad, axis=1, keepdims=True) * (1.0 / grad.shape[1])
-    back = jnp.sum(jnp.where(eye, state, 0.0), axis=0, keepdims=True)
+    parts = [jnp.sum(jnp.where(eye, state[i : i + step, :], 0.0), axis=0, keepdims=True) for i in starts]
+    back = jnp.concatenate(parts, axis=1)
     return param - grad * (0.1 / jnp.sqrt(state)), back
 
 

time: 121 us -> 122 us (level)
  transfers between devices with their start and end apart: 49 -> 49, of which waited for: 22 -> 22; matrix products, arithmetic and copies ran while one was open for 0% -> 0% of each run, Pallas kernels for 12% -> 13%
where the time goes in v6:
time: 122 us; the launch traced here: 121 us
  waiting for transfers between devices  59 us (48%)
  starting transfers between devices  36.2 us (30%)
  Pallas kernels  21.3 us (17%)
  local copies, waits for them, and re-layouts  3.95 us (3%)
    ppermute x48, waiting for transfers between devices, partner(): return lax.ppermute(value, 'blk', [(i, i ^ mask) for i in range(n)])  59 us
    ppermute x48, starting transfers between devices, partner(): return lax.ppermute(value, 'blk', [(i, i ^ mask) for i in range(n)])  35.7 us
    pallas_call x33, Pallas kernels, call(): pl.pallas_call(kernel, out_shape=[jax.ShapeDtypeStruct(s, t) for s, t in...  21.3 us
    unnamed x20, local copies, waits for them, and re-layouts  3.95 us
  transfers between devices with their start and end apart: 49, of which 22 were waited for; matrix products, arithmetic and copies ran while one was open for 0% of the time, Pallas kernels for 13%

profile of v6, /device:TPU:0, one launch (start us, length us, event | category | flops | bytes accessed | tf_op | source)
XLA Modules:
  0.0 121.4 jit_solution(13033140562701469964)
XLA Ops:
  0.6 4.1 %collective-permute-start.7 = (f32[48,768]{1,0:T(8,128)}, f32[48,768]{1,0:T(8,128)S(1)}, u32[]{:S(2)}, u32[]{:S(2)}) collective-permute-start(f32[48,768]{1,0:T(8,128)} %relation.1), channel_id=1, source_target_pairs={{0,8},{1,9},{2,10},{3,11},{4,12},{5,13},{6,14},{7,15},{8,0},{9,1},... | collective-permute-start | bytes 442376 | tf_op jit(solution)/shard_map/ppermute | solution.py:221
  4.7 1.6 %collective-permute-start.3 = (f32[48,768]{1,0:T(8,128)}, f32[48,768]{1,0:T(8,128)S(1)}, u32[]{:S(2)}, u32[]{:S(2)}) collective-permute-start(f32[48,768]{1,0:T(8,128)} %relation.1), channel_id=1, source_target_pairs={{0,4},{1,5},{2,6},{3,7},{4,0},{5,1},{6,2},{7,3},{8,12},{9,13},{10,... | collective-permute-start | bytes 442376 | tf_op jit(solution)/shard_map/ppermute | solution.py:221
  6.3 1.5 %collective-permute-start.1 = (f32[48,768]{1,0:T(8,128)}, f32[48,768]{1,0:T(8,128)S(1)}, u32[]{:S(2)}, u32[]{:S(2)}) collective-permute-start(f32[48,768]{1,0:T(8,128)} %relation.1), channel_id=1, source_target_pairs={{0,2},{1,3},{2,0},{3,1},{4,6},{5,7},{6,4},{7,5},{8,10},{9,11},{10,... | collective-permute-start | bytes 442376 | tf_op jit(solution)/shard_map/ppermute | solution.py:221
  7.8 1.1 copy-done.2
  9.6 2.5 %collective-permute-done.7.refs_1_ = f32[48,768]{1,0:T(8,128)S(1)} collective-permute-done((f32[48,768]{1,0:T(8,128)}, f32[48,768]{1,0:T(8,128)S(1)}, u32[]{:S(2)}, u32[]{:S(2)}) %collective-permute-start.7) | collective-permute-done | bytes 147488 | tf_op jit(solution)/shard_map/ppermute | solution.py:221
  12.1 0.7 collective-permute-start.11
  12.8 1.5 %collective-permute-start.5 = (f32[48,768]{1,0:T(8,128)S(1)}, f32[48,768]{1,0:T(8,128)S(1)}, u32[]{:S(2)}, u32[]{:S(2)}) collective-permute-start(f32[48,768]{1,0:T(8,128)S(1)} %collective-permute-done.3.refs_1_), channel_id=1, source_target_pairs={{0,2},{1,3},{2,0},{3,1},{4,6},{5,7},{6,4},{7,5},{8,10},{9,11},{10,... | collective-permute-start | bytes 442376 | tf_op jit(solution)/shard_map/ppermute | solution.py:221
  15.0 2.2 %collective-permute-done.11.refs_1_ = f32[48,768]{1,0:T(8,128)S(1)} collective-permute-done((f32[48,768]{1,0:T(8,128)S(1)}, f32[48,768]{1,0:T(8,128)S(1)}, u32[]{:S(2)}, u32[]{:S(2)}) %collective-permute-start.11) | collective-permute-done | bytes 147488 | tf_op jit(solution)/shard_map/ppermute | solution.py:221
  17.2 1.6 %collective-permute-start.13 = (f32[48,768]{1,0:T(8,128)S(1)}, f32[48,768]{1,0:T(8,128)S(1)}, u32[]{:S(2)}, u32[]{:S(2)}) collective-permute-start(f32[48,768]{1,0:T(8,128)S(1)} %collective-permute-done.11.refs_1_), channel_id=1, source_target_pairs={{0,2},{1,3},{2,0},{3,1},{4,6},{5,7},{6,4},{7,5},{8,10},{9,11},{10,... | collective-permute-start | bytes 442376 | tf_op jit(solution)/shard_map/ppermute | solution.py:221
  19.1 1.4 %copy-done = f32[512,768]{1,0:T(8,128)S(1)} copy-done((f32[512,768]{1,0:T(8,128)S(1)}, f32[512,768]{1,0:T(8,128)}, u32[]{:S(2)}) %copy-start) | copy-done | bytes 1572888
  20.5 0.7 copy-done.5
  21.9 0.9 shard_map.131
  26.0 2.7 %shard_map.132 = (bf16[192,768]{1,0:T(8,128)(2,1)S(1)}, bf16[192,768]{1,0:T(8,128)(2,1)S(1)}, bf16[256,768]{1,0:T(8,128)(2,1)}, bf16[256,768]{1,0:T(8,128)(2,1)}...) custom-call(f32[256,768]{1,0:T(8,128)S(1)} %get-tuple-element.108.refs_0_, ...), custom_call_target="tpu_custom_call" | custom-call | flops 1434451968 | bytes 5769216 | tf_op jit(solution)/shard_map/pallas_call | solution.py:208
  29.2 1.3 %shard_map.133 = (bf16[256,768]{1,0:T(8,128)(2,1)S(1)}, bf16[256,768]{1,0:T(8,128)(2,1)S(1)}, f32[192,768]{1,0:T(8,128)S(1)}) custom-call(bf16[768,256]{1,0:T(8,128)(2,1)S(1)} %get-tuple-element.95.turned_high, bf16[768,256]{1,0:T(8,128)(2,1)S(1)} %get-tuple-element.96.turned_low, f32[256,512]{1,0:T(8,128)S(1)} %get-tuple-element.113.scores, ...), custom_call_target="tpu_custom_call" | custom-call | flops 452984832 | bytes 2883584 | tf_op jit(solution)/shard_map/pallas_call | solution.py:208
  30.4 1.8 %collective-permute-start.16 = (f32[192,768]{1,0:T(8,128)S(1)}, f32[192,768]{1,0:T(8,128)S(1)}, u32[]{:S(2)}, u32[]{:S(2)}) collective-permute-start(f32[192,768]{1,0:T(8,128)S(1)} %get-tuple-element.119), channel_id=1, source_target_pairs={{0,1},{1,0},{2,3},{3,2},{4,5},{5,4},{6,7},{7,6},{8,9},{9,8},{10,11... | collective-permute-start | bytes 1769480 | tf_op jit(solution)/shard_map/ppermute | solution.py:221
  32.2 0.9 shard_map.134
  33.9 1.2 collective-permute-start.21
  35.1 0.9 collective-permute-start.18
  36.0 1.1 collective-permute-start.20
  37.1 17.8 %collective-permute-done.21.c = f32[48,768]{1,0:T(8,128)S(1)} collective-permute-done((f32[48,768]{1,0:T(8,128)S(1)}, f32[48,768]{1,0:T(8,128)S(1)}, u32[]{:S(2)}, u32[]{:S(2)}) %collective-permute-start.21) | collective-permute-done | bytes 147488 | tf_op jit(solution)/shard_map/ppermute | solution.py:221
  55.1 3.0 %collective-permute-done.18.c = f32[48,768]{1,0:T(8,128)S(1)} collective-permute-done((f32[48,768]{1,0:T(8,128)S(1)}, f32[48,768]{1,0:T(8,128)S(1)}, u32[]{:S(2)}, u32[]{:S(2)}) %collective-permute-start.18) | collective-permute-done | bytes 147488 | tf_op jit(solution)/shard_map/ppermute | solution.py:221
  58.2 3.0 %collective-permute-done.20.c = f32[48,768]{1,0:T(8,128)S(1)} collective-permute-done((f32[48,768]{1,0:T(8,128)S(1)}, f32[48,768]{1,0:T(8,128)S(1)}, u32[]{:S(2)}, u32[]{:S(2)}) %collective-permute-start.20) | collective-permute-done | bytes 147488 | tf_op jit(solution)/shard_map/ppermute | solution.py:221
  61.3 1.5 %collective-permute-start.23 = (f32[48,768]{1,0:T(8,128)S(1)}, f32[48,768]{1,0:T(8,128)S(1)}, u32[]{:S(2)}, u32[]{:S(2)}) collective-permute-start(f32[48,768]{1,0:T(8,128)S(1)} %shard_map.141), channel_id=1, source_target_pairs={{0,8},{1,9},{2,10},{3,11},{4,12},{5,13},{6,14},{7,15},{8,0},{9,1},... | collective-permute-start | bytes 442376 | tf_op jit(solution)/shard_map/ppermute | solution.py:221
  62.9 1.5 %collective-permute-done.17.c = f32[48,768]{1,0:T(8,128)S(1)} collective-permute-done((f32[48,768]{1,0:T(8,128)S(1)}, f32[48,768]{1,0:T(8,128)S(1)}, u32[]{:S(2)}, u32[]{:S(2)}) %collective-permute-start.17) | collective-permute-done | bytes 147488 | tf_op jit(solution)/shard_map/ppermute | solution.py:221
  64.4 6.8 %collective-permute-done.23.rest_1_ = f32[48,768]{1,0:T(8,128)S(1)} collective-permute-done((f32[48,768]{1,0:T(8,128)S(1)}, f32[48,768]{1,0:T(8,128)S(1)}, u32[]{:S(2)}, u32[]{:S(2)}) %collective-permute-start.23) | collective-permute-done | bytes 147488 | tf_op jit(solution)/shard_map/ppermute | solution.py:221
  71.5 2.8 %collective-permute-start.28 = (f32[48,768]{1,0:T(8,128)S(1)}, f32[48,768]{1,0:T(8,128)S(1)}, u32[]{:S(2)}, u32[]{:S(2)}) collective-permute-start(f32[48,768]{1,0:T(8,128)S(1)} %get-tuple-element.124.refs_0_.relation), channel_id=1, source_target_pairs={{0,4},{1,5},{2,6},{3,7},{4,0},{5,1},{6,2},{7,3},{8,12},{9,13},{10,... | collective-permute-start | bytes 442376 | tf_op jit(solution)/shard_map/ppermute | solution.py:221
  74.4 2.1 %shard_map.143 = (f32[256,768]{1,0:T(8,128)S(1)}, f32[1,256]{1,0:T(1,128)S(1)}, bf16[768,256]{1,0:T(8,128)(2,1)S(1)}, bf16[768,256]{1,0:T(8,128)(2,1)S(1)}, bf16...) custom-call(s32[1]{0:T(128)} %bitcast.me_ref, ...), custom_call_target="tpu_custom_call" | custom-call | bytes 3933188 | tf_op jit(solution)/shard_map/pallas_call | solution.py:208
  76.5 4.0 %collective-permute-done.32.refs_1_ = f32[48,768]{1,0:T(8,128)S(1)} collective-permute-done((f32[48,768]{1,0:T(8,128)S(1)}, f32[48,768]{1,0:T(8,128)S(1)}, u32[]{:S(2)}, u32[]{:S(2)}) %collective-permute-start.32) | collective-permute-done | bytes 147488 | tf_op jit(solution)/shard_map/ppermute | solution.py:221
  80.7 1.7 %collective-permute-start.30 = (f32[48,768]{1,0:T(8,128)S(1)}, f32[48,768]{1,0:T(8,128)S(1)}, u32[]{:S(2)}, u32[]{:S(2)}) collective-permute-start(f32[48,768]{1,0:T(8,128)S(1)} %collective-permute-done.28.refs_1_), channel_id=1, source_target_pairs={{0,2},{1,3},{2,0},{3,1},{4,6},{5,7},{6,4},{7,5},{8,10},{9,11},{10,... | collective-permute-start | bytes 442376 | tf_op jit(solution)/shard_map/ppermute | solution.py:221
  83.0 3.3 %collective-permute-done.36.refs_1_ = f32[48,768]{1,0:T(8,128)S(1)} collective-permute-done((f32[48,768]{1,0:T(8,128)S(1)}, f32[48,768]{1,0:T(8,128)S(1)}, u32[]{:S(2)}, u32[]{:S(2)}) %collective-permute-start.36) | collective-permute-done | bytes 147488 | tf_op jit(solution)/shard_map/ppermute | solution.py:221
  87.7 2.6 %collective-permute-done.34.refs_3_ = f32[48,768]{1,0:T(8,128)S(1)} collective-permute-done((f32[48,768]{1,0:T(8,128)S(1)}, f32[48,768]{1,0:T(8,128)S(1)}, u32[]{:S(2)}, u32[]{:S(2)}) %collective-permute-start.34) | collective-permute-done | bytes 147488 | tf_op jit(solution)/shard_map/ppermute | solution.py:221
  91.4 1.2 %collective-permute-done.38.refs_3_ = f32[48,768]{1,0:T(8,128)S(1)} collective-permute-done((f32[48,768]{1,0:T(8,128)S(1)}, f32[48,768]{1,0:T(8,128)S(1)}, u32[]{:S(2)}, u32[]{:S(2)}) %collective-permute-start.38) | collective-permute-done | bytes 147488 | tf_op jit(solution)/shard_map/ppermute | solution.py:221
  94.1 2.4 %shard_map.148 = (bf16[192,768]{1,0:T(8,128)(2,1)S(1)}, bf16[192,768]{1,0:T(8,128)(2,1)S(1)}, bf16[256,768]{1,0:T(8,128)(2,1)S(1)}, bf16[256,768]{1,0:T(8,128)(2...) custom-call(f32[256,768]{1,0:T(8,128)S(1)} %get-tuple-element.148.re, ...), custom_call_target="tpu_custom_call" | custom-call | flops 1434451968 | bytes 4980736 | tf_op jit(solution)/shard_map/pallas_call | solution.py:208
  96.9 0.9 shard_map.149
  98.6 1.2 collective-permute-start.46
  99.8 0.9 collective-permute-start.43
  100.8 1.1 collective-permute-start.45
  101.8 3.5 %collective-permute-done.46.c = f32[48,768]{1,0:T(8,128)S(1)} collective-permute-done((f32[48,768]{1,0:T(8,128)S(1)}, f32[48,768]{1,0:T(8,128)S(1)}, u32[]{:S(2)}, u32[]{:S(2)}) %collective-permute-start.46) | collective-permute-done | bytes 147488 | tf_op jit(solution)/shard_map/ppermute | solution.py:221
  105.4 1.7 %collective-permute-start.47 = (f32[48,768]{1,0:T(8,128)S(1)}, f32[48,768]{1,0:T(8,128)S(1)}, u32[]{:S(2)}, u32[]{:S(2)}) collective-permute-start(f32[48,768]{1,0:T(8,128)S(1)} %shard_map.157), channel_id=1, source_target_pairs={{0,4},{1,5},{2,6},{3,7},{4,0},{5,1},{6,2},{7,3},{8,12},{9,13},{10,... | collective-permute-start | bytes 442376 | tf_op jit(solution)/shard_map/ppermute | solution.py:221
  107.5 1.0 collective-permute-done.43.c
  108.6 1.7 %collective-permute-start.44 = (f32[48,768]{1,0:T(8,128)S(1)}, f32[48,768]{1,0:T(8,128)S(1)}, u32[]{:S(2)}, u32[]{:S(2)}) collective-permute-start(f32[48,768]{1,0:T(8,128)S(1)} %shard_map.154), channel_id=1, source_target_pairs={{0,4},{1,5},{2,6},{3,7},{4,0},{5,1},{6,2},{7,3},{8,12},{9,13},{10,... | collective-permute-start | bytes 442376 | tf_op jit(solution)/shard_map/ppermute | solution.py:221
  110.3 1.4 %collective-permute-done.45.c = f32[48,768]{1,0:T(8,128)S(1)} collective-permute-done((f32[48,768]{1,0:T(8,128)S(1)}, f32[48,768]{1,0:T(8,128)S(1)}, u32[]{:S(2)}, u32[]{:S(2)}) %collective-permute-start.45) | collective-permute-done | bytes 147488 | tf_op jit(solution)/shard_map/ppermute | solution.py:221
  111.8 1.5 %collective-permute-start.48 = (f32[48,768]{1,0:T(8,128)S(1)}, f32[48,768]{1,0:T(8,128)S(1)}, u32[]{:S(2)}, u32[]{:S(2)}) collective-permute-start(f32[48,768]{1,0:T(8,128)S(1)} %shard_map.158), channel_id=1, source_target_pairs={{0,8},{1,9},{2,10},{3,11},{4,12},{5,13},{6,14},{7,15},{8,0},{9,1},... | collective-permute-start | bytes 442376 | tf_op jit(solution)/shard_map/ppermute | solution.py:221
  113.2 1.1 collective-permute-done.41.c
  114.3 2.4 %shard_map.151 = (f32[256,768]{1,0:T(8,128)}, f32[1,256]{1,0:T(1,128)}) custom-call(s32[1]{0:T(128)} %bitcast.me_ref, bf16[256,768]{1,0:T(8,128)(2,1)S(1)} %get-tuple-element.157.grad_high, bf16[256,768]{1,0:T(8,128)(2,1)S(1)} %get-tuple-element.153.grad_low, bf16[192,768]{1,0:T(8,128)(2,1)S(1)} %get-tuple-element.158.rest_0_, ...), custom_call_target="tpu_custom_call" | custom-call | bytes 3933188 | tf_op jit(solution)/shard_map/pallas_call | solution.py:208
  116.8 2.5 %shard_map.152 = (f32[512,768]{1,0:T(8,128)}, f32[1,512]{1,0:T(1,128)}) custom-call(f32[256,512]{1,0:T(8,128)S(1)} %get-tuple-element.171.grad_scores, bf16[256,768]{1,0:T(8,128)(2,1)S(1)} %get-tuple-element.172.product_high, bf16[256,768]{1,0:T(8,128)(2,1)S(1)} %get-tuple-element.173.product_low, f32[520,768]{1,0:T(8,128)S(1)} %collective-permute-done.27.refs_0_), custom_call_target="tpu_custom_call" | custom-call | flops 603979776 | bytes 2908160 | tf_op jit(solution)/shard_map/pallas_call | solution.py:208
  119.3 1.3 %collective-permute-done.48.rest_1_ = f32[48,768]{1,0:T(8,128)S(1)} collective-permute-done((f32[48,768]{1,0:T(8,128)S(1)}, f32[48,768]{1,0:T(8,128)S(1)}, u32[]{:S(2)}, u32[]{:S(2)}) %collective-permute-start.48) | collective-permute-done | bytes 147488 | tf_op jit(solution)/shard_map/ppermute | solution.py:221
  120.7 0.8 shard_map.159
  (103 shorter events, 13.9 us)
Async XLA Ops:
  0.6 11.4 %collective-permute-start.7 = (f32[48,768]{1,0:T(8,128)}, f32[48,768]{1,0:T(8,128)S(1)}, u32[]{:S(2)}, u32[]{:S(2)}) collective-permute-start(f32[48,768]{1,0:T(8,128)} %relation.1), channel_id=1, source_target_pairs={{0,8},{1,9},{2,10},{3,11},{4,12},{5,13},{6,14},{7,15},{8,0},{9,1},... | collective-permute-start | bytes 442376 | tf_op jit(solution)/shard_map/ppermute | solution.py:221
  4.7 8.0 %collective-permute-start.3 = (f32[48,768]{1,0:T(8,128)}, f32[48,768]{1,0:T(8,128)S(1)}, u32[]{:S(2)}, u32[]{:S(2)}) collective-permute-start(f32[48,768]{1,0:T(8,128)} %relation.1), channel_id=1, source_target_pairs={{0,4},{1,5},{2,6},{3,7},{4,0},{5,1},{6,2},{7,3},{8,12},{9,13},{10,... | collective-permute-start | bytes 442376 | tf_op jit(solution)/shard_map/ppermute | solution.py:221
  6.3 8.0 %collective-permute-start.1 = (f32[48,768]{1,0:T(8,128)}, f32[48,768]{1,0:T(8,128)S(1)}, u32[]{:S(2)}, u32[]{:S(2)}) collective-permute-start(f32[48,768]{1,0:T(8,128)} %relation.1), channel_id=1, source_target_pairs={{0,2},{1,3},{2,0},{3,1},{4,6},{5,7},{6,4},{7,5},{8,10},{9,11},{10,... | collective-permute-start | bytes 442376 | tf_op jit(solution)/shard_map/ppermute | solution.py:221
  7.8 7.0 %collective-permute-start = (f32[48,768]{1,0:T(8,128)}, f32[48,768]{1,0:T(8,128)S(1)}, u32[]{:S(2)}, u32[]{:S(2)}) collective-permute-start(f32[48,768]{1,0:T(8,128)} %relation.1), channel_id=1, source_target_pairs={{0,1},{1,0},{2,3},{3,2},{4,5},{5,4},{6,7},{7,6},{8,9},{9,8},{10,11... | collective-permute-start | bytes 442376 | tf_op jit(solution)/shard_map/ppermute | solution.py:221
  12.1 5.1 %collective-permute-start.11 = (f32[48,768]{1,0:T(8,128)S(1)}, f32[48,768]{1,0:T(8,128)S(1)}, u32[]{:S(2)}, u32[]{:S(2)}) collective-permute-start(f32[48,768]{1,0:T(8,128)S(1)} %collective-permute-done.7.refs_1_), channel_id=1, source_target_pairs={{0,4},{1,5},{2,6},{3,7},{4,0},{5,1},{6,2},{7,3},{8,12},{9,13},{10,... | collective-permute-start | bytes 442376 | tf_op jit(solution)/shard_map/ppermute | solution.py:221
  12.8 6.3 %collective-permute-start.5 = (f32[48,768]{1,0:T(8,128)S(1)}, f32[48,768]{1,0:T(8,128)S(1)}, u32[]{:S(2)}, u32[]{:S(2)}) collective-permute-start(f32[48,768]{1,0:T(8,128)S(1)} %collective-permute-done.3.refs_1_), channel_id=1, source_target_pairs={{0,2},{1,3},{2,0},{3,1},{4,6},{5,7},{6,4},{7,5},{8,10},{9,11},{10,... | collective-permute-start | bytes 442376 | tf_op jit(solution)/shard_map/ppermute | solution.py:221
  14.3 8.5 %collective-permute-start.2 = (f32[48,768]{1,0:T(8,128)S(1)}, f32[48,768]{1,0:T(8,128)S(1)}, u32[]{:S(2)}, u32[]{:S(2)}) collective-permute-start(f32[48,768]{1,0:T(8,128)S(1)} %collective-permute-done.1.refs_2_), channel_id=1, source_target_pairs={{0,1},{1,0},{2,3},{3,2},{4,5},{5,4},{6,7},{7,6},{8,9},{9,8},{10,11... | collective-permute-start | bytes 442376 | tf_op jit(solution)/shard_map/ppermute | solution.py:221
  14.3 9.1 %collective-permute-start.9 = (f32[48,768]{1,0:T(8,128)S(1)}, f32[48,768]{1,0:T(8,128)S(1)}, u32[]{:S(2)}, u32[]{:S(2)}) collective-permute-start(f32[48,768]{1,0:T(8,128)S(1)} %collective-permute-done.7.refs_1_), channel_id=1, source_target_pairs={{0,2},{1,3},{2,0},{3,1},{4,6},{5,7},{6,4},{7,5},{8,10},{9,11},{10,... | collective-permute-start | bytes 442376 | tf_op jit(solution)/shard_map/ppermute | solution.py:221
  14.8 9.2 %collective-permute-start.4 = (f32[48,768]{1,0:T(8,128)S(1)}, f32[48,768]{1,0:T(8,128)S(1)}, u32[]{:S(2)}, u32[]{:S(2)}) collective-permute-start(f32[48,768]{1,0:T(8,128)S(1)} %collective-permute-done.3.refs_1_), channel_id=1, source_target_pairs={{0,1},{1,0},{2,3},{3,2},{4,5},{5,4},{6,7},{7,6},{8,9},{9,8},{10,11... | collective-permute-start | bytes 442376 | tf_op jit(solution)/shard_map/ppermute | solution.py:221
  17.2 7.4 %collective-permute-start.13 = (f32[48,768]{1,0:T(8,128)S(1)}, f32[48,768]{1,0:T(8,128)S(1)}, u32[]{:S(2)}, u32[]{:S(2)}) collective-permute-start(f32[48,768]{1,0:T(8,128)S(1)} %collective-permute-done.11.refs_1_), channel_id=1, source_target_pairs={{0,2},{1,3},{2,0},{3,1},{4,6},{5,7},{6,4},{7,5},{8,10},{9,11},{10,... | collective-permute-start | bytes 442376 | tf_op jit(solution)/shard_map/ppermute | solution.py:221
  19.1 5.5 %collective-permute-start.6 = (f32[48,768]{1,0:T(8,128)S(1)}, f32[48,768]{1,0:T(8,128)S(1)}, u32[]{:S(2)}, u32[]{:S(2)}) collective-permute-start(f32[48,768]{1,0:T(8,128)S(1)} %collective-permute-done.5.refs_3_), channel_id=1, source_target_pairs={{0,1},{1,0},{2,3},{3,2},{4,5},{5,4},{6,7},{7,6},{8,9},{9,8},{10,11... | collective-permute-start | bytes 442376 | tf_op jit(solution)/shard_map/ppermute | solution.py:221
  22.8 2.3 %collective-permute-start.8 = (f32[48,768]{1,0:T(8,128)S(1)}, f32[48,768]{1,0:T(8,128)S(1)}, u32[]{:S(2)}, u32[]{:S(2)}) collective-permute-start(f32[48,768]{1,0:T(8,128)S(1)} %collective-permute-done.7.refs_1_), channel_id=1, source_target_pairs={{0,1},{1,0},{2,3},{3,2},{4,5},{5,4},{6,7},{7,6},{8,9},{9,8},{10,11... | collective-permute-start | bytes 442376 | tf_op jit(solution)/shard_map/ppermute | solution.py:221
  23.4 1.8 %collective-permute-start.10 = (f32[48,768]{1,0:T(8,128)S(1)}, f32[48,768]{1,0:T(8,128)S(1)}, u32[]{:S(2)}, u32[]{:S(2)}) collective-permute-start(f32[48,768]{1,0:T(8,128)S(1)} %collective-permute-done.9.refs_3_), channel_id=1, source_target_pairs={{0,1},{1,0},{2,3},{3,2},{4,5},{5,4},{6,7},{7,6},{8,9},{9,8},{10,11... | collective-permute-start | bytes 442376 | tf_op jit(solution)/shard_map/ppermute | solution.py:221
  24.1 1.7 %collective-permute-start.12 = (f32[48,768]{1,0:T(8,128)S(1)}, f32[48,768]{1,0:T(8,128)S(1)}, u32[]{:S(2)}, u32[]{:S(2)}) collective-permute-start(f32[48,768]{1,0:T(8,128)S(1)} %collective-permute-done.11.refs_1_), channel_id=1, source_target_pairs={{0,1},{1,0},{2,3},{3,2},{4,5},{5,4},{6,7},{7,6},{8,9},{9,8},{10,11... | collective-permute-start | bytes 442376 | tf_op jit(solution)/shard_map/ppermute | solution.py:221
  24.6 1.4 %collective-permute-start.14 = (f32[48,768]{1,0:T(8,128)S(1)}, f32[48,768]{1,0:T(8,128)S(1)}, u32[]{:S(2)}, u32[]{:S(2)}) collective-permute-start(f32[48,768]{1,0:T(8,128)S(1)} %collective-permute-done.13.refs_3_), channel_id=1, source_target_pairs={{0,1},{1,0},{2,3},{3,2},{4,5},{5,4},{6,7},{7,6},{8,9},{9,8},{10,11... | collective-permute-start | bytes 442376 | tf_op jit(solution)/shard_map/ppermute | solution.py:221
  28.7 45.7 %collective-permute-start.27 = (f32[520,768]{1,0:T(8,128)S(1)}, f32[520,768]{1,0:T(8,128)S(1)}, u32[]{:S(2)}, u32[]{:S(2)}) collective-permute-start(f32[520,768]{1,0:T(8,128)S(1)} %get-tuple-element.125), channel_id=1, source_target_pairs={{0,1},{1,2},{2,3},{3,4},{4,5},{5,6},{6,7},{7,8},{8,9},{9,10},{10,1... | collective-permute-start | bytes 4792328 | tf_op jit(solution)/shard_map/ppermute | solution.py:357
  30.4 3.4 %collective-permute-start.16 = (f32[192,768]{1,0:T(8,128)S(1)}, f32[192,768]{1,0:T(8,128)S(1)}, u32[]{:S(2)}, u32[]{:S(2)}) collective-permute-start(f32[192,768]{1,0:T(8,128)S(1)} %get-tuple-element.119), channel_id=1, source_target_pairs={{0,1},{1,0},{2,3},{3,2},{4,5},{5,4},{6,7},{7,6},{8,9},{9,8},{10,11... | collective-permute-start | bytes 1769480 | tf_op jit(solution)/shard_map/ppermute | solution.py:221
  33.1 4.0 %collective-permute-start.15 = (f32[192,768]{1,0:T(8,128)S(1)}, f32[192,768]{1,0:T(8,128)S(1)}, u32[]{:S(2)}, u32[]{:S(2)}) collective-permute-start(f32[192,768]{1,0:T(8,128)S(1)} %get-tuple-element.117), channel_id=1, source_target_pairs={{0,1},{1,0},{2,3},{3,2},{4,5},{5,4},{6,7},{7,6},{8,9},{9,8},{10,11... | collective-permute-start | bytes 1769480 | tf_op jit(solution)/shard_map/ppermute | solution.py:221
  33.9 21.0 %collective-permute-start.21 = (f32[48,768]{1,0:T(8,128)S(1)}, f32[48,768]{1,0:T(8,128)S(1)}, u32[]{:S(2)}, u32[]{:S(2)}) collective-permute-start(f32[48,768]{1,0:T(8,128)S(1)} %get-tuple-element.123), channel_id=1, source_target_pairs={{0,2},{1,3},{2,0},{3,1},{4,6},{5,7},{6,4},{7,5},{8,10},{9,11},{10,... | collective-permute-start | bytes 442376 | tf_op jit(solution)/shard_map/ppermute | solution.py:221
  35.1 23.0 %collective-permute-start.18 = (f32[48,768]{1,0:T(8,128)S(1)}, f32[48,768]{1,0:T(8,128)S(1)}, u32[]{:S(2)}, u32[]{:S(2)}) collective-permute-start(f32[48,768]{1,0:T(8,128)S(1)} %get-tuple-element.121), channel_id=1, source_target_pairs={{0,2},{1,3},{2,0},{3,1},{4,6},{5,7},{6,4},{7,5},{8,10},{9,11},{10,... | collective-permute-start | bytes 442376 | tf_op jit(solution)/shard_map/ppermute | solution.py:221
  36.0 25.2 %collective-permute-start.20 = (f32[48,768]{1,0:T(8,128)S(1)}, f32[48,768]{1,0:T(8,128)S(1)}, u32[]{:S(2)}, u32[]{:S(2)}) collective-permute-start(f32[48,768]{1,0:T(8,128)S(1)} %get-tuple-element.122), channel_id=1, source_target_pairs={{0,2},{1,3},{2,0},{3,1},{4,6},{5,7},{6,4},{7,5},{8,10},{9,11},{10,... | collective-permute-start | bytes 442376 | tf_op jit(solution)/shard_map/ppermute | solution.py:221
  55.0 6.3 %collective-permute-start.22 = (f32[48,768]{1,0:T(8,128)S(1)}, f32[48,768]{1,0:T(8,128)S(1)}, u32[]{:S(2)}, u32[]{:S(2)}) collective-permute-start(f32[48,768]{1,0:T(8,128)S(1)} %shard_map.140), channel_id=1, source_target_pairs={{0,4},{1,5},{2,6},{3,7},{4,0},{5,1},{6,2},{7,3},{8,12},{9,13},{10,... | collective-permute-start | bytes 442376 | tf_op jit(solution)/shard_map/ppermute | solution.py:221
  55.0 9.3 %collective-permute-start.17 = (f32[48,768]{1,0:T(8,128)S(1)}, f32[48,768]{1,0:T(8,128)S(1)}, u32[]{:S(2)}, u32[]{:S(2)}) collective-permute-start(f32[48,768]{1,0:T(8,128)S(1)} %get-tuple-element.120), channel_id=1, source_target_pairs={{0,2},{1,3},{2,0},{3,1},{4,6},{5,7},{6,4},{7,5},{8,10},{9,11},{10,... | collective-permute-start | bytes 442376 | tf_op jit(solution)/shard_map/ppermute | solution.py:221
  58.1 6.3 %collective-permute-start.19 = (f32[48,768]{1,0:T(8,128)S(1)}, f32[48,768]{1,0:T(8,128)S(1)}, u32[]{:S(2)}, u32[]{:S(2)}) collective-permute-start(f32[48,768]{1,0:T(8,128)S(1)} %shard_map.137), channel_id=1, source_target_pairs={{0,4},{1,5},{2,6},{3,7},{4,0},{5,1},{6,2},{7,3},{8,12},{9,13},{10,... | collective-permute-start | bytes 442376 | tf_op jit(solution)/shard_map/ppermute | solution.py:221
  61.3 9.9 %collective-permute-start.23 = (f32[48,768]{1,0:T(8,128)S(1)}, f32[48,768]{1,0:T(8,128)S(1)}, u32[]{:S(2)}, u32[]{:S(2)}) collective-permute-start(f32[48,768]{1,0:T(8,128)S(1)} %shard_map.141), channel_id=1, source_target_pairs={{0,8},{1,9},{2,10},{3,11},{4,12},{5,13},{6,14},{7,15},{8,0},{9,1},... | collective-permute-start | bytes 442376 | tf_op jit(solution)/shard_map/ppermute | solution.py:221
  71.4 9.2 %collective-permute-start.32 = (f32[48,768]{1,0:T(8,128)S(1)}, f32[48,768]{1,0:T(8,128)S(1)}, u32[]{:S(2)}, u32[]{:S(2)}) collective-permute-start(f32[48,768]{1,0:T(8,128)S(1)} %get-tuple-element.124.refs_0_.relation), channel_id=1, source_target_pairs={{0,8},{1,9},{2,10},{3,11},{4,12},{5,13},{6,14},{7,15},{8,0},{9,1},... | collective-permute-start | bytes 442376 | tf_op jit(solution)/shard_map/ppermute | solution.py:221
  71.4 9.1 %collective-permute-start.25 = (f32[48,768]{1,0:T(8,128)S(1)}, f32[48,768]{1,0:T(8,128)S(1)}, u32[]{:S(2)}, u32[]{:S(2)}) collective-permute-start(f32[48,768]{1,0:T(8,128)S(1)} %get-tuple-element.124.refs_0_.relation), channel_id=1, source_target_pairs={{0,2},{1,3},{2,0},{3,1},{4,6},{5,7},{6,4},{7,5},{8,10},{9,11},{10,... | collective-permute-start | bytes 442376 | tf_op jit(solution)/shard_map/ppermute | solution.py:221
  71.5 9.2 %collective-permute-start.28 = (f32[48,768]{1,0:T(8,128)S(1)}, f32[48,768]{1,0:T(8,128)S(1)}, u32[]{:S(2)}, u32[]{:S(2)}) collective-permute-start(f32[48,768]{1,0:T(8,128)S(1)} %get-tuple-element.124.refs_0_.relation), channel_id=1, source_target_pairs={{0,4},{1,5},{2,6},{3,7},{4,0},{5,1},{6,2},{7,3},{8,12},{9,13},{10,... | collective-permute-start | bytes 442376 | tf_op jit(solution)/shard_map/ppermute | solution.py:221
  74.4 8.4 %collective-permute-start.24 = (f32[48,768]{1,0:T(8,128)S(1)}, f32[48,768]{1,0:T(8,128)S(1)}, u32[]{:S(2)}, u32[]{:S(2)}) collective-permute-start(f32[48,768]{1,0:T(8,128)S(1)} %get-tuple-element.124.refs_0_.relation), channel_id=1, source_target_pairs={{0,1},{1,0},{2,3},{3,2},{4,5},{5,4},{6,7},{7,6},{8,9},{9,8},{10,11... | collective-permute-start | bytes 442376 | tf_op jit(solution)/shard_map/ppermute | solution.py:221
  80.6 5.7 %collective-permute-start.36 = (f32[48,768]{1,0:T(8,128)S(1)}, f32[48,768]{1,0:T(8,128)S(1)}, u32[]{:S(2)}, u32[]{:S(2)}) collective-permute-start(f32[48,768]{1,0:T(8,128)S(1)} %collective-permute-done.32.refs_1_), channel_id=1, source_target_pairs={{0,4},{1,5},{2,6},{3,7},{4,0},{5,1},{6,2},{7,3},{8,12},{9,13},{10,... | collective-permute-start | bytes 442376 | tf_op jit(solution)/shard_map/ppermute | solution.py:221
  80.7 6.4 %collective-permute-start.30 = (f32[48,768]{1,0:T(8,128)S(1)}, f32[48,768]{1,0:T(8,128)S(1)}, u32[]{:S(2)}, u32[]{:S(2)}) collective-permute-start(f32[48,768]{1,0:T(8,128)S(1)} %collective-permute-done.28.refs_1_), channel_id=1, source_target_pairs={{0,2},{1,3},{2,0},{3,1},{4,6},{5,7},{6,4},{7,5},{8,10},{9,11},{10,... | collective-permute-start | bytes 442376 | tf_op jit(solution)/shard_map/ppermute | solution.py:221
  82.4 4.8 %collective-permute-start.26 = (f32[48,768]{1,0:T(8,128)S(1)}, f32[48,768]{1,0:T(8,128)S(1)}, u32[]{:S(2)}, u32[]{:S(2)}) collective-permute-start(f32[48,768]{1,0:T(8,128)S(1)} %collective-permute-done.25.refs_2_), channel_id=1, source_target_pairs={{0,1},{1,0},{2,3},{3,2},{4,5},{5,4},{6,7},{7,6},{8,9},{9,8},{10,11... | collective-permute-start | bytes 442376 | tf_op jit(solution)/shard_map/ppermute | solution.py:221
  82.4 7.9 %collective-permute-start.34 = (f32[48,768]{1,0:T(8,128)S(1)}, f32[48,768]{1,0:T(8,128)S(1)}, u32[]{:S(2)}, u32[]{:S(2)}) collective-permute-start(f32[48,768]{1,0:T(8,128)S(1)} %collective-permute-done.32.refs_1_), channel_id=1, source_target_pairs={{0,2},{1,3},{2,0},{3,1},{4,6},{5,7},{6,4},{7,5},{8,10},{9,11},{10,... | collective-permute-start | bytes 442376 | tf_op jit(solution)/shard_map/ppermute | solution.py:221
  82.8 8.1 %collective-permute-start.29 = (f32[48,768]{1,0:T(8,128)S(1)}, f32[48,768]{1,0:T(8,128)S(1)}, u32[]{:S(2)}, u32[]{:S(2)}) collective-permute-start(f32[48,768]{1,0:T(8,128)S(1)} %collective-permute-done.28.refs_1_), channel_id=1, source_target_pairs={{0,1},{1,0},{2,3},{3,2},{4,5},{5,4},{6,7},{7,6},{8,9},{9,8},{10,11... | collective-permute-start | bytes 442376 | tf_op jit(solution)/shard_map/ppermute | solution.py:221
  86.3 6.4 %collective-permute-start.38 = (f32[48,768]{1,0:T(8,128)S(1)}, f32[48,768]{1,0:T(8,128)S(1)}, u32[]{:S(2)}, u32[]{:S(2)}) collective-permute-start(f32[48,768]{1,0:T(8,128)S(1)} %collective-permute-done.36.refs_1_), channel_id=1, source_target_pairs={{0,2},{1,3},{2,0},{3,1},{4,6},{5,7},{6,4},{7,5},{8,10},{9,11},{10,... | collective-permute-start | bytes 442376 | tf_op jit(solution)/shard_map/ppermute | solution.py:221
  87.2 5.7 %collective-permute-start.31 = (f32[48,768]{1,0:T(8,128)S(1)}, f32[48,768]{1,0:T(8,128)S(1)}, u32[]{:S(2)}, u32[]{:S(2)}) collective-permute-start(f32[48,768]{1,0:T(8,128)S(1)} %collective-permute-done.30.refs_3_), channel_id=1, source_target_pairs={{0,1},{1,0},{2,3},{3,2},{4,5},{5,4},{6,7},{7,6},{8,9},{9,8},{10,11... | collective-permute-start | bytes 442376 | tf_op jit(solution)/shard_map/ppermute | solution.py:221
  87.2 6.3 %collective-permute-start.33 = (f32[48,768]{1,0:T(8,128)S(1)}, f32[48,768]{1,0:T(8,128)S(1)}, u32[]{:S(2)}, u32[]{:S(2)}) collective-permute-start(f32[48,768]{1,0:T(8,128)S(1)} %collective-permute-done.32.refs_1_), channel_id=1, source_target_pairs={{0,1},{1,0},{2,3},{3,2},{4,5},{5,4},{6,7},{7,6},{8,9},{9,8},{10,11... | collective-permute-start | bytes 442376 | tf_op jit(solution)/shard_map/ppermute | solution.py:221
  90.3 3.1 %collective-permute-start.35 = (f32[48,768]{1,0:T(8,128)S(1)}, f32[48,768]{1,0:T(8,128)S(1)}, u32[]{:S(2)}, u32[]{:S(2)}) collective-permute-start(f32[48,768]{1,0:T(8,128)S(1)} %collective-permute-done.34.refs_3_), channel_id=1, source_target_pairs={{0,1},{1,0},{2,3},{3,2},{4,5},{5,4},{6,7},{7,6},{8,9},{9,8},{10,11... | collective-permute-start | bytes 442376 | tf_op jit(solution)/shard_map/ppermute | solution.py:221
  90.9 3.1 %collective-permute-start.37 = (f32[48,768]{1,0:T(8,128)S(1)}, f32[48,768]{1,0:T(8,128)S(1)}, u32[]{:S(2)}, u32[]{:S(2)}) collective-permute-start(f32[48,768]{1,0:T(8,128)S(1)} %collective-permute-done.36.refs_1_), channel_id=1, source_target_pairs={{0,1},{1,0},{2,3},{3,2},{4,5},{5,4},{6,7},{7,6},{8,9},{9,8},{10,11... | collective-permute-start | bytes 442376 | tf_op jit(solution)/shard_map/ppermute | solution.py:221
  96.4 2.2 %collective-permute-start.40 = (f32[192,768]{1,0:T(8,128)S(1)}, f32[192,768]{1,0:T(8,128)S(1)}, u32[]{:S(2)}, u32[]{:S(2)}) collective-permute-start(f32[192,768]{1,0:T(8,128)S(1)} %get-tuple-element.155), channel_id=1, source_target_pairs={{0,1},{1,0},{2,3},{3,2},{4,5},{5,4},{6,7},{7,6},{8,9},{9,8},{10,11... | collective-permute-start | bytes 1769480 | tf_op jit(solution)/shard_map/ppermute | solution.py:221
  97.8 4.0 %collective-permute-start.42 = (f32[192,768]{1,0:T(8,128)S(1)}, f32[192,768]{1,0:T(8,128)S(1)}, u32[]{:S(2)}, u32[]{:S(2)}) collective-permute-start(f32[192,768]{1,0:T(8,128)S(1)} %get-tuple-element.178), channel_id=1, source_target_pairs={{0,1},{1,0},{2,3},{3,2},{4,5},{5,4},{6,7},{7,6},{8,9},{9,8},{10,11... | collective-permute-start | bytes 1769480 | tf_op jit(solution)/shard_map/ppermute | solution.py:221
  98.6 6.7 %collective-permute-start.46 = (f32[48,768]{1,0:T(8,128)S(1)}, f32[48,768]{1,0:T(8,128)S(1)}, u32[]{:S(2)}, u32[]{:S(2)}) collective-permute-start(f32[48,768]{1,0:T(8,128)S(1)} %get-tuple-element.181), channel_id=1, source_target_pairs={{0,2},{1,3},{2,0},{3,1},{4,6},{5,7},{6,4},{7,5},{8,10},{9,11},{10,... | collective-permute-start | bytes 442376 | tf_op jit(solution)/shard_map/ppermute | solution.py:221
  99.8 8.7 %collective-permute-start.43 = (f32[48,768]{1,0:T(8,128)S(1)}, f32[48,768]{1,0:T(8,128)S(1)}, u32[]{:S(2)}, u32[]{:S(2)}) collective-permute-start(f32[48,768]{1,0:T(8,128)S(1)} %get-tuple-element.179), channel_id=1, source_target_pairs={{0,2},{1,3},{2,0},{3,1},{4,6},{5,7},{6,4},{7,5},{8,10},{9,11},{10,... | collective-permute-start | bytes 442376 | tf_op jit(solution)/shard_map/ppermute | solution.py:221
  100.8 11.0 %collective-permute-start.45 = (f32[48,768]{1,0:T(8,128)S(1)}, f32[48,768]{1,0:T(8,128)S(1)}, u32[]{:S(2)}, u32[]{:S(2)}) collective-permute-start(f32[48,768]{1,0:T(8,128)S(1)} %get-tuple-element.180), channel_id=1, source_target_pairs={{0,2},{1,3},{2,0},{3,1},{4,6},{5,7},{6,4},{7,5},{8,10},{9,11},{10,... | collective-permute-start | bytes 442376 | tf_op jit(solution)/shard_map/ppermute | solution.py:221
  105.4 6.3 %collective-permute-start.47 = (f32[48,768]{1,0:T(8,128)S(1)}, f32[48,768]{1,0:T(8,128)S(1)}, u32[]{:S(2)}, u32[]{:S(2)}) collective-permute-start(f32[48,768]{1,0:T(8,128)S(1)} %shard_map.157), channel_id=1, source_target_pairs={{0,4},{1,5},{2,6},{3,7},{4,0},{5,1},{6,2},{7,3},{8,12},{9,13},{10,... | collective-permute-start | bytes 442376 | tf_op jit(solution)/shard_map/ppermute | solution.py:221
  107.2 7.2 %collective-permute-start.41 = (f32[48,768]{1,0:T(8,128)S(1)}, f32[48,768]{1,0:T(8,128)S(1)}, u32[]{:S(2)}, u32[]{:S(2)}) collective-permute-start(f32[48,768]{1,0:T(8,128)S(1)} %get-tuple-element.156), channel_id=1, source_target_pairs={{0,2},{1,3},{2,0},{3,1},{4,6},{5,7},{6,4},{7,5},{8,10},{9,11},{10,... | collective-permute-start | bytes 442376 | tf_op jit(solution)/shard_map/ppermute | solution.py:221
  108.6 10.7 %collective-permute-start.44 = (f32[48,768]{1,0:T(8,128)S(1)}, f32[48,768]{1,0:T(8,128)S(1)}, u32[]{:S(2)}, u32[]{:S(2)}) collective-permute-start(f32[48,768]{1,0:T(8,128)S(1)} %shard_map.154), channel_id=1, source_target_pairs={{0,4},{1,5},{2,6},{3,7},{4,0},{5,1},{6,2},{7,3},{8,12},{9,13},{10,... | collective-permute-start | bytes 442376 | tf_op jit(solution)/shard_map/ppermute | solution.py:221
  111.8 8.9 %collective-permute-start.48 = (f32[48,768]{1,0:T(8,128)S(1)}, f32[48,768]{1,0:T(8,128)S(1)}, u32[]{:S(2)}, u32[]{:S(2)}) collective-permute-start(f32[48,768]{1,0:T(8,128)S(1)} %shard_map.158), channel_id=1, source_target_pairs={{0,8},{1,9},{2,10},{3,11},{4,12},{5,13},{6,14},{7,15},{8,0},{9,1},... | collective-permute-start | bytes 442376 | tf_op jit(solution)/shard_map/ppermute | solution.py:221
  (11 other events, 63.0 us)
